TPU v7x, 32 devices: a whole 2x2x4 slice. The times are simulated.
32 devices in a mesh: dp: 2 (over x), fsdp: 4 (over y, core), seq: 4 (over z).
Axes of the slice: x: 2, y: 2, z: 4, core: 2. Of those that a mesh axis runs over, the one named last changes fastest.
Arguments:
- inputs: bfloat16 [24, 1024, 1024], P(('dp', 'fsdp'), 'seq'), may hold values from -6 to 6
- segment_ids: int32 [24, 1024], P(('dp', 'fsdp'), 'seq'), may hold values from 0 to 17, as said below
- out_cotangent: bfloat16 [24, 1024, 1024], P(('dp', 'fsdp'), 'seq'), may hold values from -6 to 6
- mixer_gain: bfloat16 [1024], P('fsdp'), may hold values from 0.5 to 1.5
- qkv_weight: bfloat16 [1024, 3072], P('fsdp'), may hold values from -0.1875 to 0.1875
- gate_weight: bfloat16 [1024, 1536], P('fsdp'), may hold values from -0.1875 to 0.1875
- decay_weight: bfloat16 [1024, 12], P('fsdp'), may hold values from -0.375 to 0.375
- conv_weight: bfloat16 [4, 3072], P(None, 'fsdp'), may hold values from -3 to 3
- decay_log: float32 [6], replicated, may hold values from -1 to 1
- decay_bias: float32 [6], replicated, may hold values from -8 to -3
- head_gain: bfloat16 [256], P('fsdp'), may hold values from 0.5 to 1.5
- out_weight: bfloat16 [1536, 1024], P('fsdp'), may hold values from -0.3125 to 0.3125
- ffn_gain: bfloat16 [1024], P('fsdp'), may hold values from 0.5 to 1.5
- ffn_in_weight: bfloat16 [1024, 5632], P('fsdp'), may hold values from -0.1875 to 0.1875
- down_weight: bfloat16 [2816, 1024], P('fsdp'), may hold values from -0.15625 to 0.15625
Outputs:
- output: bfloat16 [24, 1024, 1024], P(('dp', 'fsdp'), 'seq')
- input_grad: bfloat16 [24, 1024, 1024], P(('dp', 'fsdp'), 'seq')
- grad_mixer_gain: float32 [1024], P('fsdp')
- grad_qkv_weight: float32 [1024, 3072], P('fsdp')
- grad_gate_weight: float32 [1024, 1536], P('fsdp')
- grad_decay_weight: float32 [1024, 12], P('fsdp')
- grad_conv_weight: float32 [4, 3072], P(None, 'fsdp')
- grad_decay_log: float32 [6], replicated
- grad_decay_bias: float32 [6], replicated
- grad_head_gain: float32 [256], P('fsdp')
- grad_out_weight: float32 [1536, 1024], P('fsdp')
- grad_ffn_gain: float32 [1024], P('fsdp')
- grad_ffn_in_weight: float32 [1024, 5632], P('fsdp')
- grad_down_weight: float32 [2816, 1024], P('fsdp')
Inputs may be any that keep to these rules, and one draw needn't show every extreme that they name: `segment_ids`: within a sequence the ids start at 0 and rise by one where a document starts; a document has 60 to 800 tokens, except a sequence's last, which may be shorter. Of sequences 3 * j to 3 * j + 2, one drawn at random is a single document.
All inputs are finite; a program needn't handle non-finite values.
Results may differ from a plain program's by a relative error of at most 0.02.
Values may be sent and summed in bfloat16 or wider, within the bound.
No kernel may reach another device: no remote copies, remote signals or barrier semaphores. Data moves between devices by JAX's collectives and lax.ppermute only.
A program may use at most 384 MiB of HBM per device.

v0:
```python
from functools import partial

import jax
import jax.numpy as jnp
from jax import lax
from jax.sharding import PartitionSpec as P

H = 6
DK = 128
DV = 256
CONV = 4
BLOCK = 64
KD = 768
VD = 1536
C3 = 3072


EPSILON = 1e-06
HEAD_EPSILON = 0.001
PRECISE = lax.Precision.HIGHEST


def passed_along(value, axis, steps):
    count = lax.axis_size(axis)
    leading, last = (max(0, -steps), min(count, count - steps))
    return lax.ppermute(value, axis, [(source, source + steps) for source in range(leading, last)])


def rounded(values):
    return lax.optimization_barrier(values.astype(jnp.bfloat16)).astype(jnp.float32)


def rms_norm(values, gain):
    return values * lax.rsqrt(jnp.mean(values * values, axis=-1, keepdims=True) + EPSILON) * gain


def unit_rows(values):
    return values * lax.rsqrt(jnp.sum(values * values, axis=-1, keepdims=True) + EPSILON)


def block_step(carry, block):
    state, prev_id = carry
    query, key, value, log_decay, beta, seg_ids = block
    count = seg_ids.shape[0]
    order = jnp.arange(count, dtype=jnp.int32)
    causal = order[:, None] >= order[None, :]
    same = (seg_ids[:, None] == seg_ids[None, :]) & causal
    strict = (same & (order[:, None] > order[None, :])).astype(state.dtype)
    totals = jnp.cumsum(log_decay, axis=0)
    spread = jnp.transpose(totals[:, None, :] - totals[None, :, :], (2, 0, 1))
    within = jnp.where(same[None], spread, 0.0)
    decay = jnp.exp(within) * same[None].astype(state.dtype)
    alive = (seg_ids == prev_id).astype(state.dtype)
    from_start = jnp.transpose(jnp.exp(totals) * alive[:, None])
    beta_rows = jnp.transpose(beta)
    key_key = jnp.einsum("thd,shd->hts", key, key, precision=PRECISE)
    query_key = jnp.einsum("thd,shd->hts", query, key, precision=PRECISE)
    key_state = jnp.einsum("thd,hdw->htw", key, state, precision=PRECISE)
    query_state = jnp.einsum("thd,hdw->htw", query, state, precision=PRECISE)
    lower = beta_rows[:, :, None] * key_key * decay * strict[None]
    system = jnp.eye(count, dtype=state.dtype)[None] + lower
    target = beta_rows[:, :, None] * (
        jnp.transpose(value, (1, 0, 2)) - from_start[:, :, None] * key_state
    )
    fresh = jax.scipy.linalg.solve_triangular(system, target, lower=True)
    result = from_start[:, :, None] * query_state + jnp.einsum(
        "hts,hsw->htw", query_key * decay, fresh, precision=PRECISE
    )
    ending = decay[:, count - 1, :]
    new_state = from_start[:, count - 1][:, None, None] * state + jnp.einsum(
        "shd,hs,hsw->hdw", key, ending, fresh, precision=PRECISE
    )
    return ((new_state, seg_ids[count - 1]), jnp.transpose(result, (1, 0, 2)))


def conv_taps(padded, padded_ids, conv_weight):
    length = padded.shape[1] - (CONV - 1)
    current = padded_ids[:, CONV - 1 :]
    mixed = jnp.zeros((padded.shape[0], length, padded.shape[2]), padded.dtype)
    for tap in range(CONV):
        keep = (padded_ids[:, tap : tap + length] == current).astype(padded.dtype)
        mixed = mixed + conv_weight[tap] * padded[:, tap : tap + length, :] * keep[:, :, None]
    return jax.nn.silu(mixed)


def mixer_inputs(padded, conv_weight, decay_in, decay_log, decay_bias, padded_ids):
    conv_out = conv_taps(padded, padded_ids, conv_weight)
    batch, length = (conv_out.shape[0], conv_out.shape[1])
    query = unit_rows(conv_out[:, :, :KD].reshape(batch, length, H, DK)) * DK ** (-0.5)
    key = unit_rows(conv_out[:, :, KD : 2 * KD].reshape(batch, length, H, DK))
    value = conv_out[:, :, 2 * KD :].reshape(batch, length, H, DV)
    log_decay = -jnp.exp(decay_log) * jax.nn.softplus(decay_in[:, :, :H] + decay_bias)
    beta = jax.nn.sigmoid(decay_in[:, :, H:])
    return (query, key, value, log_decay, beta)


def local_delta(query, key, value, log_decay, beta, seg_ids, prev_ids):
    batch, length = (query.shape[0], query.shape[1])
    blank = jnp.zeros((batch, length, H, DK), jnp.float32)
    widened = jnp.concatenate([blank, value], axis=-1)
    identity = jnp.broadcast_to(jnp.eye(DK, dtype=jnp.float32), (H, DK, DK))
    start = jnp.concatenate([identity, jnp.zeros((H, DK, DV), jnp.float32)], axis=-1)
    blocks = length // BLOCK

    def one_sequence(query, key, widened, log_decay, beta, seg_ids, prev_id):

        def blocks_of(array):
            return array.reshape((blocks, BLOCK) + array.shape[1:])

        final, outputs = lax.scan(
            jax.checkpoint(block_step),
            (start, prev_id),
            (
                blocks_of(query),
                blocks_of(key),
                blocks_of(widened),
                blocks_of(log_decay),
                blocks_of(beta),
                blocks_of(seg_ids),
            ),
        )
        return (outputs.reshape((length, H, DK + DV)), final[0])

    outputs, finals = jax.vmap(one_sequence)(
        query, key, widened, log_decay, beta, seg_ids, prev_ids
    )
    return (outputs[..., :DK], outputs[..., DK:], finals[..., :DK], finals[..., DK:])


def advance(through, offsets, state):
    return jnp.einsum("shij,shjv->shiv", through, state, precision=PRECISE) + offsets


def head_out(carried, local_part, state_in, gate_out, head_gain):
    mixed = local_part + jnp.einsum("sthk,shkv->sthv", carried, state_in, precision=PRECISE)
    normed = (
        mixed
        * lax.rsqrt(jnp.mean(mixed * mixed, axis=-1, keepdims=True) + HEAD_EPSILON)
        * head_gain
    )
    normed = normed * jax.nn.silu(gate_out.reshape(mixed.shape))
    return normed.reshape(mixed.shape[0] * mixed.shape[1], VD)


def swiglu(gate_up):
    half = gate_up.shape[1] // 2
    return jax.nn.silu(gate_up[:, :half]) * gate_up[:, half:]


def local(
    inputs,
    segment_ids,
    out_cotangent,
    mixer_gain,
    qkv_weight,
    gate_weight,
    decay_weight,
    conv_weight,
    decay_log,
    decay_bias,
    head_gain,
    out_weight,
    ffn_gain,
    ffn_in_weight,
    down_weight,
):
    gathered = (
        lax.all_gather(mixer_gain, "fsdp", axis=0, tiled=True),
        lax.all_gather(qkv_weight, "fsdp", axis=0, tiled=True),
        lax.all_gather(gate_weight, "fsdp", axis=0, tiled=True),
        lax.all_gather(decay_weight, "fsdp", axis=0, tiled=True),
        lax.all_gather(conv_weight, "fsdp", axis=1, tiled=True),
        lax.all_gather(head_gain, "fsdp", axis=0, tiled=True),
        lax.all_gather(out_weight, "fsdp", axis=0, tiled=True),
        lax.all_gather(ffn_gain, "fsdp", axis=0, tiled=True),
        lax.all_gather(ffn_in_weight, "fsdp", axis=0, tiled=True),
        lax.all_gather(down_weight, "fsdp", axis=0, tiled=True),
    )
    (
        full_mixer_gain,
        full_qkv,
        full_gate,
        full_decay,
        full_conv,
        full_head_gain,
        full_out,
        full_ffn_gain,
        full_ffn_in,
        full_down,
    ) = gathered
    batch, length, width = inputs.shape
    count = batch * length
    margin = CONV - 1
    rows_in = inputs.astype(jnp.float32).reshape(count, width)
    normed, pull_mixer_norm = jax.vjp(rms_norm, rows_in, full_mixer_gain.astype(jnp.float32))
    normed_low = normed.astype(jnp.bfloat16)
    pre_conv = (
        jnp.dot(normed_low, full_qkv, preferred_element_type=jnp.float32)
        .astype(jnp.bfloat16)
        .reshape(batch, length, C3)
    )
    gate_out = jnp.dot(normed_low, full_gate, preferred_element_type=jnp.float32)
    decay_in = jnp.dot(normed_low, full_decay, preferred_element_type=jnp.float32).reshape(
        batch, length, 2 * H
    )
    rim_values = passed_along(pre_conv[:, length - margin :, :], "seq", 1)
    rim_seg = passed_along(segment_ids[:, length - margin :], "seq", 1)
    padded = jnp.concatenate([rim_values, pre_conv], axis=1).astype(jnp.float32)
    padded_ids = jnp.concatenate([rim_seg, segment_ids], axis=1)
    prepared, pull_prepare = jax.vjp(
        partial(mixer_inputs, padded_ids=padded_ids),
        padded,
        full_conv.astype(jnp.float32),
        decay_in,
        decay_log,
        decay_bias,
    )
    query, key, value, log_decay, beta = prepared
    query = rounded(query)
    key = rounded(key)
    value = rounded(value)
    delta_out, pull_delta = jax.vjp(
        partial(local_delta, seg_ids=segment_ids, prev_ids=rim_seg[:, margin - 1]),
        query,
        key,
        value,
        log_decay,
        beta,
    )
    carried, local_part, through, offsets = delta_out

    def forward_step(index, state):
        return passed_along(advance(through, offsets, state), "seq", 1)

    state_in = lax.fori_loop(0, lax.axis_size("seq") - 1, forward_step, jnp.zeros_like(offsets))
    heads, pull_heads = jax.vjp(
        head_out, carried, local_part, state_in, gate_out, full_head_gain.astype(jnp.float32)
    )
    heads_low = heads.astype(jnp.bfloat16)
    middle = rows_in + jnp.dot(heads_low, full_out, preferred_element_type=jnp.float32)
    normed_ffn, pull_ffn_norm = jax.vjp(rms_norm, middle, full_ffn_gain.astype(jnp.float32))
    normed_ffn_low = normed_ffn.astype(jnp.bfloat16)
    gate_up = jnp.dot(normed_ffn_low, full_ffn_in, preferred_element_type=jnp.float32)
    hidden, pull_swiglu = jax.vjp(swiglu, gate_up)
    hidden_low = hidden.astype(jnp.bfloat16)
    result = middle + jnp.dot(hidden_low, full_down, preferred_element_type=jnp.float32)
    output = result.astype(jnp.bfloat16).reshape(batch, length, width)
    again = (
        lax.all_gather(mixer_gain, "fsdp", axis=0, tiled=True),
        lax.all_gather(qkv_weight, "fsdp", axis=0, tiled=True),
        lax.all_gather(gate_weight, "fsdp", axis=0, tiled=True),
        lax.all_gather(decay_weight, "fsdp", axis=0, tiled=True),
        lax.all_gather(conv_weight, "fsdp", axis=1, tiled=True),
        lax.all_gather(head_gain, "fsdp", axis=0, tiled=True),
        lax.all_gather(out_weight, "fsdp", axis=0, tiled=True),
        lax.all_gather(ffn_gain, "fsdp", axis=0, tiled=True),
        lax.all_gather(ffn_in_weight, "fsdp", axis=0, tiled=True),
        lax.all_gather(down_weight, "fsdp", axis=0, tiled=True),
    )
    back_qkv = again[1]
    back_gate = again[2]
    back_decay = again[3]
    back_out = again[6]
    back_ffn_in = again[8]
    back_down = again[9]
    grad_rows = out_cotangent.reshape(count, width)
    grad_down = jnp.einsum("rf,rd->fd", hidden_low, grad_rows, preferred_element_type=jnp.float32)
    grad_hidden = jnp.einsum("rd,fd->rf", grad_rows, back_down, preferred_element_type=jnp.float32)
    (grad_gate_up,) = pull_swiglu(grad_hidden)
    grad_gate_up_low = grad_gate_up.astype(jnp.bfloat16)
    grad_ffn_in = jnp.einsum(
        "rd,rf->df", normed_ffn_low, grad_gate_up_low, preferred_element_type=jnp.float32
    )
    grad_normed_ffn = jnp.einsum(
        "rf,df->rd", grad_gate_up_low, back_ffn_in, preferred_element_type=jnp.float32
    )
    grad_middle_norm, grad_ffn_gain = pull_ffn_norm(grad_normed_ffn)
    grad_middle = grad_rows.astype(jnp.float32) + grad_middle_norm
    grad_branch = grad_middle.astype(jnp.bfloat16)
    grad_out = jnp.einsum("rv,rd->vd", heads_low, grad_branch, preferred_element_type=jnp.float32)
    grad_heads = jnp.einsum("rd,vd->rv", grad_branch, back_out, preferred_element_type=jnp.float32)
    grad_carried, grad_local, grad_state_in, grad_gate_out, grad_head_gain = pull_heads(grad_heads)
    flipped = jnp.swapaxes(through, 2, 3)

    def backward_step(index, state):
        return passed_along(
            advance(flipped, grad_state_in, state).astype(jnp.bfloat16), "seq", -1
        ).astype(jnp.float32)

    grad_state_out = lax.fori_loop(
        0, lax.axis_size("seq") - 1, backward_step, jnp.zeros_like(grad_state_in)
    )
    grad_through = jnp.einsum("shkv,shjv->shkj", grad_state_out, state_in, precision=PRECISE)
    grad_query, grad_key, grad_value, grad_log_decay, grad_beta = pull_delta(
        (grad_carried, grad_local, grad_through, grad_state_out)
    )
    grad_padded, grad_conv, grad_decay_in, grad_decay_log, grad_decay_bias = pull_prepare(
        (grad_query, grad_key, grad_value, grad_log_decay, grad_beta)
    )
    grad_rim = passed_along(grad_padded[:, :margin, :].astype(jnp.bfloat16), "seq", -1).astype(
        jnp.float32
    )
    grad_pre = grad_padded[:, margin:, :].at[:, length - margin :, :].add(grad_rim)
    grad_pre_low = grad_pre.reshape(count, C3).astype(jnp.bfloat16)
    grad_gate_low = grad_gate_out.astype(jnp.bfloat16)
    grad_decay_low = grad_decay_in.reshape(count, 2 * H).astype(jnp.bfloat16)
    grad_qkv = jnp.einsum("rd,rc->dc", normed_low, grad_pre_low, preferred_element_type=jnp.float32)
    grad_gate = jnp.einsum(
        "rd,rc->dc", normed_low, grad_gate_low, preferred_element_type=jnp.float32
    )
    grad_decay = jnp.einsum(
        "rd,rc->dc", normed_low, grad_decay_low, preferred_element_type=jnp.float32
    )
    grad_normed = jnp.einsum(
        "rc,dc->rd", grad_pre_low, back_qkv, preferred_element_type=jnp.float32
    )
    grad_normed = grad_normed + jnp.einsum(
        "rc,dc->rd", grad_gate_low, back_gate, preferred_element_type=jnp.float32
    )
    grad_normed = grad_normed + jnp.einsum(
        "rc,dc->rd", grad_decay_low, back_decay, preferred_element_type=jnp.float32
    )
    grad_rows_norm, grad_mixer_gain = pull_mixer_norm(grad_normed)
    input_grad = (grad_middle + grad_rows_norm).astype(jnp.bfloat16).reshape(batch, length, width)
    (
        shard_mixer,
        shard_qkv,
        shard_gate,
        shard_decay,
        shard_conv,
        shard_head,
        shard_out,
        shard_ffn,
        shard_ffn_in,
        shard_down,
    ) = (
        lax.psum_scatter(
            grad_mixer_gain.astype(jnp.bfloat16), "fsdp", scatter_dimension=0, tiled=True
        ).astype(jnp.float32),
        lax.psum_scatter(
            grad_qkv.astype(jnp.bfloat16), "fsdp", scatter_dimension=0, tiled=True
        ).astype(jnp.float32),
        lax.psum_scatter(
            grad_gate.astype(jnp.bfloat16), "fsdp", scatter_dimension=0, tiled=True
        ).astype(jnp.float32),
        lax.psum_scatter(
            grad_decay.astype(jnp.bfloat16), "fsdp", scatter_dimension=0, tiled=True
        ).astype(jnp.float32),
        lax.psum_scatter(
            grad_conv.astype(jnp.bfloat16), "fsdp", scatter_dimension=1, tiled=True
        ).astype(jnp.float32),
        lax.psum_scatter(
            grad_head_gain.astype(jnp.bfloat16), "fsdp", scatter_dimension=0, tiled=True
        ).astype(jnp.float32),
        lax.psum_scatter(
            grad_out.astype(jnp.bfloat16), "fsdp", scatter_dimension=0, tiled=True
        ).astype(jnp.float32),
        lax.psum_scatter(
            grad_ffn_gain.astype(jnp.bfloat16), "fsdp", scatter_dimension=0, tiled=True
        ).astype(jnp.float32),
        lax.psum_scatter(
            grad_ffn_in.astype(jnp.bfloat16), "fsdp", scatter_dimension=0, tiled=True
        ).astype(jnp.float32),
        lax.psum_scatter(
            grad_down.astype(jnp.bfloat16), "fsdp", scatter_dimension=0, tiled=True
        ).astype(jnp.float32),
    )
    summed = lax.psum(
        (
            shard_mixer,
            shard_qkv,
            shard_gate,
            shard_decay,
            shard_conv,
            shard_head,
            shard_out,
            shard_ffn,
            shard_ffn_in,
            shard_down,
        ),
        ("dp", "seq"),
    )
    decay_sums = lax.psum((grad_decay_log, grad_decay_bias), ("dp", "fsdp", "seq"))
    return (
        output,
        input_grad,
        summed[0],
        summed[1],
        summed[2],
        summed[3],
        summed[4],
        decay_sums[0],
        decay_sums[1],
        summed[5],
        summed[6],
        summed[7],
        summed[8],
        summed[9],
    )


def solution(mesh):
    placed = (
        P(("dp", "fsdp"), "seq", None),
        P(("dp", "fsdp"), "seq"),
        P(("dp", "fsdp"), "seq", None),
        P("fsdp"),
        P("fsdp", None),
        P("fsdp", None),
        P("fsdp", None),
        P(None, "fsdp"),
        P(),
        P(),
        P("fsdp"),
        P("fsdp", None),
        P("fsdp"),
        P("fsdp", None),
        P("fsdp", None),
    )
    return jax.shard_map(
        local,
        mesh=mesh,
        in_specs=placed,
        out_specs=(
            P(("dp", "fsdp"), "seq", None),
            P(("dp", "fsdp"), "seq", None),
            P("fsdp"),
            P("fsdp", None),
            P("fsdp", None),
            P("fsdp", None),
            P(None, "fsdp"),
            P(),
            P(),
            P("fsdp"),
            P("fsdp", None),
            P("fsdp"),
            P("fsdp", None),
            P("fsdp", None),
        ),
        check_vma=False,
    )
```

profile of v0, /device:TPU:0, one launch (start us, length us, event | category | flops | bytes accessed | tf_op | source)
XLA Modules:
  0.0 2911.0 jit_solution(6459218927669588111)
XLA Ops:
  38.7 7.7 all-reduce.23
  59.2 8.0 convolution_convert_fusion.2
  73.7 15.6 all-gather.10.cloned.1.call-done
  101.8 10.2 maximum_convert_fusion
  112.1 24.2 fusion.141
  152.6 8.1 copy.358
  160.6 6.8 copy.362
  171.3 557.1 %while.68 = (s32[]{:T(128)}, f32[3,6,128,384]{3,2,1,0:T(8,128)S(1)}, s32[3]{0:T(128)}, f32[4,3,64,6,384]{4,2,3,1,0:T(8,128)}, f32[4,3,6,128,384]{4,3,2,1,0:T(8,1...) while((s32[]{:T(128)}, ...), condition=%wide.region_5.7_spmd.clone, body=%wide.region_3.6_spmd.clone.sunk | while | flops 2950088192 | bytes 50881240 | solution.py:110
  197.3 89.9 %custom-call.26 = f32[3,6,1,64,64]{3,4,2,1,0:T(8,128)} custom-call(f32[3,6,1,64,64]{4,3,2,1,0:T(8,128)} %fusion.427), custom_call_target="InvertDiagBlocksLowerTriangular" | custom-call | tf_op jit(solution)/shard_map/jvp(vmap())/while/body/eval_jaxpr/jit(_solve_triangular)/vmap()/triangular_solve/custom-call.1 | solution.py:65
  336.4 89.9 %custom-call.26 = f32[3,6,1,64,64]{3,4,2,1,0:T(8,128)} custom-call(f32[3,6,1,64,64]{4,3,2,1,0:T(8,128)} %fusion.427), custom_call_target="InvertDiagBlocksLowerTriangular" | custom-call | tf_op jit(solution)/shard_map/jvp(vmap())/while/body/eval_jaxpr/jit(_solve_triangular)/vmap()/triangular_solve/custom-call.1 | solution.py:65
  475.6 89.9 %custom-call.26 = f32[3,6,1,64,64]{3,4,2,1,0:T(8,128)} custom-call(f32[3,6,1,64,64]{4,3,2,1,0:T(8,128)} %fusion.427), custom_call_target="InvertDiagBlocksLowerTriangular" | custom-call | tf_op jit(solution)/shard_map/jvp(vmap())/while/body/eval_jaxpr/jit(_solve_triangular)/vmap()/triangular_solve/custom-call.1 | solution.py:65
  614.8 89.9 %custom-call.26 = f32[3,6,1,64,64]{3,4,2,1,0:T(8,128)} custom-call(f32[3,6,1,64,64]{4,3,2,1,0:T(8,128)} %fusion.427), custom_call_target="InvertDiagBlocksLowerTriangular" | custom-call | tf_op jit(solution)/shard_map/jvp(vmap())/while/body/eval_jaxpr/jit(_solve_triangular)/vmap()/triangular_solve/custom-call.1 | solution.py:65
  743.0 179.5 %while.66 = (s32[]{:T(128)}, f32[3,6,128,256]{3,2,1,0:T(8,128)S(1)}, f32[3,6,128,128]{3,2,1,0:T(8,128)}, f32[3,6,128,256]{3,2,1,0:T(8,128)}, s32[]{:T(128)}) while((s32[]{:T(128)}, f32[3,6,128,256]{3,2,1,0:T(8,128)S(1)}, f32[3,6,128,128]{3,2,1,0:T(8,128)}, f32[3,6,128,256]{3,2,1,0:T(8,128)}, s32[]{:T(128)}) %tuple.208), condition=%wide.region_7.9_spmd, body=%wide.region_6.8_spmd.sunk | while | flops 906559488 | bytes 17694820 | solution.py:235
  751.8 51.1 %collective-permute-done = f32[3,6,128,256]{3,2,1,0:T(8,128)S(1)} collective-permute-done((f32[3,6,128,256]{3,2,1,0:T(8,128)}, f32[3,6,128,256]{3,2,1,0:T(8,128)S(1)}, u32[]{:S(2)}, u32[]{:S(2)}) %collective-permute-start) | collective-permute-done | bytes 2359328 | tf_op jit(solution)/shard_map/while/body/eval_jaxpr/ppermute | solution.py:26
  812.8 50.3 %collective-permute-done = f32[3,6,128,256]{3,2,1,0:T(8,128)S(1)} collective-permute-done((f32[3,6,128,256]{3,2,1,0:T(8,128)}, f32[3,6,128,256]{3,2,1,0:T(8,128)S(1)}, u32[]{:S(2)}, u32[]{:S(2)}) %collective-permute-start) | collective-permute-done | bytes 2359328 | tf_op jit(solution)/shard_map/while/body/eval_jaxpr/ppermute | solution.py:26
  873.1 49.4 %collective-permute-done = f32[3,6,128,256]{3,2,1,0:T(8,128)S(1)} collective-permute-done((f32[3,6,128,256]{3,2,1,0:T(8,128)}, f32[3,6,128,256]{3,2,1,0:T(8,128)S(1)}, u32[]{:S(2)}, u32[]{:S(2)}) %collective-permute-start) | collective-permute-done | bytes 2359328 | tf_op jit(solution)/shard_map/while/body/eval_jaxpr/ppermute | solution.py:26
  922.5 8.2 multiply_reduce_fusion.11
  940.4 7.3 multiply_reduce_fusion.14
  947.8 16.4 fusion.200
  964.2 18.2 fusion.173
  982.4 18.1 multiply_reduce_fusion.12
  1011.4 6.9 reshape.533
  1018.3 10.4 multiply_reduce_fusion.9
  1030.6 8.8 fusion.150
  1045.1 106.6 %while.69 = (s32[]{:T(128)}, f32[3,6,128,256]{3,2,1,0:T(8,128)}, f32[3,6,128,128]{3,2,1,0:T(8,128)S(1)}, f32[3,6,128,256]{3,2,1,0:T(8,128)}, s32[]{:T(128)}, /*index=5*/s32[]{:T(128)}) while((s32[]{:T(128)}, f32[3,6,128,256]{3,2,1,0:T(8,128)}, f32[3,6,128,128]{3,2,1,0:T(8,128)S(1)}, f32[3,6,128,256]{3,2,1,0:T(8,128)}, ...), condition=%wide.region_13.15_spmd.clone, body=%wide.region_12.14_spmd.clone.sunk | while | flops 908328960 | bytes 15335543 | solution.py:290
  1051.3 27.0 collective-permute-done.1
  1088.2 25.8 collective-permute-done.1
  1123.8 24.8 collective-permute-done.1
  1172.7 723.2 %while.67 = (s32[]{:T(128)}, f32[3,6,128,384]{3,2,1,0:T(8,128)}, f32[4,3,64,6,128]{4,2,3,1,0:T(8,128)}, f32[4,3,64,6,128]{4,2,3,1,0:T(8,128)}, f32[4,3,64,6,384]...) while((s32[]{:T(128)}, f32[3,6,128,384]{3,2,1,0:T(8,128)}, ...), condition=%wide.region_24.26_spmd, body=%wide.region_14.25_spmd.sunk | while | flops 7891555328 | bytes 200632496 | solution.py:110
  1200.4 90.3 %custom-call.25 = f32[3,6,1,64,64]{3,4,2,1,0:T(8,128)} custom-call(f32[3,6,1,64,64]{4,3,2,1,0:T(8,128)} %get-tuple-element.1195), custom_call_target="InvertDiagBlocksLowerTriangular" | custom-call | tf_op jit(solution)/shard_map/transpose(jvp(vmap()))/while/body/eval_jaxpr/checkpoint/jit(_solve_triangular)/vmap()/triangular_solve | solution.py:65
  1379.1 90.0 %custom-call.25 = f32[3,6,1,64,64]{3,4,2,1,0:T(8,128)} custom-call(f32[3,6,1,64,64]{4,3,2,1,0:T(8,128)} %get-tuple-element.1195), custom_call_target="InvertDiagBlocksLowerTriangular" | custom-call | tf_op jit(solution)/shard_map/transpose(jvp(vmap()))/while/body/eval_jaxpr/checkpoint/jit(_solve_triangular)/vmap()/triangular_solve | solution.py:65
  1557.8 90.0 %custom-call.25 = f32[3,6,1,64,64]{3,4,2,1,0:T(8,128)} custom-call(f32[3,6,1,64,64]{4,3,2,1,0:T(8,128)} %get-tuple-element.1195), custom_call_target="InvertDiagBlocksLowerTriangular" | custom-call | tf_op jit(solution)/shard_map/transpose(jvp(vmap()))/while/body/eval_jaxpr/checkpoint/jit(_solve_triangular)/vmap()/triangular_solve | solution.py:65
  1736.3 90.2 %custom-call.25 = f32[3,6,1,64,64]{3,4,2,1,0:T(8,128)} custom-call(f32[3,6,1,64,64]{4,3,2,1,0:T(8,128)} %get-tuple-element.1195), custom_call_target="InvertDiagBlocksLowerTriangular" | custom-call | tf_op jit(solution)/shard_map/transpose(jvp(vmap()))/while/body/eval_jaxpr/checkpoint/jit(_solve_triangular)/vmap()/triangular_solve | solution.py:65
  1950.1 31.5 %multiply_reduce_fusion.8 = (f32[3072]{0:T(1024)S(1)}, f32[3072]{0:T(1024)S(1)}, f32[3072]{0:T(1024)S(1)}, f32[3072]{0:T(1024)S(1)}, f32[3,256,3072]{1,2,0:T(8,128)}) fusion(f32[3,259,3072]{1,2,0:T(8,128)} %maximum_convert_fusion, f32[3,256]{1,0:T(4,128)S(1)} %copy-done.87, f32[3,256]{1,0:T(4,128)S(1)} %copy-done.89, f32[3,256]{1,0:T(4,128)S(1)} %copy-done.85, ...), kind=kLoop, calls=%fused_computation.199 | loop fusion | flops 51892224 | bytes 66118656 | tf_op jit(solution)/shard_map/transpose(jvp())/reduce_sum | solution.py:82
  2004.7 8.7 convolution_convert_fusion.1
  2014.1 13.0 broadcast_multiply_fusion
  2027.1 15.9 pad_add_fusion
  2050.9 8.9 slice.213
  2068.6 26.1 scatter-add.4
  2094.7 9.4 bitcast_convert_fusion
  2106.0 18.1 convolution_convert_fusion
  2125.9 40.9 %all-reduce.27 = (f32[6]{0:T(128)}, f32[6]{0:T(128)}) all-reduce(f32[6]{0:T(128)S(1)} %negate_multiply_fusion, f32[6]{0:T(128)S(1)} %get-tuple-element.864), channel_id=1, replica_groups=mesh['dp'=2,'fsdp'=4,'seq'=4] {'dp','fsdp','seq'}, use_global_device_ids=true, to_apply=%region_44.46 | all-reduce | flops 12 | bytes 96 | tf_op jit(solution)/shard_map/psum | solution.py:383
  2173.1 10.8 add_convert_fusion.2
  2191.6 9.0 fusion.213
  2203.7 7.4 all-reduce.29
  2216.2 12.7 reduce-scatter.10.cloned.1.call-done
  2228.9 94.7 %reduce-scatter.18.cloned.1.call-done = bf16[256,5632]{1,0:T(8,128)(2,1)} async-done(((bf16[1024,5632]{1,0:T(8,128)(2,1)}), bf16[256,5632]{1,0:T(8,128)(2,1)}) %reduce-scatter.18.cloned.1.call-update) | async-done | bytes 2883600 | tf_op jit(solution)/shard_map/reduce_scatter | solution.py:361
  2323.5 580.4 %all-reduce.31 = (f32[256]{0:T(256)}, f32[256,3072]{1,0:T(8,128)}, f32[256,1536]{1,0:T(8,128)}, f32[256,12]{0,1:T(8,128)}, f32[4,768]{1,0:T(4,128)}, /*index=5*/...) all-reduce(f32[256]{0:T(256)S(1)} %dynamic-slice_convert_fusion.2, ...), channel_id=1, replica_groups=mesh['dp'=2,'fsdp'=4,'seq'=4] {'dp','seq'}, use_global_device_ids=true, to_apply=%region_30.32 | all-reduce | flops 3742272 | bytes 22454784 | tf_op jit(solution)/shard_map/psum | solution.py:368
  (884 shorter events, 870.3 us)
Async XLA Ops:
  7.2 52.0 %all-gather.8.cloned.1.call-start = ((), (), s32[]{:S(2)}) async-start(), calls=%async_computation.7 | async-start | bytes 7864320 | tf_op jit(solution)/shard_map/all_gather | solution.py:169
  7.9 12.4 copy-start.23
  7.9 81.4 %all-gather.10.cloned.1.call-start = ((), (), s32[]{:S(2)}) async-start(), calls=%async_computation.8 | async-start | bytes 3932160 | tf_op jit(solution)/shard_map/all_gather | solution.py:170
  8.7 931.7 %all-gather.12.cloned.1.call-start = ((), (), s32[]{:S(2)}) async-start(), calls=%async_computation.9 | async-start | bytes 3932160 | tf_op jit(solution)/shard_map/all_gather | solution.py:174
  9.4 11.4 copy-start.97
  9.4 16.6 copy-start.112
  9.5 938.3 %all-gather.14.cloned.1.call-start = ((), (), s32[]{:S(2)}) async-start(), calls=%async_computation.10 | async-start | bytes 14417920 | tf_op jit(solution)/shard_map/all_gather | solution.py:176
  10.0 954.2 %all-gather.16.cloned.1.call-start = ((), (), s32[]{:S(2)}) async-start(), calls=%async_computation.11 | async-start | bytes 7208960 | tf_op jit(solution)/shard_map/all_gather | solution.py:177
  10.2 43.6 %collective-permute-start.2 = (s32[3,3]{1,0:T(4,128)S(1)}, s32[3,3]{1,0:T(4,128)S(1)}, u32[]{:S(2)}, u32[]{:S(2)}) collective-permute-start(s32[3,3]{1,0:T(4,128)S(1)} %slice.155), channel_id=1, source_target_pairs={{0,1},{1,2},{2,3},{4,5},{5,6},{6,7},{8,9},{9,10},{10,11},{12,13},{... | collective-permute-start | bytes 116 | tf_op jit(solution)/shard_map/ppermute | solution.py:26
  15.1 2168.8 %reduce-scatter.22.cloned.1.call-start = ((), (), s32[]{:S(2)}) async-start(), calls=%async_computation.18 | async-start | bytes 983040
  20.4 10.2 copy-start.80
  27.6 10.8 copy-start.110
  27.6 19.3 copy-start.111
  36.5 75.5 %copy-start.72 = (f32[1,3072]{1,0:T(1,128)}, f32[1,3072]{1,0:T(1,128)S(1)}, u32[]{:S(2)}) copy-start(f32[1,3072]{1,0:T(1,128)S(1)} %get-tuple-element.913) | copy-start | bytes 36868
  36.5 75.5 %copy-start.74 = (f32[1,3072]{1,0:T(1,128)}, f32[1,3072]{1,0:T(1,128)S(1)}, u32[]{:S(2)}) copy-start(f32[1,3072]{1,0:T(1,128)S(1)} %get-tuple-element.914) | copy-start | bytes 36868
  36.5 75.5 %copy-start.76 = (f32[1,3072]{1,0:T(1,128)}, f32[1,3072]{1,0:T(1,128)S(1)}, u32[]{:S(2)}) copy-start(f32[1,3072]{1,0:T(1,128)S(1)} %get-tuple-element.915) | copy-start | bytes 36868
  36.5 75.5 %copy-start.78 = (f32[1,3072]{1,0:T(1,128)}, f32[1,3072]{1,0:T(1,128)S(1)}, u32[]{:S(2)}) copy-start(f32[1,3072]{1,0:T(1,128)S(1)} %get-tuple-element.916) | copy-start | bytes 36868
  53.8 58.2 %copy-start.84 = (f32[3,256]{1,0:T(4,128)}, f32[3,256]{1,0:T(4,128)S(1)}, u32[]{:S(2)}) copy-start(f32[3,256]{1,0:T(4,128)S(1)} %get-tuple-element.917) | copy-start | bytes 9220
  53.8 58.2 %copy-start.86 = (f32[3,256]{1,0:T(4,128)}, f32[3,256]{1,0:T(4,128)S(1)}, u32[]{:S(2)}) copy-start(f32[3,256]{1,0:T(4,128)S(1)} %get-tuple-element.918) | copy-start | bytes 9220
  53.8 58.2 %copy-start.88 = (f32[3,256]{1,0:T(4,128)}, f32[3,256]{1,0:T(4,128)S(1)}, u32[]{:S(2)}) copy-start(f32[3,256]{1,0:T(4,128)S(1)} %get-tuple-element.919) | copy-start | bytes 9220
  69.5 31.2 %collective-permute-start.3 = (bf16[3,3,3072]{2,1,0:T(4,128)(2,1)S(1)}, bf16[3,3,3072]{2,1,0:T(4,128)(2,1)S(1)}, u32[]{:S(2)}, u32[]{:S(2)}) collective-permute-start(bf16[3,3,3072]{2,1,0:T(4,128)(2,1)S(1)} %slice.192), channel_id=1, source_target_pairs={{0,1},{1,2},{2,3},{4,5},{5,6},{6,7},{8,9},{9,10},{10,11},{12,13},{... | collective-permute-start | bytes 165896 | tf_op jit(solution)/shard_map/ppermute | solution.py:26
  139.9 28.4 copy-start.27
  748.6 54.3 %collective-permute-start = (f32[3,6,128,256]{3,2,1,0:T(8,128)}, f32[3,6,128,256]{3,2,1,0:T(8,128)S(1)}, u32[]{:S(2)}, u32[]{:S(2)}) collective-permute-start(f32[3,6,128,256]{3,2,1,0:T(8,128)} %convolution_add_fusion.2), channel_id=1, source_target_pairs={{0,1},{1,2},{2,3},{4,5},{5,6},{6,7},{8,9},{9,10},{10,11},{12,13},{... | collective-permute-start | bytes 7077896 | tf_op jit(solution)/shard_map/while/body/eval_jaxpr/ppermute | solution.py:26
  808.4 54.7 %collective-permute-start = (f32[3,6,128,256]{3,2,1,0:T(8,128)}, f32[3,6,128,256]{3,2,1,0:T(8,128)S(1)}, u32[]{:S(2)}, u32[]{:S(2)}) collective-permute-start(f32[3,6,128,256]{3,2,1,0:T(8,128)} %convolution_add_fusion.2), channel_id=1, source_target_pairs={{0,1},{1,2},{2,3},{4,5},{5,6},{6,7},{8,9},{9,10},{10,11},{12,13},{... | collective-permute-start | bytes 7077896 | tf_op jit(solution)/shard_map/while/body/eval_jaxpr/ppermute | solution.py:26
  868.7 53.8 %collective-permute-start = (f32[3,6,128,256]{3,2,1,0:T(8,128)}, f32[3,6,128,256]{3,2,1,0:T(8,128)S(1)}, u32[]{:S(2)}, u32[]{:S(2)}) collective-permute-start(f32[3,6,128,256]{3,2,1,0:T(8,128)} %convolution_add_fusion.2), channel_id=1, source_target_pairs={{0,1},{1,2},{2,3},{4,5},{5,6},{6,7},{8,9},{9,10},{10,11},{12,13},{... | collective-permute-start | bytes 7077896 | tf_op jit(solution)/shard_map/while/body/eval_jaxpr/ppermute | solution.py:26
  947.7 53.5 %copy-start.95 = (f32[768]{0:T(1024)}, f32[768]{0:T(1024)S(1)}, u32[]{:S(2)}) copy-start(f32[768]{0:T(1024)S(1)} %fusion.196) | copy-start | bytes 9220
  1018.3 10.4 slice-start
  1018.3 10.4 copy-start.71
  1018.3 10.4 slice-start.1
  1018.3 10.4 copy-start.65
  1050.0 28.3 collective-permute-start.1
  1086.9 27.0 collective-permute-start.1
  1122.5 26.1 collective-permute-start.1
  1950.1 32.9 %copy-start.59 = (f32[3,256,12]{1,2,0:T(8,128)S(1)}, f32[3,256,12]{1,2,0:T(8,128)}, u32[]{:S(2)}) copy-start(f32[3,256,12]{1,2,0:T(8,128)} %copy-done.58) | copy-start | bytes 110596
  1950.1 32.9 %copy-start.102 = (f32[6]{0:T(128)S(1)}, f32[6]{0:T(128)}, u32[]{:S(2)}) copy-start(f32[6]{0:T(128)} %param.36) | copy-start | bytes 76
  1950.1 32.9 %copy-start.104 = (f32[6]{0:T(128)S(1)}, f32[6]{0:T(128)}, u32[]{:S(2)}) copy-start(f32[6]{0:T(128)} %copy-done.103) | copy-start | bytes 76
  1950.1 33.2 %copy-start.38 = (bf16[3,256,1024]{2,1,0:T(8,128)(2,1)S(1)}, bf16[3,256,1024]{2,1,0:T(8,128)(2,1)}, u32[]{:S(2)}) copy-start(bf16[3,256,1024]{2,1,0:T(8,128)(2,1)} %copy-done.36) | copy-start | bytes 4718596
  1982.9 202.0 %reduce-scatter.14.cloned.1.call-start = ((), (), s32[]{:S(2)}) async-start(), calls=%async_computation.14 | async-start | bytes 40960 | tf_op jit(solution)/shard_map/reduce_scatter | solution.py:346
  1989.5 226.7 %reduce-scatter.12.cloned.1.call-start = ((), (), s32[]{:S(2)}) async-start(), calls=%async_computation.13 | async-start | bytes 3932160 | tf_op jit(solution)/shard_map/reduce_scatter | solution.py:343
  1995.7 220.5 %reduce-scatter.16.cloned.1.call-start = ((), (), s32[]{:S(2)}) async-start(), calls=%async_computation.15 | async-start | bytes 3932160 | tf_op jit(solution)/shard_map/reduce_scatter | solution.py:355
  2003.3 212.9 %reduce-scatter.20.cloned.1.call-start = ((), (), s32[]{:S(2)}) async-start(), calls=%async_computation.17 | async-start | bytes 7208960 | tf_op jit(solution)/shard_map/reduce_scatter | solution.py:364
  2013.4 215.5 %reduce-scatter.10.cloned.1.call-start = ((), (), s32[]{:S(2)}) async-start(), calls=%async_computation.12 | async-start | bytes 7864320 | tf_op jit(solution)/shard_map/reduce_scatter | solution.py:340
  2049.6 10.2 collective-permute-start.4
  2068.6 26.1 copy-start.39
  2104.1 219.4 %reduce-scatter.18.cloned.1.call-start = ((), (), s32[]{:S(2)}) async-start(), calls=%async_computation.16 | async-start | bytes 14417920 | tf_op jit(solution)/shard_map/reduce_scatter | solution.py:361
  2124.1 42.7 %copy-start.50 = (bf16[1024,1536]{1,0:T(8,128)(2,1)S(1)}, bf16[1024,1536]{1,0:T(8,128)(2,1)}, u32[]{:S(2)}) copy-start(bf16[1024,1536]{1,0:T(8,128)(2,1)} %all-gather.10.cloned.1.call-done) | copy-start | bytes 9437188
  2200.7 10.6 copy-start.91
  2211.3 112.3 %copy-start.98 = (bf16[256,12]{0,1:T(8,128)(2,1)S(1)}, bf16[256,12]{0,1:T(8,128)(2,1)}, u32[]{:S(2)}) copy-start(bf16[256,12]{0,1:T(8,128)(2,1)} %reduce-scatter.14.cloned.1.call-done) | copy-start | bytes 18436
  (172 other events, 750.9 us)
Sparse Core Ops, SparseCore 0:
  9.6 49.5 all-gather.7
  60.7 28.5 all-gather.9
  90.9 28.4 all-gather.11
  120.8 76.1 all-gather.13
  198.4 43.8 all-gather.15
  1983.0 21.9 reduce-scatter.21
  2008.1 19.3 reduce-scatter.13
  2030.1 37.9 reduce-scatter.11
  2070.8 37.9 reduce-scatter.15
  2111.7 55.9 reduce-scatter.19
  2170.5 58.3 reduce-scatter.9
  2231.3 92.1 reduce-scatter.17
where the time goes:
time: 2920 us; the launch traced here: 2910 us
  other arithmetic  949 us (32%)
  blocking collectives  657 us (22%)
  matrix products  573 us (20%)
  waiting for transfers between devices  359 us (12%)
  local copies, waits for them, and re-layouts  317 us (11%)
    another operation x16, other arithmetic, block_step(): fresh = jax.scipy.linalg.solve_triangular(system, target, lower=True)  728 us
    psum x1, blocking collectives, local(): lax.psum((shard_mixer, shard_qkv, shard_gate, shard_decay, shard_conv, sh...  580 us
    ppermute x9, waiting for transfers between devices, passed_along(): lax.ppermute(value, axis, [(source, source + steps) for source in range(l...  228 us
    reduce_scatter x1, waiting for transfers between devices, local(): lax.psum_scatter(grad_ffn_in.astype(jnp.bfloat16), 'fsdp', scatter_dimens...  94.7 us
    dot_general x16, matrix products, block_step(): key_state = jnp.einsum('thd,hdw->htw', key, state, precision=PRECISE)  73.4 us
    dot_general x16, matrix products, block_step(): query_state = jnp.einsum('thd,hdw->htw', query, state, precision=PRECISE)  67.1 us
  transfers between devices with their start and end apart: 21, of which 10 were waited for; matrix products, arithmetic and copies ran while one was open for 31% of the time, Pallas kernels for 0%

commit v1 on v0

v1 whole, which is shorter than its diff:
```python
from functools import partial

import jax
import jax.numpy as jnp
from jax import lax
from jax.experimental import pallas as pl
from jax.experimental.pallas import tpu as pltpu
from jax.sharding import PartitionSpec as P

H = 6
DK = 128
DV = 256
CONV = 4
KD = 768
VD = 1536
C3 = 3072
RIM = 8

EPSILON = 1e-06
HEAD_EPSILON = 0.001
PRECISE = lax.Precision.HIGHEST
LOW = jnp.bfloat16
F32 = jnp.float32

NN = (((1,), (0,)), ((), ()))
NT = (((1,), (1,)), ((), ()))
TN = (((0,), (0,)), ((), ()))


def mm(left, right, dims=NN):
    return lax.dot_general(
        left.astype(LOW), right.astype(LOW), dims, preferred_element_type=F32
    )


def passed_along(value, axis, steps):
    count = lax.axis_size(axis)
    leading, last = (max(0, -steps), min(count, count - steps))
    return lax.ppermute(value, axis, [(source, source + steps) for source in range(leading, last)])


def rms_norm(values, gain):
    return values * lax.rsqrt(jnp.mean(values * values, axis=-1, keepdims=True) + EPSILON) * gain


def swiglu(gate_up):
    half = gate_up.shape[1] // 2
    return jax.nn.silu(gate_up[:, :half]) * gate_up[:, half:]


def iotas(count):
    shape = (count, count)
    return lax.broadcasted_iota(jnp.int32, shape, 0), lax.broadcasted_iota(jnp.int32, shape, 1)


def conv_head(s, parts, rims, taps, cols, pad_ref):
    at = 0
    for part, rim in zip(parts, rims):
        width = part.shape[-1]
        pad_ref[s, 0:RIM, at : at + width] = rim[s].astype(F32)
        pad_ref[s, RIM:, at : at + width] = part[s].astype(F32)
        at += width
    count = parts[0].shape[1]
    shifted = []
    total = None
    for tap in range(CONV):
        first = RIM - (CONV - 1) + tap
        values = pad_ref[s, first : first + count, :]
        if tap < CONV - 1:
            values = values * cols[:, 4 + tap : 5 + tap]
        shifted.append(values)
        term = values * taps[tap : tap + 1, :]
        total = term if total is None else total + term
    sig = jax.nn.sigmoid(total)
    return shifted, total, sig, total * sig


def unit(values):
    scale = lax.rsqrt(jnp.sum(values * values, axis=-1, keepdims=True) + EPSILON)
    return values * scale, scale


def decays(cols, rows, order, other):
    causal = (cols[:, 7:8] == rows[1:2, :]) & (order >= other)
    decay = jnp.exp(jnp.where(causal, cols[:, 0:1] - rows[0:1, :], -1e30))
    return decay, jnp.where(order > other, decay, 0.0)


def forward_kernel(
    q_ref, k_ref, v_ref, rq_ref, rk_ref, rv_ref, wq_ref, wk_ref, wv_ref, cols_ref, rows_ref,
    t_ref, uw_ref, local_ref, carried_ref, through_ref, offsets_ref, pad_ref,
):
    seqs, count = q_ref.shape[0], q_ref.shape[1]
    order, other = iotas(count)
    taps = jnp.concatenate([wq_ref[...], wk_ref[...], wv_ref[...]], axis=1)
    state = []
    for s in range(seqs):
        cols, rows = cols_ref[0, s], rows_ref[0, s]
        _, _, _, out = conv_head(
            s, (q_ref, k_ref, v_ref), (rq_ref, rk_ref, rv_ref), taps, cols, pad_ref
        )
        query = (unit(out[:, :DK])[0] * DK ** (-0.5)).astype(LOW)
        key = unit(out[:, DK : 2 * DK])[0].astype(LOW)
        value = out[:, 2 * DK :].astype(LOW)
        decay, strict = decays(cols, rows, order, other)
        beta, start, end = cols[:, 1:2], cols[:, 2:3], cols[:, 3:4]
        lower = beta * mm(key, key, NT) * strict
        attend = (mm(query, key, NT) * decay).astype(LOW)
        keyf = key.astype(F32)
        target = jnp.concatenate([beta * value.astype(F32), beta * start * keyf], axis=1).astype(LOW)
        state.append(dict(lower=lower, attend=attend, target=target, query=query,
                          ending=(end * keyf).astype(LOW), start=start))
    eye = (order == other).astype(F32)
    inverse = [eye - jnp.where((order >> 1 == other >> 1) & (order > other), x["lower"], 0.0) for x in state]
    level = 1
    while (2 << level) <= count:
        pick = (
            (order >> (level + 1) == other >> (level + 1))
            & ((order >> level) & 1 == 1)
            & ((other >> level) & 1 == 0)
        )
        half = []
        for s in range(seqs):
            half.append(mm(jnp.where(pick, state[s]["lower"], 0.0), inverse[s]))
        for s in range(seqs):
            inverse[s] = inverse[s] - mm(inverse[s], half[s])
        level += 1
    for s in range(seqs):
        x = state[s]
        t = inverse[s].astype(LOW)
        t_ref[0, s] = t
        uw = mm(t, x["target"]).astype(LOW)
        uw_ref[0, s] = uw
        both = mm(x["attend"], uw)
        local_ref[s] = both[:, :DV]
        carried_ref[s] = (x["start"] * x["query"].astype(F32) - both[:, DV:]).astype(LOW)
        ends = mm(x["ending"], uw, TN)
        offsets_ref[0, s] = ends[:, :DV]
        small, small_other = iotas(DK)
        last = x["start"][count - 1 : count, :]
        through_ref[0, s] = (jnp.where(small == small_other, last, 0.0) - ends[:, DV:]).astype(LOW)


def heads_kernel(local_ref, carried_ref, state_ref, gate_ref, gain_ref, heads_ref):
    for s in range(local_ref.shape[0]):
        mixed = local_ref[s] + mm(carried_ref[s], state_ref[0, s])
        scale = lax.rsqrt(jnp.mean(mixed * mixed, axis=-1, keepdims=True) + HEAD_EPSILON)
        gate = gate_ref[s]
        heads_ref[s] = (mixed * scale * gain_ref[...] * (gate * jax.nn.sigmoid(gate))).astype(LOW)


def heads_back_kernel(
    local_ref, carried_ref, state_ref, gate_ref, gain_ref, grad_ref,
    mixed_ref, ggate_ref, ggain_ref, gstate_ref,
):
    gain = gain_ref[...]
    total = jnp.zeros_like(gain)
    for s in range(local_ref.shape[0]):
        mixed = local_ref[s] + mm(carried_ref[s], state_ref[0, s])
        scale = lax.rsqrt(jnp.mean(mixed * mixed, axis=-1, keepdims=True) + HEAD_EPSILON)
        normed = mixed * scale
        gate = gate_ref[s]
        sig = jax.nn.sigmoid(gate)
        act = gate * sig
        grad = grad_ref[s]
        gn = grad * normed
        total = total + jnp.sum(gn * act, axis=0, keepdims=True)
        ggate_ref[s] = (gn * gain * (sig + act * (1.0 - sig))).astype(LOW)
        e = grad * gain * act
        gmixed = (scale * (e - normed * jnp.mean(e * normed, axis=-1, keepdims=True))).astype(LOW)
        mixed_ref[s] = gmixed
        gstate_ref[0, s] = mm(carried_ref[s], gmixed, TN)
    ggain_ref[0] = total


def backward_kernel(
    q_ref, k_ref, v_ref, rq_ref, rk_ref, rv_ref, wq_ref, wk_ref, wv_ref, cols_ref, rows_ref,
    t_ref, uw_ref, state_ref, gout_ref, gend_ref,
    gpre_ref, grim_ref, gtail_ref, gtaps_ref, gcols_ref, pad_ref, shift_ref,
):
    head = pl.program_id(0)
    seqs, count = q_ref.shape[0], q_ref.shape[1]
    order, other = iotas(count)
    taps = jnp.concatenate([wq_ref[...], wk_ref[...], wv_ref[...]], axis=1)
    before = (order < other).astype(LOW)
    gtaps = [None] * CONV
    at = (
        pl.ds(pl.multiple_of(head * DK, DK), DK),
        pl.ds(pl.multiple_of(KD + head * DK, DK), DK),
        pl.ds(pl.multiple_of(2 * KD + head * DV, DV), DV),
    )
    spans = ((0, DK), (DK, 2 * DK), (2 * DK, 2 * DK + DV))
    for s in range(seqs):
        cols, rows = cols_ref[0, s], rows_ref[0, s]
        shifted, total, sig, out = conv_head(
            s, (q_ref, k_ref, v_ref), (rq_ref, rk_ref, rv_ref), taps, cols, pad_ref
        )
        qhat, qscale = unit(out[:, :DK])
        khat, kscale = unit(out[:, DK : 2 * DK])
        query = (qhat * DK ** (-0.5)).astype(LOW)
        key = khat.astype(LOW)
        value = out[:, 2 * DK :]
        decay, strict = decays(cols, rows, order, other)
        beta, start, end = cols[:, 1:2], cols[:, 2:3], cols[:, 3:4]
        keyf = key.astype(F32)
        weight = beta * strict
        lower = mm(key, key, NT) * weight
        attend = mm(query, key, NT) * decay
        state = state_ref[0, s]
        gend = gend_ref[0, s]
        gout = gout_ref[s]
        uw = uw_ref[0, s]
        fresh = uw[:, :DV].astype(F32) - mm(uw[:, DV:], state)
        freshl = fresh.astype(LOW)
        gfresh = mm(attend, gout, TN) + mm(end * keyf, gend)
        gtarget = mm(t_ref[0, s], gfresh, TN)
        gattend = mm(gout, freshl, NT)
        glower = -mm(gtarget, freshl, NT)
        cross = gattend * attend + glower * lower
        high = cross.astype(LOW)
        reach = mm(high, before) + mm(cross - high.astype(F32), before)
        gqk = (gattend * decay).astype(LOW)
        gkk = (glower * weight).astype(LOW)
        gout_state = mm(gout, state, NT)
        gtarget_state = beta * mm(gtarget, state, NT)
        ends = mm(freshl, gend, NT)
        gquery = mm(gqk, key) + start * gout_state
        gkey = (
            mm(gqk, query, TN)
            + mm(gkk, key)
            + mm(gkk, key, TN)
            - start * gtarget_state
            + end * ends
        )
        gvalue = beta * gtarget
        from_start = start * jnp.sum(
            query.astype(F32) * gout_state - keyf * gtarget_state, axis=-1, keepdims=True
        )
        to_end = end * jnp.sum(keyf * ends, axis=-1, keepdims=True)
        through = jnp.sum(gend.astype(F32) * state.astype(F32)) * start[count - 1 : count, :]
        glog = jnp.sum(jnp.where(order >= other, reach + from_start, to_end), axis=0, keepdims=True)
        gbeta = jnp.sum(gtarget * fresh, axis=-1, keepdims=True) * (1.0 - beta)
        gbeta = jnp.sum(jnp.where(order == other, gbeta, 0.0), axis=0, keepdims=True)
        gcols_ref[0, s] = jnp.concatenate(
            [glog + through, gbeta, jnp.zeros((6, count), F32)], axis=0
        )
        gq = gquery * DK ** (-0.5)
        gq = qscale * (gq - qhat * jnp.sum(qhat * gq, axis=-1, keepdims=True))
        gk = kscale * (gkey - khat * jnp.sum(khat * gkey, axis=-1, keepdims=True))
        gconv = jnp.concatenate([gq, gk, gvalue], axis=1) * (sig + out * (1.0 - sig))
        for tap in range(CONV):
            part = jnp.sum(gconv * shifted[tap], axis=0, keepdims=True)
            gtaps[tap] = part if gtaps[tap] is None else gtaps[tap] + part
        width = gconv.shape[1]
        blank = jnp.zeros((RIM, width), F32)
        back = None
        for tap in range(CONV):
            term = gconv * taps[tap : tap + 1, :]
            if tap < CONV - 1:
                term = term * cols[:, 4 + tap : 5 + tap]
            shift_ref[tap, 0:RIM, :] = blank
            shift_ref[tap, RIM : RIM + count, :] = term
            shift_ref[tap, RIM + count :, :] = blank
            first = CONV - 1 - tap
            moved = shift_ref[tap, first : first + RIM + count, :]
            back = moved if back is None else back + moved
        for place, (low, top) in zip(at, spans):
            gpre_ref[s, :, place] = back[RIM:, low:top].astype(LOW)
            grim_ref[s, :, place] = back[:RIM, low:top]
            gtail_ref[s, :, place] = back[count:, low:top]
    for tap in range(CONV):
        for place, (low, top) in zip(at, spans):
            gtaps_ref[tap : tap + 1, place] = gtaps[tap][:, low:top]


def head_specs(seqs, count):
    def cut(rows, width, first):
        return pl.BlockSpec((seqs, rows, width), lambda h: (0, 0, first + h))

    def taps(width, first):
        return pl.BlockSpec((CONV, width), lambda h: (0, first + h))

    channel = [cut(count, DK, 0), cut(count, DK, H), cut(count, DV, H)]
    rim = [cut(RIM, DK, 0), cut(RIM, DK, H), cut(RIM, DV, H)]
    weight = [taps(DK, 0), taps(DK, H), taps(DV, H)]
    return channel + rim + weight + [per_head(seqs, count, 8), per_head(seqs, 8, count)]


def per_head(seqs, rows, width):
    return pl.BlockSpec((1, seqs, rows, width), lambda h: (h, 0, 0, 0))


def by_column(seqs, count, width):
    return pl.BlockSpec((seqs, count, width), lambda h: (0, 0, h))


def whole(*shape):
    return pl.BlockSpec(shape, lambda h: (0,) * len(shape))


def params(limit=48):
    return pltpu.CompilerParams(
        dimension_semantics=("arbitrary",), vmem_limit_bytes=limit * 2**20
    )


def mixer_forward(pre_conv, rim, taps, cols, rows):
    seqs, count = pre_conv.shape[0], pre_conv.shape[1]
    return pl.pallas_call(
        forward_kernel,
        grid=(H,),
        in_specs=head_specs(seqs, count),
        out_specs=[
            per_head(seqs, count, count),
            per_head(seqs, count, DV + DK),
            by_column(seqs, count, DV),
            by_column(seqs, count, DK),
            per_head(seqs, DK, DK),
            per_head(seqs, DK, DV),
        ],
        out_shape=[
            jax.ShapeDtypeStruct((H, seqs, count, count), LOW),
            jax.ShapeDtypeStruct((H, seqs, count, DV + DK), LOW),
            jax.ShapeDtypeStruct((seqs, count, VD), F32),
            jax.ShapeDtypeStruct((seqs, count, KD), LOW),
            jax.ShapeDtypeStruct((H, seqs, DK, DK), LOW),
            jax.ShapeDtypeStruct((H, seqs, DK, DV), F32),
        ],
        scratch_shapes=[pltpu.VMEM((seqs, RIM + count, 2 * DK + DV), F32)],
        compiler_params=params(),
        name="mixer_forward",
    )(pre_conv, pre_conv, pre_conv, rim, rim, rim, taps, taps, taps, cols, rows)


def heads_forward(local_part, carried, state, gate, gain):
    seqs, count = local_part.shape[0], local_part.shape[1]
    return pl.pallas_call(
        heads_kernel,
        grid=(H,),
        in_specs=[
            by_column(seqs, count, DV),
            by_column(seqs, count, DK),
            per_head(seqs, DK, DV),
            by_column(seqs, count, DV),
            whole(1, DV),
        ],
        out_specs=by_column(seqs, count, DV),
        out_shape=jax.ShapeDtypeStruct((seqs, count, VD), LOW),
        compiler_params=params(),
        name="heads_forward",
    )(local_part, carried, state, gate, gain)


def heads_backward(local_part, carried, state, gate, gain, grad):
    seqs, count = local_part.shape[0], local_part.shape[1]
    return pl.pallas_call(
        heads_back_kernel,
        grid=(H,),
        in_specs=[
            by_column(seqs, count, DV),
            by_column(seqs, count, DK),
            per_head(seqs, DK, DV),
            by_column(seqs, count, DV),
            whole(1, DV),
            by_column(seqs, count, DV),
        ],
        out_specs=[
            by_column(seqs, count, DV),
            by_column(seqs, count, DV),
            pl.BlockSpec((1, 1, DV), lambda h: (h, 0, 0)),
            per_head(seqs, DK, DV),
        ],
        out_shape=[
            jax.ShapeDtypeStruct((seqs, count, VD), LOW),
            jax.ShapeDtypeStruct((seqs, count, VD), LOW),
            jax.ShapeDtypeStruct((H, 1, DV), F32),
            jax.ShapeDtypeStruct((H, seqs, DK, DV), F32),
        ],
        compiler_params=params(),
        name="heads_backward",
    )(local_part, carried, state, gate, gain, grad)


def mixer_backward(pre_conv, rim, taps, cols, rows, t, uw, state, gout, gend):
    seqs, count = pre_conv.shape[0], pre_conv.shape[1]
    return pl.pallas_call(
        backward_kernel,
        grid=(H,),
        in_specs=head_specs(seqs, count)
        + [
            per_head(seqs, count, count),
            per_head(seqs, count, DV + DK),
            per_head(seqs, DK, DV),
            by_column(seqs, count, DV),
            per_head(seqs, DK, DV),
        ],
        out_specs=[
            whole(seqs, count, C3),
            whole(seqs, RIM, C3),
            whole(seqs, RIM, C3),
            whole(CONV, C3),
            per_head(seqs, 8, count),
        ],
        out_shape=[
            jax.ShapeDtypeStruct((seqs, count, C3), LOW),
            jax.ShapeDtypeStruct((seqs, RIM, C3), F32),
            jax.ShapeDtypeStruct((seqs, RIM, C3), F32),
            jax.ShapeDtypeStruct((CONV, C3), F32),
            jax.ShapeDtypeStruct((H, seqs, 8, count), F32),
        ],
        scratch_shapes=[
            pltpu.VMEM((seqs, RIM + count, 2 * DK + DV), F32),
            pltpu.VMEM((CONV, 2 * RIM + count, 2 * DK + DV), F32),
        ],
        compiler_params=params(),
        name="mixer_backward",
    )(
        pre_conv, pre_conv, pre_conv, rim, rim, rim, taps, taps, taps, cols, rows,
        t, uw, state, gout, gend,
    )


def token_columns(log_decay, beta, seg_ids, rim_seg):
    seqs, count = seg_ids.shape
    order = jnp.arange(count, dtype=jnp.int32)
    ones = (order[:, None] >= order[None, :]).astype(F32)
    running = jnp.einsum("ts,bsh->hbt", ones, log_decay, precision=PRECISE)
    ids = jnp.broadcast_to(seg_ids.astype(F32)[None], running.shape)
    alive = (seg_ids == rim_seg[:, -1:]).astype(F32)[None]
    ending = (seg_ids == seg_ids[:, -1:]).astype(F32)[None]
    start = jnp.exp(running) * alive
    end = jnp.exp(running[:, :, -1:] - running) * ending
    padded_ids = jnp.concatenate([rim_seg, seg_ids], axis=1)
    keeps = [
        jnp.broadcast_to(
            (padded_ids[:, tap : tap + count] == seg_ids).astype(F32)[None], running.shape
        )
        for tap in range(CONV - 1)
    ]
    betas = jnp.transpose(beta, (2, 0, 1))
    cols = jnp.stack([running, betas, start, end] + keeps + [ids], axis=-1)
    blank = jnp.zeros_like(running)
    rows = jnp.stack([running, ids] + [blank] * 6, axis=2)
    return cols, rows


def local(
    inputs,
    segment_ids,
    out_cotangent,
    mixer_gain,
    qkv_weight,
    gate_weight,
    decay_weight,
    conv_weight,
    decay_log,
    decay_bias,
    head_gain,
    out_weight,
    ffn_gain,
    ffn_in_weight,
    down_weight,
):
    batch, length, width = inputs.shape
    count = batch * length
    margin = CONV - 1
    group = lax.axis_size("fsdp")
    share = width // group
    small = jnp.concatenate(
        [
            mixer_gain,
            ffn_gain,
            head_gain,
            conv_weight.reshape(-1),
            decay_weight.reshape(-1),
        ]
    )
    small = lax.all_gather(small, "fsdp", axis=0)
    cuts = [mixer_gain.size, ffn_gain.size, head_gain.size, conv_weight.size, decay_weight.size]
    pieces, first = [], 0
    for size in cuts:
        pieces.append(small[:, first : first + size])
        first += size
    full_mixer_gain = pieces[0].reshape(-1).astype(F32)
    full_ffn_gain = pieces[1].reshape(-1).astype(F32)
    full_head_gain = pieces[2].reshape(1, -1).astype(F32)
    full_conv = jnp.transpose(pieces[3].reshape(group, CONV, -1), (1, 0, 2)).reshape(CONV, C3)
    full_conv = full_conv.astype(F32)
    full_decay = pieces[4].reshape(width, 2 * H)
    full_qkv = lax.all_gather(qkv_weight, "fsdp", axis=0, tiled=True)
    full_gate = lax.all_gather(gate_weight, "fsdp", axis=0, tiled=True)
    full_out = lax.all_gather(out_weight, "fsdp", axis=0, tiled=True)
    full_ffn_in = lax.all_gather(ffn_in_weight, "fsdp", axis=0, tiled=True)
    full_down = lax.all_gather(down_weight, "fsdp", axis=0, tiled=True)

    rows_in = inputs.astype(F32).reshape(count, width)
    normed, pull_mixer_norm = jax.vjp(rms_norm, rows_in, full_mixer_gain)
    normed_low = normed.astype(LOW)
    pre_conv = (
        jnp.dot(normed_low, full_qkv, preferred_element_type=F32)
        .astype(LOW)
        .reshape(batch, length, C3)
    )
    gate_out = jnp.dot(normed_low, full_gate, preferred_element_type=F32)
    gate_out = gate_out.reshape(batch, length, VD)
    decay_in = jnp.dot(normed_low, full_decay, preferred_element_type=F32).reshape(
        batch, length, 2 * H
    )
    rim_seg = passed_along(segment_ids[:, length - margin :], "seq", 1)
    rim = passed_along(pre_conv[:, length - margin :, :], "seq", 1).astype(F32)
    rim = jnp.pad(rim, ((0, 0), (RIM - margin, 0), (0, 0)))
    rate = jnp.exp(decay_log)
    shifted_decay = decay_in[:, :, :H] + decay_bias
    log_decay = -rate * jax.nn.softplus(shifted_decay)
    beta = jax.nn.sigmoid(decay_in[:, :, H:])
    cols, rows = token_columns(log_decay, beta, segment_ids, rim_seg)
    t, uw, local_part, carried, through, offsets = mixer_forward(
        pre_conv, rim, full_conv, cols, rows
    )

    steps = lax.axis_size("seq") - 1
    state_in = jnp.zeros(offsets.shape, LOW)
    for step in range(steps):
        leaving = offsets
        if step > 0:
            leaving = offsets + jnp.einsum(
                "hsij,hsjv->hsiv", through, state_in, preferred_element_type=F32
            )
        state_in = passed_along(leaving.astype(LOW), "seq", 1)

    heads_low = heads_forward(local_part, carried, state_in, gate_out, full_head_gain)
    heads_low = heads_low.reshape(count, VD)
    middle = rows_in + jnp.dot(heads_low, full_out, preferred_element_type=F32)
    normed_ffn, pull_ffn_norm = jax.vjp(rms_norm, middle, full_ffn_gain)
    normed_ffn_low = normed_ffn.astype(LOW)
    gate_up = jnp.dot(normed_ffn_low, full_ffn_in, preferred_element_type=F32)
    hidden, pull_swiglu = jax.vjp(swiglu, gate_up)
    hidden_low = hidden.astype(LOW)
    result = middle + jnp.dot(hidden_low, full_down, preferred_element_type=F32)
    output = result.astype(LOW).reshape(batch, length, width)

    def reduced(grad):
        shard = lax.psum_scatter(grad.astype(LOW), "fsdp", scatter_dimension=0, tiled=True)
        return lax.psum(shard, ("dp", "seq")).astype(F32)

    grad_rows = out_cotangent.reshape(count, width)
    grad_down = jnp.einsum("rf,rd->fd", hidden_low, grad_rows, preferred_element_type=F32)
    sum_down = reduced(grad_down)
    grad_hidden = jnp.einsum("rd,fd->rf", grad_rows, full_down, preferred_element_type=F32)
    (grad_gate_up,) = pull_swiglu(grad_hidden)
    grad_gate_up_low = grad_gate_up.astype(LOW)
    grad_ffn_in = jnp.einsum(
        "rd,rf->df", normed_ffn_low, grad_gate_up_low, preferred_element_type=F32
    )
    sum_ffn_in = reduced(grad_ffn_in)
    grad_normed_ffn = jnp.einsum(
        "rf,df->rd", grad_gate_up_low, full_ffn_in, preferred_element_type=F32
    )
    grad_middle_norm, grad_ffn_gain = pull_ffn_norm(grad_normed_ffn)
    grad_middle = grad_rows.astype(F32) + grad_middle_norm
    grad_branch = grad_middle.astype(LOW)
    grad_out = jnp.einsum("rv,rd->vd", heads_low, grad_branch, preferred_element_type=F32)
    sum_out = reduced(grad_out)
    grad_heads = jnp.einsum("rd,vd->rv", grad_branch, full_out, preferred_element_type=F32)
    grad_mixed, grad_gate_low, grad_head_gain, grad_state_in = heads_backward(
        local_part, carried, state_in, gate_out, full_head_gain,
        grad_heads.reshape(batch, length, VD),
    )
    grad_gate_low = grad_gate_low.reshape(count, VD)
    grad_gate = jnp.einsum("rd,rc->dc", normed_low, grad_gate_low, preferred_element_type=F32)
    sum_gate = reduced(grad_gate)

    grad_state_out = jnp.zeros(grad_state_in.shape, LOW)
    for step in range(steps):
        entering = grad_state_in
        if step > 0:
            entering = grad_state_in + jnp.einsum(
                "hsji,hsjv->hsiv", through, grad_state_out, preferred_element_type=F32
            )
        grad_state_out = passed_along(entering.astype(LOW), "seq", -1)

    grad_pre, grad_rim, grad_tail, grad_conv, grad_cols = mixer_backward(
        pre_conv, rim, full_conv, cols, rows, t, uw, state_in, grad_mixed, grad_state_out
    )
    grad_rim = passed_along(grad_rim[:, RIM - margin :, :].astype(LOW), "seq", -1).astype(F32)
    grad_tail = (grad_tail[:, RIM - margin :, :] + grad_rim).astype(LOW)
    grad_pre_low = lax.dynamic_update_slice(grad_pre, grad_tail, (0, length - margin, 0))
    grad_pre_low = grad_pre_low.reshape(count, C3)
    grad_qkv = jnp.einsum("rd,rc->dc", normed_low, grad_pre_low, preferred_element_type=F32)
    sum_qkv = reduced(grad_qkv)

    grad_log_decay = jnp.transpose(grad_cols[:, :, 0, :], (1, 2, 0))
    grad_decay_b = jnp.transpose(grad_cols[:, :, 1, :], (1, 2, 0))
    grad_decay_a = grad_log_decay * (-rate) * jax.nn.sigmoid(shifted_decay)
    grad_decay_bias = jnp.sum(grad_decay_a, axis=(0, 1))
    grad_decay_log = jnp.sum(grad_log_decay * log_decay, axis=(0, 1))
    grad_decay_low = jnp.concatenate([grad_decay_a, grad_decay_b], axis=-1).astype(LOW)
    grad_decay_low = grad_decay_low.reshape(count, 2 * H)
    grad_decay = jnp.einsum("rd,rc->dc", normed_low, grad_decay_low, preferred_element_type=F32)
    grad_normed = jnp.einsum("rc,dc->rd", grad_pre_low, full_qkv, preferred_element_type=F32)
    grad_normed = grad_normed + jnp.einsum(
        "rc,dc->rd", grad_gate_low, full_gate, preferred_element_type=F32
    )
    grad_normed = grad_normed + jnp.einsum(
        "rc,dc->rd", grad_decay_low, full_decay, preferred_element_type=F32
    )
    grad_rows_norm, grad_mixer_gain = pull_mixer_norm(grad_normed)
    input_grad = (grad_middle + grad_rows_norm).astype(LOW).reshape(batch, length, width)

    little = (
        grad_mixer_gain,
        grad_ffn_gain,
        jnp.sum(grad_head_gain, axis=(0, 1)),
        grad_conv.reshape(-1),
        grad_decay.reshape(-1),
        grad_decay_log,
        grad_decay_bias,
    )
    flat = lax.psum(jnp.concatenate(little), ("dp", "fsdp", "seq"))
    parts, first = [], 0
    for item in little:
        parts.append(flat[first : first + item.size])
        first += item.size
    place = lax.axis_index("fsdp")

    def own(values, axis=0):
        size = values.shape[axis] // group
        return lax.dynamic_slice_in_dim(values, place * size, size, axis)

    return (
        output,
        input_grad,
        own(parts[0]),
        sum_qkv,
        sum_gate,
        own(parts[4].reshape(width, 2 * H)),
        own(parts[3].reshape(CONV, C3), 1),
        parts[5],
        parts[6],
        own(parts[2]),
        sum_out,
        own(parts[1]),
        sum_ffn_in,
        sum_down,
    )


def solution(mesh):
    rows = P(("dp", "fsdp"), "seq", None)
    split = P("fsdp", None)
    placed = (
        rows,
        P(("dp", "fsdp"), "seq"),
        rows,
        P("fsdp"),
        split,
        split,
        split,
        P(None, "fsdp"),
        P(),
        P(),
        P("fsdp"),
        split,
        P("fsdp"),
        split,
        split,
    )
    return jax.shard_map(
        local,
        mesh=mesh,
        in_specs=placed,
        out_specs=(
            rows,
            rows,
            P("fsdp"),
            split,
            split,
            split,
            P(None, "fsdp"),
            P(),
            P(),
            P("fsdp"),
            split,
            P("fsdp"),
            split,
            split,
        ),
        check_vma=False,
    )
```

time: 2920 us -> 1050 us (0.36)
  other arithmetic: 949 us -> 26.1 us
  blocking collectives: 657 us -> 12.8 us
  matrix products: 573 us -> 166 us
  waiting for transfers between devices: 359 us -> 648 us
  local copies, waits for them, and re-layouts: 317 us -> 29 us
  Pallas kernels: 0 us -> 119 us
    another operation x34 -> x1, other arithmetic: 748 us -> 0.08 us  [token_columns(): rows = jnp.stack([running, ids] + [blank] * 6, axis=2)]
    psum x2 -> x0, blocking collectives: 621 us -> none  [the longest x1 580 us: local(): lax.psum((shard_mixer, shard_qkv, shard_gate, shard_decay, shard_conv, sh...]
    psum x0 -> x2, waiting for transfers between devices: none -> 360 us  [the longest x1 246 us: reduced(): return lax.psum(shard, ('dp', 'seq')).astype(F32)]
    dot_general x116 -> x19, matrix products: 483 us -> 130 us  [the longest x1 18.1 us: local(): jnp.einsum('rd,fd->rf', grad_rows, full_down, preferred_element_type=F32)]
    pallas_call x0 -> x4, Pallas kernels: none -> 119 us  [the longest x1 59.1 us: mixer_backward(): pl.pallas_call(backward_kernel, grid=(H,), in_specs=head_specs(seqs, coun...]
    ppermute x9, waiting for transfers between devices: 228 us -> 154 us  [passed_along(): lax.ppermute(value, axis, [(source, source + steps) for source in range(l...]
    reduce_sum x19 -> x2, other arithmetic: 60.3 us -> 0.27 us  [the longest x1 0.24 us: local(): grad_decay_bias = jnp.sum(grad_decay_a, axis=(0, 1))]
    squeeze x32 -> x0, local copies, waits for them, and re-layouts: 58.2 us -> none  [one_sequence(): lax.scan(jax.checkpoint(block_step), (start, prev_id), (blocks_of(query),...]
  transfers between devices with their start and end apart: 21 -> 21, of which waited for: 10 -> 13; matrix products, arithmetic and copies ran while one was open for 31% -> 15% of each run, Pallas kernels for 0% -> 11%
where the time goes in v1:
time: 1050 us
  waiting for transfers between devices  648 us (62%)
  matrix products  166 us (16%)
  Pallas kernels  119 us (11%)
  local copies, waits for them, and re-layouts  29 us (3%)
  starting transfers between devices  28.6 us (3%)
  other arithmetic  26.1 us (2%)
  between operations  16.1 us (2%)
  blocking collectives  12.8 us (1%)
    psum x1, waiting for transfers between devices, reduced(): return lax.psum(shard, ('dp', 'seq')).astype(F32)  246 us
    ppermute x9, waiting for transfers between devices, passed_along(): lax.ppermute(value, axis, [(source, source + steps) for source in range(l...  154 us
    psum x1, waiting for transfers between devices, local(): flat = lax.psum(jnp.concatenate(little), ('dp', 'fsdp', 'seq'))  114 us
    reduce_scatter x5, waiting for transfers between devices, reduced(): lax.psum_scatter(grad.astype(LOW), 'fsdp', scatter_dimension=0, tiled=True)  110 us
    pallas_call x1, Pallas kernels, mixer_backward(): pl.pallas_call(backward_kernel, grid=(H,), in_specs=head_specs(seqs, coun...  59.1 us
    pallas_call x1, Pallas kernels, mixer_forward(): pl.pallas_call(forward_kernel, grid=(H,), in_specs=head_specs(seqs, count...  39.9 us
    ppermute x9, starting transfers between devices, passed_along(): lax.ppermute(value, axis, [(source, source + steps) for source in range(l...  27.9 us
  transfers between devices with their start and end apart: 21, of which 13 were waited for; matrix products, arithmetic and copies ran while one was open for 15% of the time, Pallas kernels for 11%

profile of v1, /device:TPU:0, one launch (start us, length us, event | category | flops | bytes accessed | tf_op | source)
XLA Modules:
  0.0 1045.2 jit_solution(12628156729254486296)
XLA Ops:
  10.8 5.5 collective-permute-start.1
  18.5 12.8 %all-reduce.3 = bf16[26880]{0:T(1024)(128)(2,1)S(1)} all-reduce(bf16[26880]{0:T(1024)(128)(2,1)S(1)} %dynamic-update-slice), channel_id=2, replica_groups=mesh['dp'=2,'fsdp'=4,'seq'=4] {'fsdp'}, use_global_device_ids=true, to_apply=%add.3 | all-reduce | flops 26880 | bytes 107520
  41.1 18.3 %all-gather.7.cloned.1.call-done = bf16[1024,3072]{1,0:T(8,128)(2,1)} async-done(((bf16[256,3072]{1,0:T(8,128)(2,1)}), bf16[1024,3072]{1,0:T(8,128)(2,1)}) %all-gather.7.cloned.1.call-update) | async-done | bytes 6291472 | tf_op jit(solution)/shard_map/all_gather | solution.py:490
  59.4 8.0 convolution_convert_fusion.2
  67.5 2.3 copy-done.7
  69.8 3.9 collective-permute-start
  73.7 2.1 copy.50.cols_ref
  75.8 39.9 %mixer_forward.1 = (bf16[6,3,256,256]{3,2,1,0:T(8,128)(2,1)S(1)}, bf16[6,3,256,384]{3,2,1,0:T(8,128)(2,1)}, f32[3,256,1536]{2,1,0:T(8,128)}, bf16[3,256,768]{2,1...) custom-call(bf16[3,256,3072]{2,1,0:T(8,128)(2,1)} %bitcast.133, ...), custom_call_target="tpu_custom_call" | custom-call | tf_op jit(solution)/shard_map/mixer_forward/pallas_call | solution.py:309
  115.7 2.7 convert_element_type.165
  118.4 3.8 collective-permute-start.2
  122.2 25.0 %collective-permute-done.2 = bf16[6,3,128,256]{3,2,1,0:T(8,128)(2,1)S(1)} collective-permute-done((bf16[6,3,128,256]{3,2,1,0:T(8,128)(2,1)S(1)}, bf16[6,3,128,256]{3,2,1,0:T(8,128)(2,1)S(1)}, u32[]{:S(2)}, u32[]{:S(2)}) %collective-permute-start.2) | collective-permute-done | bytes 1179680 | tf_op jit(solution)/shard_map/ppermute | solution.py:39
  147.7 4.5 collective-permute-start.3
  152.2 24.2 %collective-permute-done.3 = bf16[6,3,128,256]{3,2,1,0:T(8,128)(2,1)S(1)} collective-permute-done((bf16[6,3,128,256]{3,2,1,0:T(8,128)(2,1)S(1)}, bf16[6,3,128,256]{3,2,1,0:T(8,128)(2,1)S(1)}, u32[]{:S(2)}, u32[]{:S(2)}) %collective-permute-start.3) | collective-permute-done | bytes 1179680 | tf_op jit(solution)/shard_map/ppermute | solution.py:39
  177.9 4.4 collective-permute-start.4
  182.5 7.2 fusion.6.gate_ref
  189.7 16.4 %collective-permute-done.4.state_ref = bf16[6,3,128,256]{3,2,1,0:T(8,128)(2,1)S(1)} collective-permute-done((bf16[6,3,128,256]{3,2,1,0:T(8,128)(2,1)}, bf16[6,3,128,256]{3,2,1,0:T(8,128)(2,1)S(1)}, u32[]{:S(2)}, u32[]{:S(2)}) %collective-permute-start.4) | collective-permute-done | bytes 1179680 | tf_op jit(solution)/shard_map/ppermute | solution.py:39
  206.0 6.9 heads_forward.1
  214.3 7.3 multiply_reduce_fusion.2
  221.7 16.4 %fusion.48 = f32[768,5632]{1,0:T(8,128)} fusion(bf16[1024,5632]{1,0:T(8,128)(2,1)} %all-gather.13.cloned.1.call-done, f32[768,1024]{1,0:T(8,128)} %get-tuple-element.95, f32[1024]{0:T(1024)S(1)} %bitcast.159, f32[768]{0:T(1024)S(1)} %fusion.42), kind=kOutput, calls=%fused_computation.113 | convolution fusion | flops 8860729344 | bytes 31988736 | tf_op jit(solution)/shard_map/dot_general | solution.py:536
  238.1 3.9 all-gather.15.cloned.1.call-done
  242.0 18.1 %fusion.17 = (f32[768,2816]{1,0:T(8,128)}, f32[768,2816]{1,0:T(8,128)}, bf16[768,2816]{1,0:T(8,128)(2,1)}) fusion(f32[768,5632]{1,0:T(8,128)} %fusion.48, bf16[768,1024]{1,0:T(8,128)(2,1)} %bitcast.141, bf16[2816,1024]{1,0:T(8,128)(2,1)} %all-gather.15.cloned.1.call-done), kind=kOutput, calls=%fused_computation.45 | convolution fusion | flops 4459462656 | bytes 46268416 | tf_op jit(solution)/shard_map/rd,fd->rf/dot_general | solution.py:549
  260.1 17.3 %multiply_reduce_fusion = (f32[1024]{0:T(1024)S(1)}, f32[768]{0:T(1024)S(1)}, f32[768,1024]{1,0:T(8,128)}) fusion(f32[768,1024]{1,0:T(8,128)} %get-tuple-element.95, f32[768]{0:T(1024)S(1)} %fusion.42, f32[1024]{0:T(1024)S(1)} %bitcast.160, bf16[1024,5632]{1,0:T(8,128)(2,1)} %all-gather.13.cloned.1.call-done, f32[768,2816]{1,0:T(8,128)} %get-tuple-element.70, ...), kind=kOutput, calls=%fused_computation.34 | convolution fusion | flops 8871737344 | bytes 35141632 | tf_op jit(solution)/shard_map/rf,df->rd/dot_general | solution.py:556
  277.4 4.2 fusion.3
  283.4 4.0 convolution_convert_fusion.3
  287.5 7.7 fusion.19
  295.2 12.9 %heads_backward.1 = (bf16[3,256,1536]{2,1,0:T(8,128)(2,1)S(1)}, bf16[3,256,1536]{2,1,0:T(8,128)(2,1)}, f32[6,1,256]{2,1,0:T(1,128)S(1)}, f32[6,3,128,256]{3,2,1,0:T(8,128)}) custom-call(f32[3,256,1536]{2,1,0:T(8,128)} %get-tuple-element.29.local_ref, bf16[3,256,768]{2,1,0:T(8,128)(2,1)S(1)} %get-tuple-element.30.carried_ref, ...), custom_call_target="tpu_custom_call" | custom-call | tf_op jit(solution)/shard_map/heads_backward/pallas_call | solution.py:356
  309.5 5.9 bitcast_convert_fusion.1
  315.5 10.0 convolution_convert_fusion.1
  325.6 2.0 convert_element_type.178
  328.9 28.7 %collective-permute-done.5 = bf16[6,3,128,256]{3,2,1,0:T(8,128)(2,1)S(1)} collective-permute-done((bf16[6,3,128,256]{3,2,1,0:T(8,128)(2,1)S(1)}, bf16[6,3,128,256]{3,2,1,0:T(8,128)(2,1)S(1)}, u32[]{:S(2)}, u32[]{:S(2)}) %collective-permute-start.5) | collective-permute-done | bytes 1179680 | tf_op jit(solution)/shard_map/ppermute | solution.py:39
  358.1 1.8 collective-permute-start.6
  359.9 27.6 %collective-permute-done.6 = bf16[6,3,128,256]{3,2,1,0:T(8,128)(2,1)S(1)} collective-permute-done((bf16[6,3,128,256]{3,2,1,0:T(8,128)(2,1)S(1)}, bf16[6,3,128,256]{3,2,1,0:T(8,128)(2,1)S(1)}, u32[]{:S(2)}, u32[]{:S(2)}) %collective-permute-start.6) | collective-permute-done | bytes 1179680 | tf_op jit(solution)/shard_map/ppermute | solution.py:39
  389.3 27.1 %collective-permute-done.7.gend_ref = bf16[6,3,128,256]{3,2,1,0:T(8,128)(2,1)S(1)} collective-permute-done((bf16[6,3,128,256]{3,2,1,0:T(8,128)(2,1)S(1)}, bf16[6,3,128,256]{3,2,1,0:T(8,128)(2,1)S(1)}, u32[]{:S(2)}, u32[]{:S(2)}) %collective-permute-start.7) | collective-permute-done | bytes 1179680 | tf_op jit(solution)/shard_map/ppermute | solution.py:39
  416.4 59.1 %mixer_backward.1 = (bf16[3,256,3072]{2,1,0:T(8,128)(2,1)}, f32[3,8,3072]{2,1,0:T(8,128)S(1)}, f32[3,8,3072]{2,1,0:T(8,128)S(1)}, f32[4,3072]{1,0:T(4,128)S(1)}, f32[6,3,8,256]{3,2,1,0:T(8,128)S(1)}) custom-call(bf16[3,256,3072]{2,1,0:T(8,128)(2,1)} %bitcast.136, bf16[3,256,3072]{2,1,0:T(8,128)(2,1)} %bitcast.137, bf16[3,256,3072]{2,1,0:T(8,128)(2,1)} %bitcast.138, ...), custom_call_target="tpu_custom_call" | custom-call | tf_op jit(solution)/shard_map/mixer_backward/pallas_call | solution.py:386
  477.6 4.8 collective-permute-done.8
  484.2 9.9 bitcast_convert_fusion
  494.1 19.7 %convolution_convert_fusion = bf16[1024,5632]{1,0:T(8,128)(2,1)} fusion(f32[768,2816]{1,0:T(8,128)} %get-tuple-element.70, f32[768,2816]{1,0:T(8,128)} %get-tuple-element.69, f32[768,1024]{1,0:T(8,128)} %get-tuple-element.95, f32[1024]{0:T(1024)S(1)} %bitcast.162, f32[768]{0:T(1024)S(1)} %fusion.42), kind=kOutput, calls=%fused_computation.3 | convolution fusion | flops 8875147264 | bytes 31988736 | tf_op jit(solution)/shard_map/rd,rf->df/dot_general | solution.py:552
  514.2 7.6 fusion.55
  525.2 10.7 %fusion.11 = (f32[1024]{0:T(1024)S(1)}, f32[768]{0:T(1024)S(1)}, f32[768,1024]{1,0:T(8,128)}) fusion(bf16[3,256,1024]{2,1,0:T(8,128)(2,1)S(1)} %copy-done.12, f32[768]{0:T(1024)S(1)} %copy-done.27, f32[1024]{0:T(1024)S(1)} %bitcast.157, f32[768,1024]{1,0:T(8,128)S(1)} %fusion.33, f32[768,1024]{1,0:T(8,128)S(1)} %copy-done.49, ...), kind=kOutput, calls=%fused_computation.29 | convolution fusion | flops 4838914048 | bytes 22034432 | tf_op jit(solution)/shard_map/rc,dc->rd/dot_general | solution.py:600
  536.7 15.0 %reduce-scatter.6.cloned.1.call-done = bf16[256,3072]{1,0:T(8,128)(2,1)} async-done(((bf16[1024,3072]{1,0:T(8,128)(2,1)}), bf16[256,3072]{1,0:T(8,128)(2,1)}) %reduce-scatter.6.cloned.1.call-update) | async-done | bytes 1572880 | tf_op jit(solution)/shard_map/reduce_scatter | solution.py:543
  551.8 94.7 %reduce-scatter.12.cloned.1.call-done = bf16[256,5632]{1,0:T(8,128)(2,1)} async-done(((bf16[1024,5632]{1,0:T(8,128)(2,1)}), bf16[256,5632]{1,0:T(8,128)(2,1)}) %reduce-scatter.12.cloned.1.call-update) | async-done | bytes 2883600 | tf_op jit(solution)/shard_map/reduce_scatter | solution.py:543
  646.5 10.7 %add_convert_fusion.1 = bf16[768,1024]{1,0:T(8,128)(2,1)} fusion(f32[768,1024]{1,0:T(8,128)} %get-tuple-element.95, bf16[768,2816]{1,0:T(8,128)(2,1)} %get-tuple-element.71, bf16[2816,1024]{1,0:T(8,128)(2,1)} %all-gather.15.cloned.1.call-done), kind=kOutput, calls=%fused_computation.37 | convolution fusion | flops 4430757888 | bytes 14811136 | tf_op jit(solution)/shard_map/dot_general | solution.py:539
  657.2 2.0 fusion.5
  659.3 114.0 %all-reduce.8.cloned.1.call-done = f32[26892]{0:T(1024)} async-done(((f32[26892]{0:T(1024)}), f32[26892]{0:T(1024)}) %all-reduce.8.cloned.1.call-update) | async-done | bytes 107584 | tf_op jit(solution)/shard_map/psum | solution.py:619
  780.6 245.7 %all-reduce.10.cloned.1.call-done = (bf16[256,3072]{1,0:T(8,128)(2,1)}, bf16[256,1536]{1,0:T(8,128)(2,1)}, bf16[384,1024]{1,0:T(8,128)(2,1)}, bf16[256,5632]{1,0:T(8,128)(2,1)}, bf16[704,1024]{1,0:T(8,128)(2,1)}) async-done(((bf16[256,3072]{1,0:T(8,128)(2,1)}, bf16[256,1536]{1,0:T(8,128)(2,1)}, bf16[384,1024]{1,0:T(8,128)(2,1)}, bf16[256,5632]{1,0:T(8,128)(2,1)}, bf16[704,1024]{1,0:T(8,128)(2,1)}), ...) | async-done | bytes 7471120 | tf_op jit(solution)/shard_map/psum | solution.py:544
  1026.3 5.1 convert_element_type.191
  1031.5 2.0 convert_element_type.185
  1033.5 1.9 convert_element_type.193
  (219 shorter events, 43.5 us)
Async XLA Ops:
  7.2 52.2 %all-gather.7.cloned.1.call-start = ((), (), s32[]{:S(2)}) async-start(), calls=%async_computation.5 | async-start | bytes 7864320 | tf_op jit(solution)/shard_map/all_gather | solution.py:490
  7.9 8.4 copy-start.34
  7.9 8.7 copy-start.35
  7.9 8.7 copy-start.48
  8.0 10.0 copy-start.38
  8.0 10.0 copy-start.39
  8.0 10.0 copy-start.40
  8.0 174.5 %all-gather.9.cloned.1.call-start = ((), (), s32[]{:S(2)}) async-start(), calls=%async_computation.6 | async-start | bytes 3932160 | tf_op jit(solution)/shard_map/all_gather | solution.py:491
  8.7 25.3 %copy-start.10 = (bf16[3,256,1024]{2,1,0:T(8,128)(2,1)S(1)}, bf16[3,256,1024]{2,1,0:T(8,128)(2,1)}, u32[]{:S(2)}) copy-start(bf16[3,256,1024]{2,1,0:T(8,128)(2,1)} %param.15) | copy-start | bytes 4718596
  8.8 205.6 %all-gather.11.cloned.1.call-start = ((), (), s32[]{:S(2)}) async-start(), calls=%async_computation.7 | async-start | bytes 3932160 | tf_op jit(solution)/shard_map/all_gather | solution.py:492
  9.5 212.2 %all-gather.13.cloned.1.call-start = ((), (), s32[]{:S(2)}) async-start(), calls=%async_computation.8 | async-start | bytes 14417920 | tf_op jit(solution)/shard_map/all_gather | solution.py:493
  10.1 232.0 %all-gather.15.cloned.1.call-start = ((), (), s32[]{:S(2)}) async-start(), calls=%async_computation.9 | async-start | bytes 7208960 | tf_op jit(solution)/shard_map/all_gather | solution.py:494
  10.8 28.4 %collective-permute-start.1 = (s32[3,3]{1,0:T(4,128)}, s32[3,3]{1,0:T(4,128)}, u32[]{:S(2)}, u32[]{:S(2)}) collective-permute-start(s32[3,3]{1,0:T(4,128)} %slice.100), channel_id=1, source_target_pairs={{0,1},{1,2},{2,3},{4,5},{5,6},{6,7},{8,9},{9,10},{10,11},{12,13},{... | collective-permute-start | bytes 116 | tf_op jit(solution)/shard_map/ppermute | solution.py:39
  16.3 18.8 %copy-start.47 = (f32[6]{0:T(128)S(1)}, f32[6]{0:T(128)}, u32[]{:S(2)}) copy-start(f32[6]{0:T(128)} %param.23) | copy-start | bytes 76
  16.3 18.9 %copy-start.41 = (f32[6]{0:T(128)S(1)}, f32[6]{0:T(128)}, u32[]{:S(2)}) copy-start(f32[6]{0:T(128)} %param.24) | copy-start | bytes 76
  16.3 520.4 %reduce-scatter.10.cloned.1.call-start = ((), (), s32[]{:S(2)}) async-start(), calls=%async_computation.13 | async-start | bytes 3932160 | tf_op jit(solution)/shard_map/reduce_scatter | solution.py:543
  37.8 29.7 %copy-start.26 = (f32[768]{0:T(1024)}, f32[768]{0:T(1024)S(1)}, u32[]{:S(2)}) copy-start(f32[768]{0:T(1024)S(1)} %rsqrt.23) | copy-start | bytes 9220
  38.2 29.2 %copy-start.15 = (bf16[768,1024]{1,0:T(8,128)(2,1)}, bf16[768,1024]{1,0:T(8,128)(2,1)S(1)}, u32[]{:S(2)}) copy-start(bf16[768,1024]{1,0:T(8,128)(2,1)S(1)} %fusion.10) | copy-start | bytes 4718596
  41.1 32.5 %copy-start.31 = (f32[3,256]{1,0:T(4,128)S(1)}, f32[3,256]{1,0:T(4,128)}, u32[]{:S(2)}) copy-start(f32[3,256]{1,0:T(4,128)} %convert_element_type.164) | copy-start | bytes 9220
  69.8 6.0 collective-permute-start
  115.7 32.0 %copy-start.1 = (bf16[6,3,256,256]{3,2,1,0:T(8,128)(2,1)}, bf16[6,3,256,256]{3,2,1,0:T(8,128)(2,1)S(1)}, u32[]{:S(2)}) copy-start(bf16[6,3,256,256]{3,2,1,0:T(8,128)(2,1)S(1)} %get-tuple-element.33.t_ref) | copy-start | bytes 7077892
  115.7 31.5 %copy-start.9 = (f32[6,3,128,256]{3,2,1,0:T(8,128)S(1)}, f32[6,3,128,256]{3,2,1,0:T(8,128)}, u32[]{:S(2)}) copy-start(f32[6,3,128,256]{3,2,1,0:T(8,128)} %get-tuple-element.31) | copy-start | bytes 7077892
  118.4 28.8 %collective-permute-start.2 = (bf16[6,3,128,256]{3,2,1,0:T(8,128)(2,1)S(1)}, bf16[6,3,128,256]{3,2,1,0:T(8,128)(2,1)S(1)}, u32[]{:S(2)}, u32[]{:S(2)}) collective-permute-start(bf16[6,3,128,256]{3,2,1,0:T(8,128)(2,1)S(1)} %convert_element_type.165), channel_id=1, source_target_pairs={{0,1},{1,2},{2,3},{4,5},{5,6},{6,7},{8,9},{9,10},{10,11},{12,13},{... | collective-permute-start | bytes 3538952 | tf_op jit(solution)/shard_map/ppermute | solution.py:39
  147.7 34.7 %copy-start.33 = (f32[1,2,4,128]{3,2,1,0:T(4,128)S(1)}, f32[1,2,4,128]{3,2,1,0:T(4,128)}, u32[]{:S(2)}) copy-start(f32[1,2,4,128]{3,2,1,0:T(4,128)} %get-tuple-element.79) | copy-start | bytes 12292
  147.7 34.7 %copy-start.37 = (f32[3,256]{1,0:T(4,128)S(1)}, f32[3,256]{1,0:T(4,128)}, u32[]{:S(2)}) copy-start(f32[3,256]{1,0:T(4,128)} %copy-done.36) | copy-start | bytes 9220
  147.7 28.7 %collective-permute-start.3 = (bf16[6,3,128,256]{3,2,1,0:T(8,128)(2,1)S(1)}, bf16[6,3,128,256]{3,2,1,0:T(8,128)(2,1)S(1)}, u32[]{:S(2)}, u32[]{:S(2)}) collective-permute-start(bf16[6,3,128,256]{3,2,1,0:T(8,128)(2,1)S(1)} %add_convert_fusion.5), channel_id=1, source_target_pairs={{0,1},{1,2},{2,3},{4,5},{5,6},{6,7},{8,9},{9,10},{10,11},{12,13},{... | collective-permute-start | bytes 3538952 | tf_op jit(solution)/shard_map/ppermute | solution.py:39
  177.9 28.2 %collective-permute-start.4 = (bf16[6,3,128,256]{3,2,1,0:T(8,128)(2,1)}, bf16[6,3,128,256]{3,2,1,0:T(8,128)(2,1)S(1)}, u32[]{:S(2)}, u32[]{:S(2)}) collective-permute-start(bf16[6,3,128,256]{3,2,1,0:T(8,128)(2,1)} %add_convert_fusion.4), channel_id=1, source_target_pairs={{0,1},{1,2},{2,3},{4,5},{5,6},{6,7},{8,9},{9,10},{10,11},{12,13},{... | collective-permute-start | bytes 3538952 | tf_op jit(solution)/shard_map/ppermute | solution.py:39
  287.4 249.3 %reduce-scatter.8.cloned.1.call-start = ((), (), s32[]{:S(2)}) async-start(), calls=%async_computation.12 | async-start | bytes 3932160 | tf_op jit(solution)/shard_map/reduce_scatter | solution.py:543
  295.2 14.3 %copy-start.11 = (bf16[3,256,1024]{2,1,0:T(8,128)(2,1)S(1)}, bf16[3,256,1024]{2,1,0:T(8,128)(2,1)}, u32[]{:S(2)}) copy-start(bf16[3,256,1024]{2,1,0:T(8,128)(2,1)} %param.15) | copy-start | bytes 4718596
  315.4 221.3 %reduce-scatter.14.cloned.1.call-start = ((), (), s32[]{:S(2)}) async-start(), calls=%async_computation.15 | async-start | bytes 7208960 | tf_op jit(solution)/shard_map/reduce_scatter | solution.py:543
  325.5 226.3 %reduce-scatter.6.cloned.1.call-start = ((), (), s32[]{:S(2)}) async-start(), calls=%async_computation.11 | async-start | bytes 7864320 | tf_op jit(solution)/shard_map/reduce_scatter | solution.py:543
  325.6 32.0 %copy-start.8 = (f32[6,3,128,256]{3,2,1,0:T(8,128)S(1)}, f32[6,3,128,256]{3,2,1,0:T(8,128)}, u32[]{:S(2)}) copy-start(f32[6,3,128,256]{3,2,1,0:T(8,128)} %get-tuple-element.36) | copy-start | bytes 7077892
  327.6 30.0 %collective-permute-start.5 = (bf16[6,3,128,256]{3,2,1,0:T(8,128)(2,1)S(1)}, bf16[6,3,128,256]{3,2,1,0:T(8,128)(2,1)S(1)}, u32[]{:S(2)}, u32[]{:S(2)}) collective-permute-start(bf16[6,3,128,256]{3,2,1,0:T(8,128)(2,1)S(1)} %convert_element_type.178), channel_id=1, source_target_pairs={{1,0},{2,1},{3,2},{5,4},{6,5},{7,6},{9,8},{10,9},{11,10},{13,12},{... | collective-permute-start | bytes 3538952 | tf_op jit(solution)/shard_map/ppermute | solution.py:39
  358.1 58.3 %copy-start = (f32[6,3,256,8]{3,2,1,0:T(8,128)S(1)}, f32[6,3,256,8]{3,2,1,0:T(8,128)}, u32[]{:S(2)}) copy-start(f32[6,3,256,8]{3,2,1,0:T(8,128)} %copy.50.cols_ref) | copy-start | bytes 442372
  358.1 29.4 %collective-permute-start.6 = (bf16[6,3,128,256]{3,2,1,0:T(8,128)(2,1)S(1)}, bf16[6,3,128,256]{3,2,1,0:T(8,128)(2,1)S(1)}, u32[]{:S(2)}, u32[]{:S(2)}) collective-permute-start(bf16[6,3,128,256]{3,2,1,0:T(8,128)(2,1)S(1)} %add_convert_fusion.3), channel_id=1, source_target_pairs={{1,0},{2,1},{3,2},{5,4},{6,5},{7,6},{9,8},{10,9},{11,10},{13,12},{... | collective-permute-start | bytes 3538952 | tf_op jit(solution)/shard_map/ppermute | solution.py:39
  388.0 28.4 %collective-permute-start.7 = (bf16[6,3,128,256]{3,2,1,0:T(8,128)(2,1)S(1)}, bf16[6,3,128,256]{3,2,1,0:T(8,128)(2,1)S(1)}, u32[]{:S(2)}, u32[]{:S(2)}) collective-permute-start(bf16[6,3,128,256]{3,2,1,0:T(8,128)(2,1)S(1)} %add_convert_fusion.2), channel_id=1, source_target_pairs={{1,0},{2,1},{3,2},{5,4},{6,5},{7,6},{9,8},{10,9},{11,10},{13,12},{... | collective-permute-start | bytes 3538952 | tf_op jit(solution)/shard_map/ppermute | solution.py:39
  476.2 6.2 collective-permute-start.8
  494.1 152.4 %reduce-scatter.12.cloned.1.call-start = ((), (), s32[]{:S(2)}) async-start(), calls=%async_computation.14 | async-start | bytes 14417920 | tf_op jit(solution)/shard_map/reduce_scatter | solution.py:543
  513.8 259.4 %all-reduce.8.cloned.1.call-start = ((), (), s32[]{:S(2)}) async-start(), calls=%async_computation.10 | async-start | bytes 221184 | tf_op jit(solution)/shard_map/psum | solution.py:619
  514.1 7.7 copy-start.6
  514.1 7.8 copy-start.25
  514.2 7.8 copy-start.42
  514.2 7.8 copy-start.44
  514.2 8.0 copy-start.16
  536.6 489.7 %all-reduce.10.cloned.1.call-start = ((), (), s32[]{:S(2)}) async-start(), calls=%async_computation.16 | async-start | bytes 14942208 | tf_op jit(solution)/shard_map/psum | solution.py:544
  646.5 10.8 %copy-start.30 = (f32[768]{0:T(1024)S(1)}, f32[768]{0:T(1024)}, u32[]{:S(2)}) copy-start(f32[768]{0:T(1024)} %copy-done.29) | copy-start | bytes 9220
  646.5 10.8 %copy-start.14 = (f32[768,1024]{1,0:T(8,128)S(1)}, f32[768,1024]{1,0:T(8,128)}, u32[]{:S(2)}) copy-start(f32[768,1024]{1,0:T(8,128)} %copy-done.13) | copy-start | bytes 9437188
  646.5 10.8 %copy-start.17 = (f32[768,1024]{1,0:T(8,128)S(1)}, f32[768,1024]{1,0:T(8,128)}, u32[]{:S(2)}) copy-start(f32[768,1024]{1,0:T(8,128)} %get-tuple-element.97) | copy-start | bytes 9437188
  (23 other events, 50.4 us)
Sparse Core Ops, SparseCore 0:
  9.6 49.7 all-gather.6
  61.0 28.4 all-gather.8
  91.0 28.5 all-gather.10
  121.0 76.1 all-gather.12
  198.6 43.3 all-gather.14
  287.6 38.0 reduce-scatter.9
  328.3 37.9 reduce-scatter.7
  369.4 54.8 reduce-scatter.13
  494.2 57.5 reduce-scatter.5
  554.2 92.1 reduce-scatter.11
  652.6 120.6 all-reduce.7
  778.1 248.2 all-reduce.9

commit v2 on v1

--- a/solution.py
+++ b/solution.py
@@ -15,6 +15,8 @@
 VD = 1536
 C3 = 3072
 RIM = 8
+HEAD = 2 * DK + DV
+GROUPS = 3
 
 EPSILON = 1e-06
 HEAD_EPSILON = 0.001
@@ -54,19 +56,21 @@
 
 
 def conv_head(s, parts, rims, taps, cols, pad_ref):
+    count = pad_ref.shape[1] - RIM
+    margin = CONV - 1
     at = 0
     for part, rim in zip(parts, rims):
         width = part.shape[-1]
-        pad_ref[s, 0:RIM, at : at + width] = rim[s].astype(F32)
-        pad_ref[s, RIM:, at : at + width] = part[s].astype(F32)
+        pad_ref[s, RIM:, at : at + width] = part[s * count : (s + 1) * count, :].astype(F32)
+        edge = rim[...].astype(F32)[margin * s : margin * (s + 1), :]
+        pad_ref[s, RIM - margin : RIM, at : at + width] = edge
         at += width
-    count = parts[0].shape[1]
     shifted = []
     total = None
     for tap in range(CONV):
-        first = RIM - (CONV - 1) + tap
+        first = RIM - margin + tap
         values = pad_ref[s, first : first + count, :]
-        if tap < CONV - 1:
+        if tap < margin:
             values = values * cols[:, 4 + tap : 5 + tap]
         shifted.append(values)
         term = values * taps[tap : tap + 1, :]
@@ -88,9 +92,10 @@
 
 def forward_kernel(
     q_ref, k_ref, v_ref, rq_ref, rk_ref, rv_ref, wq_ref, wk_ref, wv_ref, cols_ref, rows_ref,
-    t_ref, uw_ref, local_ref, carried_ref, through_ref, offsets_ref, pad_ref,
+    t_ref, uw_ref, local_ref, carried_ref,
+    through_ref, offsets_ref, pad_ref,
 ):
-    seqs, count = q_ref.shape[0], q_ref.shape[1]
+    seqs, count = cols_ref.shape[1], cols_ref.shape[2]
     order, other = iotas(count)
     taps = jnp.concatenate([wq_ref[...], wk_ref[...], wv_ref[...]], axis=1)
     state = []
@@ -178,18 +183,18 @@
     t_ref, uw_ref, state_ref, gout_ref, gend_ref,
     gpre_ref, grim_ref, gtail_ref, gtaps_ref, gcols_ref, pad_ref, shift_ref,
 ):
-    head = pl.program_id(0)
-    seqs, count = q_ref.shape[0], q_ref.shape[1]
+    seqs, count = cols_ref.shape[1], cols_ref.shape[2]
     order, other = iotas(count)
     taps = jnp.concatenate([wq_ref[...], wk_ref[...], wv_ref[...]], axis=1)
     before = (order < other).astype(LOW)
-    gtaps = [None] * CONV
+    head, heads = pl.program_id(0), pl.num_programs(0)
     at = (
         pl.ds(pl.multiple_of(head * DK, DK), DK),
-        pl.ds(pl.multiple_of(KD + head * DK, DK), DK),
-        pl.ds(pl.multiple_of(2 * KD + head * DV, DV), DV),
-    )
-    spans = ((0, DK), (DK, 2 * DK), (2 * DK, 2 * DK + DV))
+        pl.ds(pl.multiple_of((heads + head) * DK, DK), DK),
+        pl.ds(pl.multiple_of(2 * heads * DK + head * DV, DV), DV),
+    )
+    spans = ((0, DK), (DK, 2 * DK), (2 * DK, HEAD))
+    gtaps = [None] * CONV
     for s in range(seqs):
         cols, rows = cols_ref[0, s], rows_ref[0, s]
         shifted, total, sig, out = conv_head(
@@ -268,30 +273,34 @@
             gpre_ref[s, :, place] = back[RIM:, low:top].astype(LOW)
             grim_ref[s, :, place] = back[:RIM, low:top]
             gtail_ref[s, :, place] = back[count:, low:top]
-    for tap in range(CONV):
-        for place, (low, top) in zip(at, spans):
-            gtaps_ref[tap : tap + 1, place] = gtaps[tap][:, low:top]
-
-
-def head_specs(seqs, count):
-    def cut(rows, width, first):
-        return pl.BlockSpec((seqs, rows, width), lambda h: (0, 0, first + h))
-
-    def taps(width, first):
-        return pl.BlockSpec((CONV, width), lambda h: (0, first + h))
-
-    channel = [cut(count, DK, 0), cut(count, DK, H), cut(count, DV, H)]
-    rim = [cut(RIM, DK, 0), cut(RIM, DK, H), cut(RIM, DV, H)]
-    weight = [taps(DK, 0), taps(DK, H), taps(DV, H)]
-    return channel + rim + weight + [per_head(seqs, count, 8), per_head(seqs, 8, count)]
-
-
-def per_head(seqs, rows, width):
-    return pl.BlockSpec((1, seqs, rows, width), lambda h: (h, 0, 0, 0))
-
-
-def by_column(seqs, count, width):
-    return pl.BlockSpec((seqs, count, width), lambda h: (0, 0, h))
+    gtaps = jnp.concatenate(gtaps, axis=0)
+    for place, (low, top) in zip(at, spans):
+        gtaps_ref[:, place] = gtaps[:, low:top]
+
+
+def per_head(seqs, rows, width, first=0):
+    return pl.BlockSpec((1, seqs, rows, width), lambda h: (first + h, 0, 0, 0))
+
+
+def by_column(seqs, count, width, first=0):
+    return pl.BlockSpec((seqs, count, width), lambda h: (0, 0, first + h))
+
+
+def head_specs(seqs, count, first, heads):
+    def cut(rows, row, width, column):
+        return pl.BlockSpec((rows, width), lambda h: (row, column + h))
+
+    rows, edge = seqs * count, edge_rows(seqs)
+    late = 2 * heads * DK // DV
+    specs = [cut(rows, 0, DK, 0), cut(rows, 0, DK, heads), cut(rows, 0, DV, late)]
+    at = rows // edge
+    specs += [cut(edge, at, DK, 0), cut(edge, at, DK, heads), cut(edge, at, DV, late)]
+    specs += [cut(CONV, 0, DK, 0), cut(CONV, 0, DK, heads), cut(CONV, 0, DV, late)]
+    return specs + [per_head(seqs, count, 8, first), per_head(seqs, 8, count, first)]
+
+
+def edge_rows(seqs):
+    return -(-seqs * (CONV - 1) // 16) * 16
 
 
 def whole(*shape):
@@ -304,12 +313,12 @@
     )
 
 
-def mixer_forward(pre_conv, rim, taps, cols, rows):
-    seqs, count = pre_conv.shape[0], pre_conv.shape[1]
+def mixer_forward(pre_conv, taps, cols, rows, first, heads):
+    seqs, count = cols.shape[1], cols.shape[2]
     return pl.pallas_call(
         forward_kernel,
-        grid=(H,),
-        in_specs=head_specs(seqs, count),
+        grid=(heads,),
+        in_specs=head_specs(seqs, count, first, heads),
         out_specs=[
             per_head(seqs, count, count),
             per_head(seqs, count, DV + DK),
@@ -319,74 +328,101 @@
             per_head(seqs, DK, DV),
         ],
         out_shape=[
-            jax.ShapeDtypeStruct((H, seqs, count, count), LOW),
-            jax.ShapeDtypeStruct((H, seqs, count, DV + DK), LOW),
-            jax.ShapeDtypeStruct((seqs, count, VD), F32),
-            jax.ShapeDtypeStruct((seqs, count, KD), LOW),
-            jax.ShapeDtypeStruct((H, seqs, DK, DK), LOW),
-            jax.ShapeDtypeStruct((H, seqs, DK, DV), F32),
+            jax.ShapeDtypeStruct((heads, seqs, count, count), LOW),
+            jax.ShapeDtypeStruct((heads, seqs, count, DV + DK), LOW),
+            jax.ShapeDtypeStruct((seqs, count, heads * DV), F32),
+            jax.ShapeDtypeStruct((seqs, count, heads * DK), LOW),
+            jax.ShapeDtypeStruct((heads, seqs, DK, DK), LOW),
+            jax.ShapeDtypeStruct((heads, seqs, DK, DV), F32),
         ],
-        scratch_shapes=[pltpu.VMEM((seqs, RIM + count, 2 * DK + DV), F32)],
+        scratch_shapes=[pltpu.VMEM((seqs, RIM + count, HEAD), F32)],
         compiler_params=params(),
         name="mixer_forward",
-    )(pre_conv, pre_conv, pre_conv, rim, rim, rim, taps, taps, taps, cols, rows)
-
-
-def heads_forward(local_part, carried, state, gate, gain):
+    )(*[pre_conv] * 6, *[taps] * 3, cols, rows)
+
+
+def heads_forward(local_part, carried, state, gate, gain, first, kept):
     seqs, count = local_part.shape[0], local_part.shape[1]
+    heads = state.shape[0]
+    operands = [local_part, carried, state, gate, gain]
+    in_specs = [
+        by_column(seqs, count, DV),
+        by_column(seqs, count, DK),
+        per_head(seqs, DK, DV),
+        by_column(seqs, count, DV, first),
+        pl.BlockSpec((1, DV), lambda h: (0, 0)),
+    ]
+    aliases = {}
+    if kept is not None:
+        operands.append(kept)
+        in_specs.append(pl.BlockSpec(memory_space=pl.ANY))
+        aliases = {5: 0}
+
+    def kernel(*refs):
+        heads_kernel(*refs[:5], refs[-1])
+
     return pl.pallas_call(
-        heads_kernel,
-        grid=(H,),
-        in_specs=[
-            by_column(seqs, count, DV),
-            by_column(seqs, count, DK),
-            per_head(seqs, DK, DV),
-            by_column(seqs, count, DV),
-            whole(1, DV),
-        ],
-        out_specs=by_column(seqs, count, DV),
+        kernel,
+        grid=(heads,),
+        in_specs=in_specs,
+        out_specs=by_column(seqs, count, DV, first),
         out_shape=jax.ShapeDtypeStruct((seqs, count, VD), LOW),
+        input_output_aliases=aliases,
         compiler_params=params(),
         name="heads_forward",
-    )(local_part, carried, state, gate, gain)
-
-
-def heads_backward(local_part, carried, state, gate, gain, grad):
+    )(*operands)
+
+
+def heads_backward(local_part, carried, state, gate, gain, grad, first, kept):
     seqs, count = local_part.shape[0], local_part.shape[1]
+    heads = state.shape[0]
+    operands = [local_part, carried, state, gate, gain, grad]
+    in_specs = [
+        by_column(seqs, count, DV),
+        by_column(seqs, count, DK),
+        per_head(seqs, DK, DV),
+        by_column(seqs, count, DV, first),
+        pl.BlockSpec((1, DV), lambda h: (0, 0)),
+        by_column(seqs, count, DV, first),
+    ]
+    aliases = {}
+    if kept is not None:
+        operands.append(kept)
+        in_specs.append(pl.BlockSpec(memory_space=pl.ANY))
+        aliases = {6: 1}
+
+    def kernel(*refs):
+        heads_back_kernel(*refs[:6], *refs[-4:])
+
     return pl.pallas_call(
-        heads_back_kernel,
-        grid=(H,),
-        in_specs=[
-            by_column(seqs, count, DV),
-            by_column(seqs, count, DK),
-            per_head(seqs, DK, DV),
-            by_column(seqs, count, DV),
-            whole(1, DV),
-            by_column(seqs, count, DV),
-        ],
+        kernel,
+        grid=(heads,),
+        in_specs=in_specs,
         out_specs=[
             by_column(seqs, count, DV),
-            by_column(seqs, count, DV),
+            by_column(seqs, count, DV, first),
             pl.BlockSpec((1, 1, DV), lambda h: (h, 0, 0)),
             per_head(seqs, DK, DV),
         ],
         out_shape=[
+            jax.ShapeDtypeStruct((seqs, count, heads * DV), LOW),
             jax.ShapeDtypeStruct((seqs, count, VD), LOW),
-            jax.ShapeDtypeStruct((seqs, count, VD), LOW),
-            jax.ShapeDtypeStruct((H, 1, DV), F32),
-            jax.ShapeDtypeStruct((H, seqs, DK, DV), F32),
+            jax.ShapeDtypeStruct((heads, 1, DV), F32),
+            jax.ShapeDtypeStruct((heads, seqs, DK, DV), F32),
         ],
+        input_output_aliases=aliases,
         compiler_params=params(),
         name="heads_backward",
-    )(local_part, carried, state, gate, gain, grad)
-
-
-def mixer_backward(pre_conv, rim, taps, cols, rows, t, uw, state, gout, gend):
-    seqs, count = pre_conv.shape[0], pre_conv.shape[1]
+    )(*operands)
+
+
+def mixer_backward(pre_conv, taps, cols, rows, t, uw, state, gout, gend, first):
+    seqs, count = cols.shape[1], cols.shape[2]
+    heads = state.shape[0]
     return pl.pallas_call(
         backward_kernel,
-        grid=(H,),
-        in_specs=head_specs(seqs, count)
+        grid=(heads,),
+        in_specs=head_specs(seqs, count, first, heads)
         + [
             per_head(seqs, count, count),
             per_head(seqs, count, DV + DK),
@@ -395,29 +431,274 @@
             per_head(seqs, DK, DV),
         ],
         out_specs=[
-            whole(seqs, count, C3),
-            whole(seqs, RIM, C3),
-            whole(seqs, RIM, C3),
-            whole(CONV, C3),
+            whole(seqs, count, heads * HEAD),
+            whole(seqs, RIM, heads * HEAD),
+            whole(seqs, RIM, heads * HEAD),
+            whole(CONV, heads * HEAD),
             per_head(seqs, 8, count),
         ],
         out_shape=[
-            jax.ShapeDtypeStruct((seqs, count, C3), LOW),
-            jax.ShapeDtypeStruct((seqs, RIM, C3), F32),
-            jax.ShapeDtypeStruct((seqs, RIM, C3), F32),
-            jax.ShapeDtypeStruct((CONV, C3), F32),
-            jax.ShapeDtypeStruct((H, seqs, 8, count), F32),
+            jax.ShapeDtypeStruct((seqs, count, heads * HEAD), LOW),
+            jax.ShapeDtypeStruct((seqs, RIM, heads * HEAD), F32),
+            jax.ShapeDtypeStruct((seqs, RIM, heads * HEAD), F32),
+            jax.ShapeDtypeStruct((CONV, heads * HEAD), F32),
+            jax.ShapeDtypeStruct((heads, seqs, 8, count), F32),
         ],
         scratch_shapes=[
-            pltpu.VMEM((seqs, RIM + count, 2 * DK + DV), F32),
-            pltpu.VMEM((CONV, 2 * RIM + count, 2 * DK + DV), F32),
+            pltpu.VMEM((seqs, RIM + count, HEAD), F32),
+            pltpu.VMEM((CONV, 2 * RIM + count, HEAD), F32),
         ],
         compiler_params=params(),
         name="mixer_backward",
-    )(
-        pre_conv, pre_conv, pre_conv, rim, rim, rim, taps, taps, taps, cols, rows,
-        t, uw, state, gout, gend,
-    )
+    )(*[pre_conv] * 6, *[taps] * 3, cols, rows, t, uw, state, gout, gend)
+
+
+def group_cuts(g):
+    heads = H // GROUPS
+    return (
+        (g * heads * DK, heads * DK),
+        (KD + g * heads * DK, heads * DK),
+        (2 * KD + g * heads * DV, heads * DV),
+    )
+
+
+def of_group(values, g):
+    return jnp.concatenate([values[:, at : at + size] for at, size in group_cuts(g)], axis=1)
+
+
+def pack_groups(weight):
+    rows = weight.shape[0]
+    width = C3 // GROUPS
+
+    def kernel(weight_ref, *outs):
+        for g, out in enumerate(outs):
+            first = 0
+            for at, size in group_cuts(g):
+                out[:, first : first + size] = weight_ref[:, at : at + size]
+                first += size
+
+    return pl.pallas_call(
+        kernel,
+        out_shape=[jax.ShapeDtypeStruct((rows, width), weight.dtype)] * GROUPS,
+        compiler_params=pltpu.CompilerParams(vmem_limit_bytes=48 * 2**20),
+        name="pack_groups",
+    )(weight)
+
+
+def unpack_groups(parts):
+    rows = parts[0].shape[0]
+
+    def kernel(*refs):
+        for g, part in enumerate(refs[:-1]):
+            first = 0
+            for at, size in group_cuts(g):
+                refs[-1][:, at : at + size] = part[:, first : first + size].astype(F32)
+                first += size
+
+    return pl.pallas_call(
+        kernel,
+        out_shape=jax.ShapeDtypeStruct((rows, C3), F32),
+        compiler_params=pltpu.CompilerParams(vmem_limit_bytes=48 * 2**20),
+        name="unpack_groups",
+    )(*parts)
+
+
+def swap(values, axis, bit):
+    count = lax.axis_size(axis)
+    return lax.ppermute(values, axis, [(at, at ^ bit) for at in range(count)])
+
+
+def my_bit(axis, bit):
+    return (lax.axis_index(axis) // bit) % 2
+
+
+def plus(left, right):
+    return (left.astype(F32) + right.astype(F32)).astype(LOW)
+
+
+def bits_of(axis):
+    count, bits, bit = lax.axis_size(axis), [], 1
+    while bit < count:
+        bits.append(bit)
+        bit *= 2
+    return bits if bit == count else None
+
+
+def split(values):
+    return values.reshape((2, values.shape[0] // 2) + values.shape[1:])
+
+
+class Mover:
+    pending = None
+    value = None
+
+    def __init__(self):
+        self.todo = []
+
+    def begin(self):
+        if self.todo:
+            send, self.then = self.todo.pop(0)
+            self.pending = send()
+        return self
+
+    def settle(self, came):
+        self.pending = None
+        self.value = self.then(came)
+
+    def finish(self):
+        while self.todo or self.pending is not None:
+            if self.pending is None:
+                self.begin()
+            self.settle(self.pending)
+        return self.value
+
+
+class ShardSum(Mover):
+    def __init__(self, grad, scattered=False):
+        super().__init__()
+        self.value = grad.astype(LOW)
+        self.plain = any(bits_of(axis) is None for axis in ("fsdp", "dp", "seq"))
+        if self.plain:
+            shard = lax.psum_scatter(self.value, "fsdp", scatter_dimension=0, tiled=True)
+            self.value = lax.psum(shard, ("dp", "seq"))
+            return
+        if scattered:
+            self.value = lax.psum_scatter(
+                self.value, ("fsdp", "dp"), scatter_dimension=0, tiled=True
+            )
+        else:
+            bits = bits_of("fsdp")
+            self.value = self.value.reshape((2,) * len(bits) + (-1, grad.shape[1]))
+            for at, bit in enumerate(bits):
+                self.halved("fsdp", bit, len(bits) - 1 - at)
+        undo = []
+        for axis in ("dp", "seq"):
+            bits = bits_of(axis)
+            if axis == "dp" and scattered:
+                undo += [(axis, bit) for bit in reversed(bits)]
+                continue
+            for bit in bits:
+                if axis == "seq" and bit == bits[-1]:
+                    self.added(axis, bit)
+                else:
+                    self.halved(axis, bit, None)
+                    undo.append((axis, bit))
+        for axis, bit in reversed(undo):
+            self.joined(axis, bit)
+
+    def halved(self, axis, bit, dim):
+        def entries():
+            return (split(self.value), 0) if dim is None else (self.value, dim)
+
+        def send():
+            values, at = entries()
+            part = lax.dynamic_index_in_dim(values, 1 - my_bit(axis, bit), at, keepdims=False)
+            return swap(part, axis, bit)
+
+        def then(came):
+            values, at = entries()
+            part = lax.dynamic_index_in_dim(values, my_bit(axis, bit), at, keepdims=False)
+            return plus(part, came)
+
+        self.todo.append((send, then))
+
+    def added(self, axis, bit):
+        self.todo.append(
+            (lambda: swap(self.value, axis, bit), lambda came: plus(self.value, came))
+        )
+
+    def joined(self, axis, bit):
+        self.todo.append(
+            (lambda: swap(self.value, axis, bit), lambda came: put_together(self.value, came, axis, bit))
+        )
+
+
+class AllSum(Mover):
+    def __init__(self, values):
+        super().__init__()
+        self.value = values
+        for axis in ("fsdp", "dp", "seq"):
+            bits = bits_of(axis)
+            if bits is None:
+                self.value = lax.psum(self.value, axis)
+            else:
+                for bit in bits:
+                    self.step(axis, bit)
+
+    def step(self, axis, bit):
+        self.todo.append(
+            (lambda: swap(self.value, axis, bit), lambda came: self.value + came)
+        )
+
+
+def meet(movers, *arrays):
+    movers = [mover for mover in movers if mover.pending is not None]
+    count = len(arrays)
+    out = lax.optimization_barrier(tuple(arrays) + tuple(mover.pending for mover in movers))
+    for mover, came in zip(movers, out[count:]):
+        mover.settle(came)
+    return out[:count]
+
+
+def begin(*movers):
+    for mover in movers:
+        mover.begin()
+
+
+def put_together(mine, came, axis, bit):
+    first = my_bit(axis, bit) == 0
+    both = jnp.where(first, jnp.stack([mine, came]), jnp.stack([came, mine]))
+    return both.reshape((2 * mine.shape[0],) + mine.shape[1:])
+
+
+class ShardGather(Mover):
+    def __init__(self, shard):
+        super().__init__()
+        if lax.axis_size("fsdp") != 4:
+            self.value = lax.all_gather(shard, "fsdp", axis=0, tiled=True)
+            return
+        beside = swap(shard, "fsdp", 1)
+        self.todo = [
+            (lambda: swap(shard, "fsdp", 2), lambda came: came),
+            (
+                lambda: swap(self.value, "fsdp", 1),
+                lambda came: assemble((shard, beside, self.value, came)),
+            ),
+        ]
+
+
+def assemble(pieces):
+    rows, width = pieces[0].shape
+    tiles = 1
+    rows_at = rows // tiles
+
+    def piece_at(i):
+        def at(j, t, me):
+            return (jnp.where(j == i, t, jnp.where(j < i, 0, tiles - 1)), 0)
+
+        return pl.BlockSpec((rows_at, width), at)
+
+    def kernel(me_ref, *refs):
+        for i in range(4):
+
+            @pl.when(pl.program_id(0) == i)
+            def _():
+                refs[4][...] = refs[i][...]
+
+    return pl.pallas_call(
+        kernel,
+        grid_spec=pltpu.PrefetchScalarGridSpec(
+            num_scalar_prefetch=1,
+            grid=(4, tiles),
+            in_specs=[piece_at(i) for i in range(4)],
+            out_specs=pl.BlockSpec((rows_at, width), lambda j, t, me: ((me[0] ^ j) * tiles + t, 0)),
+        ),
+        out_shape=jax.ShapeDtypeStruct((4 * rows, width), pieces[0].dtype),
+        compiler_params=pltpu.CompilerParams(
+            dimension_semantics=("arbitrary", "arbitrary"), vmem_limit_bytes=48 * 2**20
+        ),
+        name="assemble",
+    )(lax.axis_index("fsdp").astype(jnp.int32).reshape(1), *pieces)
 
 
 def token_columns(log_decay, beta, seg_ids, rim_seg):
@@ -485,9 +766,11 @@
     full_ffn_gain = pieces[1].reshape(-1).astype(F32)
     full_head_gain = pieces[2].reshape(1, -1).astype(F32)
     full_conv = jnp.transpose(pieces[3].reshape(group, CONV, -1), (1, 0, 2)).reshape(CONV, C3)
-    full_conv = full_conv.astype(F32)
+    full_conv = [of_group(full_conv.astype(F32), g) for g in range(GROUPS)]
     full_decay = pieces[4].reshape(width, 2 * H)
-    full_qkv = lax.all_gather(qkv_weight, "fsdp", axis=0, tiled=True)
+    packed = list(pack_groups(qkv_weight))
+    gathers = [ShardGather(packed[0])]
+    begin(gathers[0])
     full_gate = lax.all_gather(gate_weight, "fsdp", axis=0, tiled=True)
     full_out = lax.all_gather(out_weight, "fsdp", axis=0, tiled=True)
     full_ffn_in = lax.all_gather(ffn_in_weight, "fsdp", axis=0, tiled=True)
@@ -496,39 +779,66 @@
     rows_in = inputs.astype(F32).reshape(count, width)
     normed, pull_mixer_norm = jax.vjp(rms_norm, rows_in, full_mixer_gain)
     normed_low = normed.astype(LOW)
-    pre_conv = (
-        jnp.dot(normed_low, full_qkv, preferred_element_type=F32)
-        .astype(LOW)
-        .reshape(batch, length, C3)
-    )
-    gate_out = jnp.dot(normed_low, full_gate, preferred_element_type=F32)
-    gate_out = gate_out.reshape(batch, length, VD)
+    edge = passed_along(inputs[:, length - margin :, :], "seq", 1).reshape(-1, width)
+    edge = jnp.pad(edge, ((0, edge_rows(batch) - edge.shape[0]), (0, 0)))
+    edge = rms_norm(edge.astype(F32), full_mixer_gain).astype(LOW)
+    normed_all = jnp.concatenate([normed_low, edge], axis=0)
     decay_in = jnp.dot(normed_low, full_decay, preferred_element_type=F32).reshape(
         batch, length, 2 * H
     )
     rim_seg = passed_along(segment_ids[:, length - margin :], "seq", 1)
-    rim = passed_along(pre_conv[:, length - margin :, :], "seq", 1).astype(F32)
-    rim = jnp.pad(rim, ((0, 0), (RIM - margin, 0), (0, 0)))
     rate = jnp.exp(decay_log)
     shifted_decay = decay_in[:, :, :H] + decay_bias
     log_decay = -rate * jax.nn.softplus(shifted_decay)
     beta = jax.nn.sigmoid(decay_in[:, :, H:])
     cols, rows = token_columns(log_decay, beta, segment_ids, rim_seg)
-    t, uw, local_part, carried, through, offsets = mixer_forward(
-        pre_conv, rim, full_conv, cols, rows
-    )
-
-    steps = lax.axis_size("seq") - 1
-    state_in = jnp.zeros(offsets.shape, LOW)
-    for step in range(steps):
+    hops = lax.axis_size("seq") - 1
+    heads = H // GROUPS
+    made, states, pre_convs, full_qkv = [], [None] * GROUPS, [], []
+
+    def state_hop(hop, g):
+        _, _, _, _, through, offsets = made[g]
         leaving = offsets
-        if step > 0:
-            leaving = offsets + jnp.einsum(
-                "hsij,hsjv->hsiv", through, state_in, preferred_element_type=F32
+        if hop > 0:
+            leaving = leaving + jnp.einsum(
+                "hsij,hsjv->hsiv", through, states[g], preferred_element_type=F32
             )
-        state_in = passed_along(leaving.astype(LOW), "seq", 1)
-
-    heads_low = heads_forward(local_part, carried, state_in, gate_out, full_head_gain)
+        came = lax.ppermute(leaving.astype(LOW), "seq", [(hop, hop + 1)])
+        states[g] = came if hop == 0 else states[g] + came
+
+    def mixer_group(g):
+        weight = gathers[g].finish()
+        full_qkv.append(weight)
+        pre_convs.append(jnp.dot(normed_all, weight, preferred_element_type=F32).astype(LOW))
+        made.append(mixer_forward(pre_convs[g], full_conv[g], cols, rows, g * heads, heads))
+
+    normed_all, cols, packed[1] = meet([gathers[0]], normed_all, cols, packed[1])
+    gathers.append(ShardGather(packed[1]))
+    begin(*gathers)
+    mixer_group(0)
+    state_hop(0, 0)
+    normed_all, packed[2], _ = meet([gathers[1]], normed_all, packed[2], made[0][1])
+    gathers.append(ShardGather(packed[2]))
+    begin(*gathers)
+    mixer_group(1)
+    state_hop(0, 1)
+    state_hop(1, 0)
+    normed_all, _ = meet([gathers[2]], normed_all, made[1][1])
+    mixer_group(2)
+    state_hop(0, 2)
+    state_hop(1, 1)
+    state_hop(2, 0)
+    state_hop(1, 2)
+    state_hop(2, 1)
+    state_hop(2, 2)
+    gate_out = jnp.dot(normed_low, full_gate, preferred_element_type=F32)
+    gate_out = gate_out.reshape(batch, length, VD)
+    heads_low = None
+    for g in range(GROUPS):
+        _, _, local_part, carried, _, _ = made[g]
+        heads_low = heads_forward(
+            local_part, carried, states[g], gate_out, full_head_gain, g * heads, heads_low
+        )
     heads_low = heads_low.reshape(count, VD)
     middle = rows_in + jnp.dot(heads_low, full_out, preferred_element_type=F32)
     normed_ffn, pull_ffn_norm = jax.vjp(rms_norm, middle, full_ffn_gain)
@@ -536,59 +846,117 @@
     gate_up = jnp.dot(normed_ffn_low, full_ffn_in, preferred_element_type=F32)
     hidden, pull_swiglu = jax.vjp(swiglu, gate_up)
     hidden_low = hidden.astype(LOW)
-    result = middle + jnp.dot(hidden_low, full_down, preferred_element_type=F32)
-    output = result.astype(LOW).reshape(batch, length, width)
-
-    def reduced(grad):
-        shard = lax.psum_scatter(grad.astype(LOW), "fsdp", scatter_dimension=0, tiled=True)
-        return lax.psum(shard, ("dp", "seq")).astype(F32)
 
     grad_rows = out_cotangent.reshape(count, width)
-    grad_down = jnp.einsum("rf,rd->fd", hidden_low, grad_rows, preferred_element_type=F32)
-    sum_down = reduced(grad_down)
     grad_hidden = jnp.einsum("rd,fd->rf", grad_rows, full_down, preferred_element_type=F32)
     (grad_gate_up,) = pull_swiglu(grad_hidden)
     grad_gate_up_low = grad_gate_up.astype(LOW)
-    grad_ffn_in = jnp.einsum(
-        "rd,rf->df", normed_ffn_low, grad_gate_up_low, preferred_element_type=F32
-    )
-    sum_ffn_in = reduced(grad_ffn_in)
+    grad_down = jnp.einsum("rf,rd->fd", hidden_low, grad_rows, preferred_element_type=F32)
+    grad_gate_up_low, grad_down = meet([], grad_gate_up_low, grad_down.astype(LOW))
+    r_down = ShardSum(grad_down, True)
     grad_normed_ffn = jnp.einsum(
         "rf,df->rd", grad_gate_up_low, full_ffn_in, preferred_element_type=F32
     )
     grad_middle_norm, grad_ffn_gain = pull_ffn_norm(grad_normed_ffn)
     grad_middle = grad_rows.astype(F32) + grad_middle_norm
-    grad_branch = grad_middle.astype(LOW)
+    grad_branch, grad_gate_up_low = meet([], grad_middle.astype(LOW), grad_gate_up_low)
+    grad_in = jnp.einsum(
+        "rd,rf->df", normed_ffn_low, grad_gate_up_low, preferred_element_type=F32
+    )
+    grad_heads = jnp.einsum("rd,vd->rv", grad_branch, full_out, preferred_element_type=F32)
     grad_out = jnp.einsum("rv,rd->vd", heads_low, grad_branch, preferred_element_type=F32)
-    sum_out = reduced(grad_out)
-    grad_heads = jnp.einsum("rd,vd->rv", grad_branch, full_out, preferred_element_type=F32)
-    grad_mixed, grad_gate_low, grad_head_gain, grad_state_in = heads_backward(
-        local_part, carried, state_in, gate_out, full_head_gain,
-        grad_heads.reshape(batch, length, VD),
-    )
+    grad_heads, grad_in, grad_out, r_down.value, hidden_low = meet(
+        [], grad_heads, grad_in.astype(LOW), grad_out.astype(LOW), r_down.value, hidden_low
+    )
+    r_in = ShardSum(grad_in, True)
+    r_out = ShardSum(grad_out, True)
+    begin(r_down)
+    grad_heads = grad_heads.reshape(batch, length, VD)
+    back, grad_gate_low = [], None
+    for g in range(GROUPS):
+        _, _, local_part, carried, _, _ = made[g]
+        back.append(
+            heads_backward(
+                local_part, carried, states[g], gate_out, full_head_gain, grad_heads,
+                g * heads, grad_gate_low,
+            )
+        )
+        grad_gate_low = back[g][1]
+    grad_head_gain = sum(jnp.sum(item[2], axis=(0, 1)) for item in back)
     grad_gate_low = grad_gate_low.reshape(count, VD)
     grad_gate = jnp.einsum("rd,rc->dc", normed_low, grad_gate_low, preferred_element_type=F32)
-    sum_gate = reduced(grad_gate)
-
-    grad_state_out = jnp.zeros(grad_state_in.shape, LOW)
-    for step in range(steps):
-        entering = grad_state_in
-        if step > 0:
-            entering = grad_state_in + jnp.einsum(
-                "hsji,hsjv->hsiv", through, grad_state_out, preferred_element_type=F32
-            )
-        grad_state_out = passed_along(entering.astype(LOW), "seq", -1)
-
-    grad_pre, grad_rim, grad_tail, grad_conv, grad_cols = mixer_backward(
-        pre_conv, rim, full_conv, cols, rows, t, uw, state_in, grad_mixed, grad_state_out
-    )
-    grad_rim = passed_along(grad_rim[:, RIM - margin :, :].astype(LOW), "seq", -1).astype(F32)
-    grad_tail = (grad_tail[:, RIM - margin :, :] + grad_rim).astype(LOW)
-    grad_pre_low = lax.dynamic_update_slice(grad_pre, grad_tail, (0, length - margin, 0))
-    grad_pre_low = grad_pre_low.reshape(count, C3)
-    grad_qkv = jnp.einsum("rd,rc->dc", normed_low, grad_pre_low, preferred_element_type=F32)
-    sum_qkv = reduced(grad_qkv)
-
+    result = middle + jnp.dot(hidden_low, full_down, preferred_element_type=F32)
+    output = result.astype(LOW).reshape(batch, length, width)
+
+    grad_states = [None] * GROUPS
+    for hop in range(hops, 0, -1):
+        for g in range(GROUPS):
+            entering = back[g][3]
+            if hop < hops:
+                entering = entering + jnp.einsum(
+                    "hsji,hsjv->hsiv", made[g][4], grad_states[g], preferred_element_type=F32
+                )
+            came = lax.ppermute(entering.astype(LOW), "seq", [(hop, hop - 1)])
+            grad_states[g] = came if hop == hops else grad_states[g] + came
+    mixed_a, grad_gate, output = meet([r_down], back[0][0], grad_gate.astype(LOW), output)
+    r_gate = ShardSum(grad_gate, True)
+    begin(r_down)
+    mixed_a, grad_states[0] = meet([r_down], mixed_a, grad_states[0])
+
+    def mixer_back(g, grad_mixed):
+        t, uw, _, _, _, _ = made[g]
+        return mixer_backward(
+            pre_convs[g], full_conv[g], cols, rows, t, uw, states[g], grad_mixed, grad_states[g],
+            g * heads,
+        )
+
+    def with_rim(grad_pre, grad_rim, grad_tail):
+        came = passed_along(grad_rim[:, RIM - margin :, :].astype(LOW), "seq", -1).astype(F32)
+        grad_tail = (grad_tail[:, RIM - margin :, :] + came).astype(LOW)
+        grad_pre = lax.dynamic_update_slice(grad_pre, grad_tail, (0, length - margin, 0))
+        return grad_pre.reshape(count, heads * HEAD)
+
+    def qkv_sum(grad_pre):
+        grad = jnp.einsum("rd,rc->dc", normed_low, grad_pre, preferred_element_type=F32)
+        return ShardSum(grad)
+
+    def normed_part(grad_pre, weight):
+        return jnp.einsum("rc,dc->rd", grad_pre, weight, preferred_element_type=F32)
+
+    begin(r_down)
+    got_a = mixer_back(0, mixed_a)
+    mixed_b, pre_a, rim_a, tail_a, r_in.value = meet(
+        [r_down], back[1][0], got_a[0], got_a[1], got_a[2], r_in.value
+    )
+    begin(r_down, r_in)
+    got_b = mixer_back(1, mixed_b)
+    pre_a = with_rim(pre_a, rim_a, tail_a)
+    mixed_c, pre_a, pre_b, rim_b, tail_b, r_out.value = meet(
+        [r_down, r_in], back[2][0], pre_a, got_b[0], got_b[1], got_b[2], r_out.value
+    )
+    sum_a = qkv_sum(pre_a)
+    begin(r_in, sum_a, r_out)
+    got_c = mixer_back(2, mixed_c)
+    pre_b = with_rim(pre_b, rim_b, tail_b)
+    pre_b, pre_c, rim_c, tail_c, grad_gate_low = meet(
+        [r_in, sum_a, r_out], pre_b, got_c[0], got_c[1], got_c[2], grad_gate_low
+    )
+    begin(r_in, sum_a, r_out)
+    sum_b = qkv_sum(pre_b)
+    pre_c = with_rim(pre_c, rim_c, tail_c)
+    pre_c, sum_b.value, grad_gate_low = meet([], pre_c, sum_b.value, grad_gate_low)
+    sum_c = qkv_sum(pre_c)
+    begin(sum_b, sum_c)
+    grad_normed = normed_part(pre_a, full_qkv[0]) + normed_part(pre_b, full_qkv[1])
+    pre_c, grad_normed = meet([r_in, sum_a, r_out, sum_b, sum_c], pre_c, grad_normed)
+    begin(r_in, sum_a, r_out, sum_b, sum_c)
+    grad_normed = grad_normed + normed_part(pre_c, full_qkv[2])
+    grad_cols = jnp.concatenate([got_a[4], got_b[4], got_c[4]], axis=0)
+    conv_parts = [got_a[3], got_b[3], got_c[3]]
+    spans = [0, heads * DK, 2 * heads * DK, heads * HEAD]
+    grad_conv = jnp.concatenate(
+        [part[:, low:top] for low, top in zip(spans, spans[1:]) for part in conv_parts], axis=1
+    )
     grad_log_decay = jnp.transpose(grad_cols[:, :, 0, :], (1, 2, 0))
     grad_decay_b = jnp.transpose(grad_cols[:, :, 1, :], (1, 2, 0))
     grad_decay_a = grad_log_decay * (-rate) * jax.nn.sigmoid(shifted_decay)
@@ -597,7 +965,6 @@
     grad_decay_low = jnp.concatenate([grad_decay_a, grad_decay_b], axis=-1).astype(LOW)
     grad_decay_low = grad_decay_low.reshape(count, 2 * H)
     grad_decay = jnp.einsum("rd,rc->dc", normed_low, grad_decay_low, preferred_element_type=F32)
-    grad_normed = jnp.einsum("rc,dc->rd", grad_pre_low, full_qkv, preferred_element_type=F32)
     grad_normed = grad_normed + jnp.einsum(
         "rc,dc->rd", grad_gate_low, full_gate, preferred_element_type=F32
     )
@@ -610,13 +977,22 @@
     little = (
         grad_mixer_gain,
         grad_ffn_gain,
-        jnp.sum(grad_head_gain, axis=(0, 1)),
+        grad_head_gain,
         grad_conv.reshape(-1),
         grad_decay.reshape(-1),
         grad_decay_log,
         grad_decay_bias,
     )
-    flat = lax.psum(jnp.concatenate(little), ("dp", "fsdp", "seq"))
+    small_grads = jnp.concatenate(little)
+    movers = [r_down, r_in, sum_a, sum_b, r_out, sum_c, r_gate]
+    small_grads, r_gate.value = meet(movers, small_grads, r_gate.value)
+    all_sum = AllSum(small_grads)
+    movers.append(all_sum)
+    while any(mover.todo for mover in movers):
+        begin(*movers)
+        meet(movers, small_grads)
+    flat = all_sum.value
+    sum_qkv = unpack_groups([sum_a.value, sum_b.value, sum_c.value])
     parts, first = [], 0
     for item in little:
         parts.append(flat[first : first + item.size])
@@ -632,16 +1008,16 @@
         input_grad,
         own(parts[0]),
         sum_qkv,
-        sum_gate,
+        r_gate.value.astype(F32),
         own(parts[4].reshape(width, 2 * H)),
         own(parts[3].reshape(CONV, C3), 1),
         parts[5],
         parts[6],
         own(parts[2]),
-        sum_out,
+        r_out.value.astype(F32),
         own(parts[1]),
-        sum_ffn_in,
-        sum_down,
+        r_in.value.astype(F32),
+        r_down.value.astype(F32),
     )
 
 

time: 1050 us -> 707 us (0.67)
  waiting for transfers between devices: 648 us -> 135 us
  starting transfers between devices: 28.6 us -> 97.7 us
  other arithmetic: 26.1 us -> 78.4 us
  local copies, waits for them, and re-layouts: 29 us -> 51.2 us
  Pallas kernels: 119 us -> 130 us
    psum x2 -> x0, waiting for transfers between devices: 360 us -> none  [the longest x1 246 us: reduced(): return lax.psum(shard, ('dp', 'seq')).astype(F32)]
    ppermute x9 -> x5, waiting for transfers between devices: 154 us -> 0.92 us  [passed_along(): lax.ppermute(value, axis, [(source, source + steps) for source in range(l...]
    ppermute x0 -> x69, waiting for transfers between devices: none -> 98 us  [the longest x51 71.4 us: swap(): return lax.ppermute(values, axis, [(at, at ^ bit) for at in range(count)])]
    reduce_scatter x5 -> x4, waiting for transfers between devices: 110 us -> 12.6 us  [__init__(): lax.psum_scatter(self.value, ('fsdp', 'dp'), scatter_dimension=0, tiled=T...]
    ppermute x0 -> x69, starting transfers between devices: none -> 86.2 us  [the longest x51 58.7 us: swap(): return lax.ppermute(values, axis, [(at, at ^ bit) for at in range(count)])]
    convert_element_type x8 -> x39, other arithmetic: 16.5 us -> 36.6 us  [the longest x23 15.8 us: plus(): return (left.astype(F32) + right.astype(F32)).astype(LOW)]
    all_gather x1 -> x0, waiting for transfers between devices: 18.3 us -> none  [local(): full_qkv = lax.all_gather(qkv_weight, 'fsdp', axis=0, tiled=True)]
    unnamed x114 -> x312, local copies, waits for them, and re-layouts: 11.2 us -> 28.5 us
  transfers between devices with their start and end apart: 21 -> 82, of which waited for: 13 -> 21; matrix products, arithmetic and copies ran while one was open for 15% -> 33% of each run, Pallas kernels for 11% -> 18%
where the time goes in v2:
time: 707 us; the launch traced here: 695 us
  matrix products  170 us (24%)
  waiting for transfers between devices  135 us (19%)
  Pallas kernels  130 us (18%)
  starting transfers between devices  97.7 us (14%)
  other arithmetic  78.4 us (11%)
  local copies, waits for them, and re-layouts  51.2 us (7%)
  between operations  17.9 us (3%)
  blocking collectives  16 us (2%)
    ppermute x51, waiting for transfers between devices, swap(): return lax.ppermute(values, axis, [(at, at ^ bit) for at in range(count)])  71.4 us
    pallas_call x3, Pallas kernels, mixer_backward(): pl.pallas_call(backward_kernel, grid=(heads,), in_specs=head_specs(seqs,...  59.3 us
    ppermute x51, starting transfers between devices, swap(): return lax.ppermute(values, axis, [(at, at ^ bit) for at in range(count)])  58.7 us
    pallas_call x3, Pallas kernels, mixer_forward(): pl.pallas_call(forward_kernel, grid=(heads,), in_specs=head_specs(seqs, c...  41.9 us
    unnamed x312, local copies, waits for them, and re-layouts  28.5 us
    all_gather x1, waiting for transfers between devices, local(): full_down = lax.all_gather(down_weight, 'fsdp', axis=0, tiled=True)  20.3 us
    ppermute x9, waiting for transfers between devices, local(): came = lax.ppermute(entering.astype(LOW), 'seq', [(hop, hop - 1)])  19.4 us
    dot_general x1, matrix products, local(): jnp.einsum('rd,fd->rf', grad_rows, full_down, preferred_element_type=F32)  18.5 us
  transfers between devices with their start and end apart: 82, of which 21 were waited for; matrix products, arithmetic and copies ran while one was open for 33% of the time, Pallas kernels for 18%

profile of v2, /device:TPU:0, one launch (start us, length us, event | category | flops | bytes accessed | tf_op | source)
XLA Modules:
  0.0 695.3 jit_solution(13834763168446138067)
XLA Ops:
  12.8 3.5 collective-permute-start.1
  17.1 3.5 collective-permute-start
  22.7 16.0 %all-reduce.3 = bf16[26880]{0:T(1024)(128)(2,1)S(1)} all-reduce(bf16[26880]{0:T(1024)(128)(2,1)S(1)} %dynamic-update-slice), channel_id=2, replica_groups=mesh['dp'=2,'fsdp'=4,'seq'=4] {'fsdp'}, use_global_device_ids=true, to_apply=%add.3 | all-reduce | flops 26880 | bytes 107520
  60.1 13.9 %mixer_forward.3 = (bf16[2,3,256,256]{3,2,1,0:T(8,128)(2,1)S(1)}, bf16[2,3,256,384]{3,2,1,0:T(8,128)(2,1)S(1)}, f32[3,256,512]{2,1,0:T(8,128)S(1)}, bf16[3,256,2...) custom-call(bf16[784,1024]{1,0:T(8,128)(2,1)} %convolution_convert_fusion.8.q_ref.k_ref.v_, ...), custom_call_target="tpu_custom_call" | custom-call | tf_op jit(solution)/shard_map/mixer_forward/pallas_call | solution.py:318
  79.4 3.4 collective-permute-start.5
  88.7 13.9 %mixer_forward.4 = (bf16[2,3,256,256]{3,2,1,0:T(8,128)(2,1)S(1)}, bf16[2,3,256,384]{3,2,1,0:T(8,128)(2,1)S(1)}, f32[3,256,512]{2,1,0:T(8,128)S(1)}, bf16[3,256,2...) custom-call(bf16[784,1024]{1,0:T(8,128)(2,1)} %convolution_convert_fusion.7.q_ref.k_ref.v_, ...), custom_call_target="tpu_custom_call" | custom-call | tf_op jit(solution)/shard_map/mixer_forward/pallas_call | solution.py:318
  105.1 4.3 collective-permute-start.17
  114.1 14.0 %mixer_forward.5 = (bf16[2,3,256,256]{3,2,1,0:T(8,128)(2,1)S(1)}, bf16[2,3,256,384]{3,2,1,0:T(8,128)(2,1)S(1)}, f32[3,256,512]{2,1,0:T(8,128)S(1)}, bf16[3,256,2...) custom-call(bf16[784,1024]{1,0:T(8,128)(2,1)} %convolution_convert_fusion.6.q_ref.k_ref.v_, ...), custom_call_target="tpu_custom_call" | custom-call | tf_op jit(solution)/shard_map/mixer_forward/pallas_call | solution.py:318
  130.6 7.2 %collective-permute-done.14 = bf16[2,3,128,256]{3,2,1,0:T(8,128)(2,1)S(1)} collective-permute-done((bf16[2,3,128,256]{3,2,1,0:T(8,128)(2,1)S(1)}, bf16[2,3,128,256]{3,2,1,0:T(8,128)(2,1)S(1)}, u32[]{:S(2)}, u32[]{:S(2)}) %collective-permute-start.14) | collective-permute-done | bytes 393248 | tf_op jit(solution)/shard_map/ppermute | solution.py:806
  151.5 6.5 fusion.6.refs_3_
  164.9 6.7 multiply_reduce_fusion.2
  171.7 17.5 %fusion.72 = f32[768,5632]{1,0:T(8,128)} fusion(bf16[1024,5632]{1,0:T(8,128)(2,1)} %all-gather.10.cloned.1.call-done, f32[768,1024]{1,0:T(8,128)} %get-tuple-element.342, f32[1024]{0:T(1024)S(1)} %bitcast.395, f32[768]{0:T(1024)S(1)} %fusion.68), kind=kOutput, calls=%fused_computation.232 | convolution fusion | flops 8860729344 | bytes 31988736 | tf_op jit(solution)/shard_map/dot_general | solution.py:846
  189.2 20.3 %all-gather.12.cloned.1.call-done = bf16[2816,1024]{1,0:T(8,128)(2,1)} async-done(((bf16[704,1024]{1,0:T(8,128)(2,1)}), bf16[2816,1024]{1,0:T(8,128)(2,1)}) %all-gather.12.cloned.1.call-update) | async-done | bytes 5767184 | tf_op jit(solution)/shard_map/all_gather | solution.py:777
  209.5 18.5 %fusion.35 = (f32[768,2816]{1,0:T(8,128)}, f32[768,2816]{1,0:T(8,128)}, bf16[768,2816]{1,0:T(8,128)(2,1)}) fusion(f32[768,5632]{1,0:T(8,128)} %fusion.72, bf16[768,1024]{1,0:T(8,128)(2,1)} %bitcast.321, bf16[2816,1024]{1,0:T(8,128)(2,1)} %all-gather.12.cloned.1.call-done), kind=kOutput, calls=%fused_computation.93 | convolution fusion | flops 4459462656 | bytes 46268416 | tf_op jit(solution)/shard_map/rd,fd->rf/dot_general | solution.py:851
  228.0 9.9 %convolution_convert_fusion.1 = bf16[2816,1024]{1,0:T(8,128)(2,1)} fusion(bf16[768,2816]{1,0:T(8,128)(2,1)} %get-tuple-element.185, bf16[768,1024]{1,0:T(8,128)(2,1)} %bitcast.322), kind=kOutput, calls=%fused_computation.9 | convolution fusion | flops 4432068608 | bytes 11665408 | tf_op jit(solution)/shard_map/rf,rd->fd/dot_general | solution.py:854
  237.9 9.2 %add_convert_fusion = bf16[768,5632]{1,0:T(8,128)(2,1)} fusion(f32[768,2816]{1,0:T(8,128)} %get-tuple-element.308, f32[768,2816]{1,0:T(8,128)} %get-tuple-element.307), kind=kLoop, calls=%fused_computation | loop fusion | flops 8650752 | bytes 25952256 | tf_op jit(solution)/shard_map/convert_element_type | solution.py:853
  247.2 16.3 %multiply_reduce_fusion = (f32[1024]{0:T(1024)}, f32[768]{0:T(1024)S(1)}, f32[768,1024]{1,0:T(8,128)S(1)}) fusion(f32[768,1024]{1,0:T(8,128)} %get-tuple-element.342, f32[768]{0:T(1024)S(1)} %fusion.68, f32[1024]{0:T(1024)S(1)} %bitcast.396, bf16[768,5632]{1,0:T(8,128)(2,1)} %add_convert_fusion, bf16[1024,5632]{1,0:T(8,128)(2,1)} %all-gather.10.cloned.1.call-done), kind=kOutput, calls=%fused_computation.32 | convolution fusion | flops 8863086592 | bytes 26490880 | tf_op jit(solution)/shard_map/rf,df->rd/dot_general | solution.py:857
  266.4 4.1 convolution_convert_fusion.2
  270.5 7.6 %fusion.82 = f32[768,1536]{1,0:T(8,128)} fusion(bf16[768,1024]{1,0:T(8,128)(2,1)} %copy-done.97, bf16[1536,1024]{1,0:T(8,128)(2,1)} %all-gather.8.cloned.1.call-done), kind=kOutput, calls=%fused_computation.241 | convolution fusion | flops 2415919104 | bytes 9437184 | tf_op jit(solution)/shard_map/rd,vd->rv/dot_general | solution.py:866
  278.1 15.7 %convolution_convert_fusion = bf16[1024,5632]{1,0:T(8,128)(2,1)} fusion(bf16[768,5632]{1,0:T(8,128)(2,1)} %add_convert_fusion, f32[768,1024]{1,0:T(8,128)S(1)} %copy-done.73, f32[1024]{0:T(1024)S(1)} %bitcast.398, f32[768]{0:T(1024)S(1)} %fusion.68), kind=kOutput, calls=%fused_computation.2 | convolution fusion | flops 8866496512 | bytes 23337984 | tf_op jit(solution)/shard_map/rd,rf->df/dot_general | solution.py:863
  293.8 12.6 %reduce-scatter.5.cloned.1.call-done = bf16[352,1024]{1,0:T(8,128)(2,1)} async-done(((bf16[2816,1024]{1,0:T(8,128)(2,1)}), bf16[352,1024]{1,0:T(8,128)(2,1)}) %reduce-scatter.5.cloned.1.call-update) | async-done | bytes 720912 | tf_op jit(solution)/shard_map/reduce_scatter | solution.py:566
  308.9 5.4 heads_backward.3
  315.2 5.5 heads_backward.4
  321.6 5.7 heads_backward.5
  337.5 4.2 bitcast_convert_fusion
  341.7 11.0 %add_convert_fusion.1 = bf16[768,1024]{1,0:T(8,128)(2,1)} fusion(f32[768,1024]{1,0:T(8,128)} %get-tuple-element.342, bf16[768,2816]{1,0:T(8,128)(2,1)} %get-tuple-element.185, bf16[2816,1024]{1,0:T(8,128)(2,1)} %all-gather.12.cloned.1.call-done), kind=kOutput, calls=%fused_computation.34 | convolution fusion | flops 4430757888 | bytes 14811136 | tf_op jit(solution)/shard_map/dot_general | solution.py:888
  375.3 19.4 %collective-permute-done.23 = bf16[2,3,128,256]{3,2,1,0:T(8,128)(2,1)} collective-permute-done((bf16[2,3,128,256]{3,2,1,0:T(8,128)(2,1)}, bf16[2,3,128,256]{3,2,1,0:T(8,128)(2,1)}, u32[]{:S(2)}, u32[]{:S(2)}) %collective-permute-start.23) | collective-permute-done | bytes 393248 | tf_op jit(solution)/shard_map/ppermute | solution.py:899
  397.1 6.3 collective-permute-start.25
  405.8 19.7 %mixer_backward.3 = (bf16[3,256,1024]{2,1,0:T(8,128)(2,1)S(1)}, f32[3,8,1024]{2,1,0:T(8,128)S(1)}, f32[3,8,1024]{2,1,0:T(8,128)S(1)}, f32[4,1024]{1,0:T(4,128)S(1)}, f32[2,3,8,256]{3,2,1,0:T(8,128)S(1)}) custom-call(bf16[784,1024]{1,0:T(8,128)(2,1)} %convolution_convert_fusion.8.q_ref.k_ref.v_ref.rq_ref.rk_ref.rv_ref, ...), custom_call_target="tpu_custom_call" | custom-call | tf_op jit(solution)/shard_map/mixer_backward/pallas_call | solution.py:422
  433.2 3.5 collective-permute-start.31
  440.9 19.9 %mixer_backward.4 = (bf16[3,256,1024]{2,1,0:T(8,128)(2,1)S(1)}, f32[3,8,1024]{2,1,0:T(8,128)S(1)}, f32[3,8,1024]{2,1,0:T(8,128)S(1)}, f32[4,1024]{1,0:T(4,128)S(1)}, f32[2,3,8,256]{3,2,1,0:T(8,128)S(1)}) custom-call(bf16[784,1024]{1,0:T(8,128)(2,1)} %convolution_convert_fusion.7.q_ref.k_ref.v_ref.rq_ref.rk_ref.rv_ref, ...), custom_call_target="tpu_custom_call" | custom-call | tf_op jit(solution)/shard_map/mixer_backward/pallas_call | solution.py:422
  468.4 19.7 %mixer_backward.5 = (bf16[3,256,1024]{2,1,0:T(8,128)(2,1)S(1)}, f32[3,8,1024]{2,1,0:T(8,128)S(1)}, f32[3,8,1024]{2,1,0:T(8,128)S(1)}, f32[4,1024]{1,0:T(4,128)S(1)}, f32[2,3,8,256]{3,2,1,0:T(8,128)S(1)}) custom-call(bf16[784,1024]{1,0:T(8,128)(2,1)} %convolution_convert_fusion.6.q_ref.k_ref.v_ref.rq_ref.rk_ref.rv_ref, ...), custom_call_target="tpu_custom_call" | custom-call | tf_op jit(solution)/shard_map/mixer_backward/pallas_call | solution.py:422
  515.2 12.5 %collective-permute-done.36 = bf16[64,5632]{1,0:T(8,128)(2,1)} collective-permute-done((bf16[64,5632]{1,0:T(8,128)(2,1)}, bf16[64,5632]{1,0:T(8,128)(2,1)}, u32[]{:S(2)}, u32[]{:S(2)}) %collective-permute-start.36) | collective-permute-done | bytes 720928 | tf_op jit(solution)/shard_map/ppermute | solution.py:508
  527.8 5.1 fusion.83
  548.2 3.4 convolution_convert_fusion.3
  553.7 3.5 convolution_add_fusion
  557.2 4.3 fusion.85
  575.0 3.5 fusion.84
  578.6 5.6 fusion.11
  587.9 19.9 %collective-permute-done.45 = bf16[128,5632]{1,0:T(8,128)(2,1)} collective-permute-done((bf16[128,5632]{1,0:T(8,128)(2,1)}, bf16[128,5632]{1,0:T(8,128)(2,1)}, u32[]{:S(2)}, u32[]{:S(2)}) %collective-permute-start.45) | collective-permute-done | bytes 1441824 | tf_op jit(solution)/shard_map/ppermute | solution.py:508
  618.8 3.4 maximum_select_fusion
  624.0 5.7 collective-permute-done.51
  635.8 3.4 bitcast_convert_fusion.1
  640.1 4.0 collective-permute-done.56
  649.7 4.6 collective-permute-done.65
  662.9 3.4 collective-permute-done.70
  666.3 5.6 collective-permute-done.66
  675.8 5.7 collective-permute-done.73
  (653 shorter events, 238.7 us)
Async XLA Ops:
  7.2 144.2 %all-gather.6.cloned.1.call-start = ((), (), s32[]{:S(2)}) async-start(), calls=%async_computation.4 | async-start | bytes 3932160 | tf_op jit(solution)/shard_map/all_gather | solution.py:774
  7.9 157.0 %all-gather.8.cloned.1.call-start = ((), (), s32[]{:S(2)}) async-start(), calls=%async_computation.5 | async-start | bytes 3932160 | tf_op jit(solution)/shard_map/all_gather | solution.py:775
  8.7 162.9 %all-gather.10.cloned.1.call-start = ((), (), s32[]{:S(2)}) async-start(), calls=%async_computation.6 | async-start | bytes 14417920 | tf_op jit(solution)/shard_map/all_gather | solution.py:776
  9.5 200.0 %all-gather.12.cloned.1.call-start = ((), (), s32[]{:S(2)}) async-start(), calls=%async_computation.7 | async-start | bytes 7208960 | tf_op jit(solution)/shard_map/all_gather | solution.py:777
  9.6 41.7 %collective-permute-start.2 = (bf16[256,1024]{1,0:T(8,128)(2,1)S(1)}, bf16[256,1024]{1,0:T(8,128)(2,1)S(1)}, u32[]{:S(2)}, u32[]{:S(2)}) collective-permute-start(bf16[256,1024]{1,0:T(8,128)(2,1)S(1)} %get-tuple-element.151.refs_0_), channel_id=1, source_target_pairs={{0,8},{4,12},{8,0},{12,4},{1,9},{5,13},{9,1},{13,5},{2,10},{6,14},... | collective-permute-start | bytes 1572872 | tf_op jit(solution)/shard_map/ppermute | solution.py:508
  12.7 41.6 %collective-permute-start.3 = (bf16[256,1024]{1,0:T(8,128)(2,1)S(1)}, bf16[256,1024]{1,0:T(8,128)(2,1)S(1)}, u32[]{:S(2)}, u32[]{:S(2)}) collective-permute-start(bf16[256,1024]{1,0:T(8,128)(2,1)S(1)} %get-tuple-element.151.refs_0_), channel_id=1, source_target_pairs={{0,4},{4,0},{8,12},{12,8},{1,5},{5,1},{9,13},{13,9},{2,6},{6,2},{1... | collective-permute-start | bytes 1572872 | tf_op jit(solution)/shard_map/ppermute | solution.py:508
  12.8 35.2 %collective-permute-start.1 = (s32[3,3]{1,0:T(4,128)S(1)}, s32[3,3]{1,0:T(4,128)S(1)}, u32[]{:S(2)}, u32[]{:S(2)}) collective-permute-start(s32[3,3]{1,0:T(4,128)S(1)} %slice.169), channel_id=1, source_target_pairs={{0,1},{1,2},{2,3},{4,5},{5,6},{6,7},{8,9},{9,10},{10,11},{12,13},{... | collective-permute-start | bytes 116 | tf_op jit(solution)/shard_map/ppermute | solution.py:41
  17.1 31.3 %collective-permute-start = (bf16[3,3,1024]{2,1,0:T(4,128)(2,1)S(1)}, bf16[3,3,1024]{2,1,0:T(4,128)(2,1)S(1)}, u32[]{:S(2)}, u32[]{:S(2)}) collective-permute-start(bf16[3,3,1024]{2,1,0:T(4,128)(2,1)S(1)} %slice.165), channel_id=1, source_target_pairs={{0,1},{1,2},{2,3},{4,5},{5,6},{6,7},{8,9},{9,10},{10,11},{12,13},{... | collective-permute-start | bytes 55304 | tf_op jit(solution)/shard_map/ppermute | solution.py:41
  20.6 285.8 %reduce-scatter.5.cloned.1.call-start = ((), (), s32[]{:S(2)}) async-start(), calls=%async_computation.8 | async-start | bytes 6488064 | tf_op jit(solution)/shard_map/reduce_scatter | solution.py:566
  51.6 25.6 %collective-permute-start.8 = (bf16[256,1024]{1,0:T(8,128)(2,1)S(1)}, bf16[256,1024]{1,0:T(8,128)(2,1)}, u32[]{:S(2)}, u32[]{:S(2)}) collective-permute-start(bf16[256,1024]{1,0:T(8,128)(2,1)S(1)} %get-tuple-element.161.refs_0_), channel_id=1, source_target_pairs={{0,8},{4,12},{8,0},{12,4},{1,9},{5,13},{9,1},{13,5},{2,10},{6,14},... | collective-permute-start | bytes 1572872 | tf_op jit(solution)/shard_map/ppermute | solution.py:508
  51.9 31.0 %collective-permute-start.9 = (bf16[256,1024]{1,0:T(8,128)(2,1)S(1)}, bf16[256,1024]{1,0:T(8,128)(2,1)}, u32[]{:S(2)}, u32[]{:S(2)}) collective-permute-start(bf16[256,1024]{1,0:T(8,128)(2,1)S(1)} %get-tuple-element.161.refs_0_), channel_id=1, source_target_pairs={{0,4},{4,0},{8,12},{12,8},{1,5},{5,1},{9,13},{13,9},{2,6},{6,2},{1... | collective-permute-start | bytes 1572872 | tf_op jit(solution)/shard_map/ppermute | solution.py:508
  77.4 26.4 %collective-permute-start.11 = (bf16[256,1024]{1,0:T(8,128)(2,1)S(1)}, bf16[256,1024]{1,0:T(8,128)(2,1)S(1)}, u32[]{:S(2)}, u32[]{:S(2)}) collective-permute-start(bf16[256,1024]{1,0:T(8,128)(2,1)S(1)} %get-tuple-element.165.refs_0_), channel_id=1, source_target_pairs={{0,8},{4,12},{8,0},{12,4},{1,9},{5,13},{9,1},{13,5},{2,10},{6,14},... | collective-permute-start | bytes 1572872 | tf_op jit(solution)/shard_map/ppermute | solution.py:508
  79.3 30.2 %collective-permute-start.12 = (bf16[256,1024]{1,0:T(8,128)(2,1)S(1)}, bf16[256,1024]{1,0:T(8,128)(2,1)S(1)}, u32[]{:S(2)}, u32[]{:S(2)}) collective-permute-start(bf16[256,1024]{1,0:T(8,128)(2,1)S(1)} %get-tuple-element.165.refs_0_), channel_id=1, source_target_pairs={{0,4},{4,0},{8,12},{12,8},{1,5},{5,1},{9,13},{13,9},{2,6},{6,2},{1... | collective-permute-start | bytes 1572872 | tf_op jit(solution)/shard_map/ppermute | solution.py:508
  79.4 24.7 %collective-permute-start.5 = (bf16[2,3,128,256]{3,2,1,0:T(8,128)(2,1)S(1)}, bf16[2,3,128,256]{3,2,1,0:T(8,128)(2,1)S(1)}, u32[]{:S(2)}, u32[]{:S(2)}) collective-permute-start(bf16[2,3,128,256]{3,2,1,0:T(8,128)(2,1)S(1)} %convert_element_type.502), channel_id=1, source_target_pairs={{0,1},{4,5},{8,9},{12,13},{16,17},{20,21},{24,25},{28,29}} | collective-permute-start | bytes 1179656 | tf_op jit(solution)/shard_map/ppermute | solution.py:806
  104.4 25.2 %collective-permute-start.6 = (bf16[2,3,128,256]{3,2,1,0:T(8,128)(2,1)S(1)}, bf16[2,3,128,256]{3,2,1,0:T(8,128)(2,1)S(1)}, u32[]{:S(2)}, u32[]{:S(2)}) collective-permute-start(bf16[2,3,128,256]{3,2,1,0:T(8,128)(2,1)S(1)} %fusion.20), channel_id=1, source_target_pairs={{1,2},{5,6},{9,10},{13,14},{17,18},{21,22},{25,26},{29,30}} | collective-permute-start | bytes 1179656 | tf_op jit(solution)/shard_map/ppermute | solution.py:806
  105.1 24.6 %collective-permute-start.17 = (bf16[2,3,128,256]{3,2,1,0:T(8,128)(2,1)S(1)}, bf16[2,3,128,256]{3,2,1,0:T(8,128)(2,1)S(1)}, u32[]{:S(2)}, u32[]{:S(2)}) collective-permute-start(bf16[2,3,128,256]{3,2,1,0:T(8,128)(2,1)S(1)} %convert_element_type.513), channel_id=1, source_target_pairs={{0,1},{4,5},{8,9},{12,13},{16,17},{20,21},{24,25},{28,29}} | collective-permute-start | bytes 1179656 | tf_op jit(solution)/shard_map/ppermute | solution.py:806
  247.1 180.2 %reduce-scatter.7.cloned.1.call-start = ((), (), s32[]{:S(2)}) async-start(), calls=%async_computation.9 | async-start | bytes 12976128 | tf_op jit(solution)/shard_map/reduce_scatter | solution.py:566
  306.4 158.2 %reduce-scatter.9.cloned.1.call-start = ((), (), s32[]{:S(2)}) async-start(), calls=%async_computation.10 | async-start | bytes 3538944 | tf_op jit(solution)/shard_map/reduce_scatter | solution.py:566
  307.2 280.4 %reduce-scatter.11.cloned.1.call-start = ((), (), s32[]{:S(2)}) async-start(), calls=%async_computation.11 | async-start | bytes 3538944 | tf_op jit(solution)/shard_map/reduce_scatter | solution.py:566
  329.1 23.7 %collective-permute-start.20 = (bf16[176,1024]{1,0:T(8,128)(2,1)}, bf16[176,1024]{1,0:T(8,128)(2,1)}, u32[]{:S(2)}, u32[]{:S(2)}) collective-permute-start(bf16[176,1024]{1,0:T(8,128)(2,1)} %dynamic-slice_bitcast_fusion.7), channel_id=1, source_target_pairs={{0,1},{1,0},{2,3},{3,2},{4,5},{5,4},{6,7},{7,6},{8,9},{9,8},{10,11... | collective-permute-start | bytes 1081352 | tf_op jit(solution)/shard_map/ppermute | solution.py:508
  331.7 25.4 %collective-permute-start.21 = (bf16[2,3,128,256]{3,2,1,0:T(8,128)(2,1)}, bf16[2,3,128,256]{3,2,1,0:T(8,128)(2,1)}, u32[]{:S(2)}, u32[]{:S(2)}) collective-permute-start(bf16[2,3,128,256]{3,2,1,0:T(8,128)(2,1)} %convert_element_type.527), channel_id=1, source_target_pairs={{3,2},{7,6},{11,10},{15,14},{19,18},{23,22},{27,26},{31,30}} | collective-permute-start | bytes 1179656 | tf_op jit(solution)/shard_map/ppermute | solution.py:899
  333.9 25.2 %collective-permute-start.27 = (bf16[2,3,128,256]{3,2,1,0:T(8,128)(2,1)}, bf16[2,3,128,256]{3,2,1,0:T(8,128)(2,1)}, u32[]{:S(2)}, u32[]{:S(2)}) collective-permute-start(bf16[2,3,128,256]{3,2,1,0:T(8,128)(2,1)} %convert_element_type.539), channel_id=1, source_target_pairs={{3,2},{7,6},{11,10},{15,14},{19,18},{23,22},{27,26},{31,30}} | collective-permute-start | bytes 1179656 | tf_op jit(solution)/shard_map/ppermute | solution.py:899
  336.1 26.5 %collective-permute-start.33 = (bf16[2,3,128,256]{3,2,1,0:T(8,128)(2,1)}, bf16[2,3,128,256]{3,2,1,0:T(8,128)(2,1)}, u32[]{:S(2)}, u32[]{:S(2)}) collective-permute-start(bf16[2,3,128,256]{3,2,1,0:T(8,128)(2,1)} %convert_element_type.544), channel_id=1, source_target_pairs={{3,2},{7,6},{11,10},{15,14},{19,18},{23,22},{27,26},{31,30}} | collective-permute-start | bytes 1179656 | tf_op jit(solution)/shard_map/ppermute | solution.py:899
  355.0 40.8 %collective-permute-start.24 = (bf16[176,1024]{1,0:T(8,128)(2,1)}, bf16[176,1024]{1,0:T(8,128)(2,1)}, u32[]{:S(2)}, u32[]{:S(2)}) collective-permute-start(bf16[176,1024]{1,0:T(8,128)(2,1)} %fusion.40), channel_id=1, source_target_pairs={{0,2},{1,3},{2,0},{3,1},{4,6},{5,7},{6,4},{7,5},{8,10},{9,11},{10,... | collective-permute-start | bytes 1081352 | tf_op jit(solution)/shard_map/ppermute | solution.py:508
  368.2 26.5 %collective-permute-start.23 = (bf16[2,3,128,256]{3,2,1,0:T(8,128)(2,1)}, bf16[2,3,128,256]{3,2,1,0:T(8,128)(2,1)}, u32[]{:S(2)}, u32[]{:S(2)}) collective-permute-start(bf16[2,3,128,256]{3,2,1,0:T(8,128)(2,1)} %fusion.27), channel_id=1, source_target_pairs={{1,0},{5,4},{9,8},{13,12},{17,16},{21,20},{25,24},{29,28}} | collective-permute-start | bytes 1179656 | tf_op jit(solution)/shard_map/ppermute | solution.py:899
  372.5 64.8 %collective-permute-start.29 = (bf16[2,3,128,256]{3,2,1,0:T(8,128)(2,1)}, bf16[2,3,128,256]{3,2,1,0:T(8,128)(2,1)}, u32[]{:S(2)}, u32[]{:S(2)}) collective-permute-start(bf16[2,3,128,256]{3,2,1,0:T(8,128)(2,1)} %fusion.29), channel_id=1, source_target_pairs={{1,0},{5,4},{9,8},{13,12},{17,16},{21,20},{25,24},{29,28}} | collective-permute-start | bytes 1179656 | tf_op jit(solution)/shard_map/ppermute | solution.py:899
  397.1 30.2 %collective-permute-start.25 = (bf16[176,1024]{1,0:T(8,128)(2,1)S(1)}, bf16[176,1024]{1,0:T(8,128)(2,1)}, u32[]{:S(2)}, u32[]{:S(2)}) collective-permute-start(bf16[176,1024]{1,0:T(8,128)(2,1)S(1)} %add_convert_fusion.3), channel_id=1, source_target_pairs={{0,1},{1,0},{2,3},{3,2},{4,5},{5,4},{6,7},{7,6},{8,9},{9,8},{10,11... | collective-permute-start | bytes 1081352 | tf_op jit(solution)/shard_map/ppermute | solution.py:508
  404.4 34.0 %collective-permute-start.35 = (bf16[2,3,128,256]{3,2,1,0:T(8,128)(2,1)}, bf16[2,3,128,256]{3,2,1,0:T(8,128)(2,1)}, u32[]{:S(2)}, u32[]{:S(2)}) collective-permute-start(bf16[2,3,128,256]{3,2,1,0:T(8,128)(2,1)} %fusion.31), channel_id=1, source_target_pairs={{1,0},{5,4},{9,8},{13,12},{17,16},{21,20},{25,24},{29,28}} | collective-permute-start | bytes 1179656 | tf_op jit(solution)/shard_map/ppermute | solution.py:899
  429.8 34.8 %collective-permute-start.30 = (bf16[352,1024]{1,0:T(8,128)(2,1)}, bf16[352,1024]{1,0:T(8,128)(2,1)}, u32[]{:S(2)}, u32[]{:S(2)}) collective-permute-start(bf16[352,1024]{1,0:T(8,128)(2,1)} %bitcast.26), channel_id=1, source_target_pairs={{0,16},{16,0},{1,17},{17,1},{2,18},{18,2},{3,19},{19,3},{4,20},{20... | collective-permute-start | bytes 2162696 | tf_op jit(solution)/shard_map/ppermute | solution.py:508
  433.2 31.4 %collective-permute-start.31 = (bf16[64,5632]{1,0:T(8,128)(2,1)}, bf16[64,5632]{1,0:T(8,128)(2,1)}, u32[]{:S(2)}, u32[]{:S(2)}) collective-permute-start(bf16[64,5632]{1,0:T(8,128)(2,1)} %dynamic-slice_bitcast_fusion.3), channel_id=1, source_target_pairs={{0,1},{1,0},{2,3},{3,2},{4,5},{5,4},{6,7},{7,6},{8,9},{9,8},{10,11... | collective-permute-start | bytes 2162696 | tf_op jit(solution)/shard_map/ppermute | solution.py:508
  439.5 23.6 %collective-permute-start.26 = (bf16[3,3,1024]{2,1,0:T(4,128)(2,1)S(1)}, bf16[3,3,1024]{2,1,0:T(4,128)(2,1)S(1)}, u32[]{:S(2)}, u32[]{:S(2)}) collective-permute-start(bf16[3,3,1024]{2,1,0:T(4,128)(2,1)S(1)} %slice.313), channel_id=1, source_target_pairs={{1,0},{2,1},{3,2},{5,4},{6,5},{7,6},{9,8},{10,9},{11,10},{13,12},{... | collective-permute-start | bytes 55304 | tf_op jit(solution)/shard_map/ppermute | solution.py:41
  495.1 32.7 %collective-permute-start.36 = (bf16[64,5632]{1,0:T(8,128)(2,1)}, bf16[64,5632]{1,0:T(8,128)(2,1)}, u32[]{:S(2)}, u32[]{:S(2)}) collective-permute-start(bf16[64,5632]{1,0:T(8,128)(2,1)} %fusion.19), channel_id=1, source_target_pairs={{0,2},{1,3},{2,0},{3,1},{4,6},{5,7},{6,4},{7,5},{8,10},{9,11},{10,... | collective-permute-start | bytes 2162696 | tf_op jit(solution)/shard_map/ppermute | solution.py:508
  498.1 12.6 %collective-permute-start.32 = (bf16[3,3,1024]{2,1,0:T(4,128)(2,1)S(1)}, bf16[3,3,1024]{2,1,0:T(4,128)(2,1)S(1)}, u32[]{:S(2)}, u32[]{:S(2)}) collective-permute-start(bf16[3,3,1024]{2,1,0:T(4,128)(2,1)S(1)} %slice.312), channel_id=1, source_target_pairs={{1,0},{2,1},{3,2},{5,4},{6,5},{7,6},{9,8},{10,9},{11,10},{13,12},{... | collective-permute-start | bytes 55304 | tf_op jit(solution)/shard_map/ppermute | solution.py:41
  502.8 25.0 %collective-permute-start.37 = (bf16[2,256,1024]{2,1,0:T(8,128)(2,1)}, bf16[2,256,1024]{2,1,0:T(8,128)(2,1)}, u32[]{:S(2)}, u32[]{:S(2)}) collective-permute-start(bf16[2,256,1024]{2,1,0:T(8,128)(2,1)} %dynamic-slice_bitcast_fusion.2), channel_id=1, source_target_pairs={{0,4},{4,0},{8,12},{12,8},{1,5},{5,1},{9,13},{13,9},{2,6},{6,2},{1... | collective-permute-start | bytes 3145736 | tf_op jit(solution)/shard_map/ppermute | solution.py:508
  537.0 24.5 %collective-permute-start.42 = (bf16[96,1024]{1,0:T(8,128)(2,1)S(1)}, bf16[96,1024]{1,0:T(8,128)(2,1)S(1)}, u32[]{:S(2)}, u32[]{:S(2)}) collective-permute-start(bf16[96,1024]{1,0:T(8,128)(2,1)S(1)} %fusion.45), channel_id=1, source_target_pairs={{0,2},{1,3},{2,0},{3,1},{4,6},{5,7},{6,4},{7,5},{8,10},{9,11},{10,... | collective-permute-start | bytes 589832 | tf_op jit(solution)/shard_map/ppermute | solution.py:508
  540.9 20.7 %collective-permute-start.41 = (bf16[256,1024]{1,0:T(8,128)(2,1)}, bf16[256,1024]{1,0:T(8,128)(2,1)}, u32[]{:S(2)}, u32[]{:S(2)}) collective-permute-start(bf16[256,1024]{1,0:T(8,128)(2,1)} %dynamic-slice_bitcast_fusion.6), channel_id=1, source_target_pairs={{0,8},{4,12},{8,0},{12,4},{1,9},{5,13},{9,1},{13,5},{2,10},{6,14},... | collective-permute-start | bytes 1572872 | tf_op jit(solution)/shard_map/ppermute | solution.py:508
  544.1 18.5 %collective-permute-start.40 = (bf16[64,5632]{1,0:T(8,128)(2,1)S(1)}, bf16[64,5632]{1,0:T(8,128)(2,1)}, u32[]{:S(2)}, u32[]{:S(2)}) collective-permute-start(bf16[64,5632]{1,0:T(8,128)(2,1)S(1)} %add_convert_fusion.2), channel_id=1, source_target_pairs={{0,1},{1,0},{2,3},{3,2},{4,5},{5,4},{6,7},{7,6},{8,9},{9,8},{10,11... | collective-permute-start | bytes 2162696 | tf_op jit(solution)/shard_map/ppermute | solution.py:508
  563.8 23.7 %collective-permute-start.49 = (bf16[256,1024]{1,0:T(8,128)(2,1)}, bf16[256,1024]{1,0:T(8,128)(2,1)}, u32[]{:S(2)}, u32[]{:S(2)}) collective-permute-start(bf16[256,1024]{1,0:T(8,128)(2,1)} %dynamic-slice_bitcast_fusion.4), channel_id=1, source_target_pairs={{0,8},{4,12},{8,0},{12,4},{1,9},{5,13},{9,1},{13,5},{2,10},{6,14},... | collective-permute-start | bytes 1572872 | tf_op jit(solution)/shard_map/ppermute | solution.py:508
  564.4 23.1 %collective-permute-start.48 = (bf16[96,1024]{1,0:T(8,128)(2,1)S(1)}, bf16[96,1024]{1,0:T(8,128)(2,1)}, u32[]{:S(2)}, u32[]{:S(2)}) collective-permute-start(bf16[96,1024]{1,0:T(8,128)(2,1)S(1)} %add_convert_fusion.5), channel_id=1, source_target_pairs={{0,1},{1,0},{2,3},{3,2},{4,5},{5,4},{6,7},{7,6},{8,9},{9,8},{10,11... | collective-permute-start | bytes 589832 | tf_op jit(solution)/shard_map/ppermute | solution.py:508
  566.8 21.0 %collective-permute-start.47 = (bf16[256,1024]{1,0:T(8,128)(2,1)}, bf16[256,1024]{1,0:T(8,128)(2,1)}, u32[]{:S(2)}, u32[]{:S(2)}) collective-permute-start(bf16[256,1024]{1,0:T(8,128)(2,1)} %dynamic-slice_bitcast_fusion.5), channel_id=1, source_target_pairs={{0,8},{4,12},{8,0},{12,4},{1,9},{5,13},{9,1},{13,5},{2,10},{6,14},... | collective-permute-start | bytes 1572872 | tf_op jit(solution)/shard_map/ppermute | solution.py:508
  570.2 17.3 %collective-permute-start.46 = (bf16[128,1024]{1,0:T(8,128)(2,1)}, bf16[128,1024]{1,0:T(8,128)(2,1)}, u32[]{:S(2)}, u32[]{:S(2)}) collective-permute-start(bf16[128,1024]{1,0:T(8,128)(2,1)} %dynamic-slice_bitcast_fusion.10), channel_id=1, source_target_pairs={{0,16},{16,0},{1,17},{17,1},{2,18},{18,2},{3,19},{19,3},{4,20},{20... | collective-permute-start | bytes 786440 | tf_op jit(solution)/shard_map/ppermute | solution.py:508
  574.6 33.2 %collective-permute-start.45 = (bf16[128,5632]{1,0:T(8,128)(2,1)}, bf16[128,5632]{1,0:T(8,128)(2,1)}, u32[]{:S(2)}, u32[]{:S(2)}) collective-permute-start(bf16[128,5632]{1,0:T(8,128)(2,1)} %bitcast.52), channel_id=1, source_target_pairs={{0,16},{16,0},{1,17},{17,1},{2,18},{18,2},{3,19},{19,3},{4,20},{20... | collective-permute-start | bytes 4325384 | tf_op jit(solution)/shard_map/ppermute | solution.py:508
  609.4 14.6 %collective-permute-start.53 = (bf16[128,1024]{1,0:T(8,128)(2,1)S(1)}, bf16[128,1024]{1,0:T(8,128)(2,1)S(1)}, u32[]{:S(2)}, u32[]{:S(2)}) collective-permute-start(bf16[128,1024]{1,0:T(8,128)(2,1)S(1)} %dynamic-slice_bitcast_fusion.8), channel_id=1, source_target_pairs={{0,16},{16,0},{1,17},{17,1},{2,18},{18,2},{3,19},{19,3},{4,20},{20... | collective-permute-start | bytes 786440 | tf_op jit(solution)/shard_map/ppermute | solution.py:508
  612.0 17.7 %collective-permute-start.52 = (bf16[192,1024]{1,0:T(8,128)(2,1)S(1)}, bf16[192,1024]{1,0:T(8,128)(2,1)S(1)}, u32[]{:S(2)}, u32[]{:S(2)}) collective-permute-start(bf16[192,1024]{1,0:T(8,128)(2,1)S(1)} %bitcast.336), channel_id=1, source_target_pairs={{0,16},{16,0},{1,17},{17,1},{2,18},{18,2},{3,19},{19,3},{4,20},{20... | collective-permute-start | bytes 1179656 | tf_op jit(solution)/shard_map/ppermute | solution.py:508
  613.9 15.8 %collective-permute-start.51 = (bf16[128,1024]{1,0:T(8,128)(2,1)S(1)}, bf16[128,1024]{1,0:T(8,128)(2,1)S(1)}, u32[]{:S(2)}, u32[]{:S(2)}) collective-permute-start(bf16[128,1024]{1,0:T(8,128)(2,1)S(1)} %dynamic-slice_bitcast_fusion.9), channel_id=1, source_target_pairs={{0,16},{16,0},{1,17},{17,1},{2,18},{18,2},{3,19},{19,3},{4,20},{20... | collective-permute-start | bytes 786440 | tf_op jit(solution)/shard_map/ppermute | solution.py:508
  629.8 14.3 %collective-permute-start.59 = (bf16[64,1536]{1,0:T(8,128)(2,1)S(1)}, bf16[64,1536]{1,0:T(8,128)(2,1)S(1)}, u32[]{:S(2)}, u32[]{:S(2)}) collective-permute-start(bf16[64,1536]{1,0:T(8,128)(2,1)S(1)} %fusion.44), channel_id=1, source_target_pairs={{0,2},{1,3},{2,0},{3,1},{4,6},{5,7},{6,4},{7,5},{8,10},{9,11},{10,... | collective-permute-start | bytes 589832 | tf_op jit(solution)/shard_map/ppermute | solution.py:508
  644.1 12.8 %collective-permute-start.64 = (bf16[64,1536]{1,0:T(8,128)(2,1)S(1)}, bf16[64,1536]{1,0:T(8,128)(2,1)S(1)}, u32[]{:S(2)}, u32[]{:S(2)}) collective-permute-start(bf16[64,1536]{1,0:T(8,128)(2,1)S(1)} %add_convert_fusion.4), channel_id=1, source_target_pairs={{0,1},{1,0},{2,3},{3,2},{4,5},{5,4},{6,7},{7,6},{8,9},{9,8},{10,11... | collective-permute-start | bytes 589832 | tf_op jit(solution)/shard_map/ppermute | solution.py:508
  657.0 14.9 %collective-permute-start.69 = (bf16[128,1536]{1,0:T(8,128)(2,1)S(1)}, bf16[128,1536]{1,0:T(8,128)(2,1)S(1)}, u32[]{:S(2)}, u32[]{:S(2)}) collective-permute-start(bf16[128,1536]{1,0:T(8,128)(2,1)S(1)} %bitcast.338), channel_id=1, source_target_pairs={{0,16},{16,0},{1,17},{17,1},{2,18},{18,2},{3,19},{19,3},{4,20},{20... | collective-permute-start | bytes 1179656 | tf_op jit(solution)/shard_map/ppermute | solution.py:508
  (177 other events, 2038.2 us)
Sparse Core Ops, SparseCore 0:
  9.6 34.4 all-gather.5
  45.6 40.9 all-gather.7
  88.2 76.3 all-gather.9
  166.1 43.3 all-gather.11
  247.2 59.0 reduce-scatter.4
  310.1 86.7 reduce-scatter.6
  400.7 52.8 reduce-scatter.8
  457.0 46.2 reduce-scatter.10

commit v3 on v2

--- a/solution.py
+++ b/solution.py
@@ -43,11 +43,6 @@
 
 def rms_norm(values, gain):
     return values * lax.rsqrt(jnp.mean(values * values, axis=-1, keepdims=True) + EPSILON) * gain
-
-
-def swiglu(gate_up):
-    half = gate_up.shape[1] // 2
-    return jax.nn.silu(gate_up[:, :half]) * gate_up[:, half:]
 
 
 def iotas(count):
@@ -115,24 +110,35 @@
         target = jnp.concatenate([beta * value.astype(F32), beta * start * keyf], axis=1).astype(LOW)
         state.append(dict(lower=lower, attend=attend, target=target, query=query,
                           ending=(end * keyf).astype(LOW), start=start))
-    eye = (order == other).astype(F32)
-    inverse = [eye - jnp.where((order >> 1 == other >> 1) & (order > other), x["lower"], 0.0) for x in state]
+    inverse, lowers = [], []
+    joined = order ^ other
+    eye = (joined == 0).astype(LOW)
+    for x in state:
+        lower = x["lower"].astype(LOW)
+        lowers.append(lower)
+        inverse.append(eye - lower * ((joined == 1) & (order > other)).astype(LOW))
     level = 1
-    while (2 << level) <= count:
-        pick = (
-            (order >> (level + 1) == other >> (level + 1))
-            & ((order >> level) & 1 == 1)
-            & ((other >> level) & 1 == 0)
+    while (4 << level) <= count:
+        pick = ((joined >> level) == 1).astype(LOW)
+        half = [mm(lowers[s] * pick, inverse[s]).astype(LOW) for s in range(seqs)]
+        for s in range(seqs):
+            inverse[s] = inverse[s] - mm(inverse[s], half[s]).astype(LOW)
+        level += 1
+    mid = count // 2
+    corner = [mm(lowers[s][mid:, :mid], inverse[s][:mid, :mid]) for s in range(seqs)]
+    blank = jnp.zeros((mid, mid), LOW)
+    for s in range(seqs):
+        left = mm(inverse[s][mid:, mid:], corner[s]).astype(LOW)
+        inverse[s] = jnp.concatenate(
+            [
+                jnp.concatenate([inverse[s][:mid, :mid], blank], axis=1),
+                jnp.concatenate([-left, inverse[s][mid:, mid:]], axis=1),
+            ],
+            axis=0,
         )
-        half = []
-        for s in range(seqs):
-            half.append(mm(jnp.where(pick, state[s]["lower"], 0.0), inverse[s]))
-        for s in range(seqs):
-            inverse[s] = inverse[s] - mm(inverse[s], half[s])
-        level += 1
     for s in range(seqs):
         x = state[s]
-        t = inverse[s].astype(LOW)
+        t = inverse[s]
         t_ref[0, s] = t
         uw = mm(t, x["target"]).astype(LOW)
         uw_ref[0, s] = uw
@@ -416,11 +422,25 @@
     )(*operands)
 
 
-def mixer_backward(pre_conv, taps, cols, rows, t, uw, state, gout, gend, first):
+def mixer_backward(
+    pre_conv, taps, cols, rows, t, uw, state, gout, gend, first, place, width, rims, kept
+):
     seqs, count = cols.shape[1], cols.shape[2]
     heads = state.shape[0]
+    run = heads * HEAD
+
+    def at(*shape):
+        return pl.BlockSpec(shape, lambda h: (0, 0, place))
+
+    operands = [*[pre_conv] * 6, *[taps] * 3, cols, rows, t, uw, state, gout, gend]
+    inputs = len(operands)
+    aliases = {inputs + i: i for i in range(len(kept))}
+
+    def kernel(*refs):
+        backward_kernel(*refs[:inputs], *refs[inputs + len(kept) :])
+
     return pl.pallas_call(
-        backward_kernel,
+        kernel,
         grid=(heads,),
         in_specs=head_specs(seqs, count, first, heads)
         + [
@@ -429,28 +449,82 @@
             per_head(seqs, DK, DV),
             by_column(seqs, count, DV),
             per_head(seqs, DK, DV),
-        ],
+        ]
+        + [pl.BlockSpec(memory_space=pl.ANY)] * len(kept),
         out_specs=[
-            whole(seqs, count, heads * HEAD),
-            whole(seqs, RIM, heads * HEAD),
-            whole(seqs, RIM, heads * HEAD),
-            whole(CONV, heads * HEAD),
+            at(seqs, count, run),
+            at(seqs, RIM, run),
+            at(seqs, RIM, run),
+            whole(CONV, run),
             per_head(seqs, 8, count),
         ],
         out_shape=[
-            jax.ShapeDtypeStruct((seqs, count, heads * HEAD), LOW),
-            jax.ShapeDtypeStruct((seqs, RIM, heads * HEAD), F32),
-            jax.ShapeDtypeStruct((seqs, RIM, heads * HEAD), F32),
-            jax.ShapeDtypeStruct((CONV, heads * HEAD), F32),
+            jax.ShapeDtypeStruct((seqs, count, width), LOW),
+            jax.ShapeDtypeStruct((seqs, RIM, rims), F32),
+            jax.ShapeDtypeStruct((seqs, RIM, rims), F32),
+            jax.ShapeDtypeStruct((CONV, run), F32),
             jax.ShapeDtypeStruct((heads, seqs, 8, count), F32),
         ],
         scratch_shapes=[
             pltpu.VMEM((seqs, RIM + count, HEAD), F32),
             pltpu.VMEM((CONV, 2 * RIM + count, HEAD), F32),
         ],
+        input_output_aliases=aliases,
         compiler_params=params(),
         name="mixer_backward",
-    )(*[pre_conv] * 6, *[taps] * 3, cols, rows, t, uw, state, gout, gend)
+    )(*operands, *kept)
+
+
+def ffn_kernel(x_ref, up_ref, side_ref, grad_ref, down_ref, hidden_ref, back_ref):
+    tile = up_ref.shape[1]
+    half = back_ref.shape[1] // 2
+    at = pl.program_id(0) * tile
+    rows = x_ref.shape[0]
+    step = 256 if rows % 256 == 0 else rows
+
+    def part(i, _):
+        here = pl.ds(pl.multiple_of(i * step, step), step)
+        x = x_ref[here, :]
+        a = mm(x, up_ref[...])
+        b = mm(x, side_ref[...])
+        grad = mm(grad_ref[here, :], down_ref[...], NT)
+        sig = jax.nn.sigmoid(a)
+        act = a * sig
+        hidden_ref[here, :] = (act * b).astype(LOW)
+        first = grad * b * (sig + act * (1.0 - sig))
+        back_ref[here, pl.ds(pl.multiple_of(at, tile), tile)] = first.astype(LOW)
+        back_ref[here, pl.ds(pl.multiple_of(half + at, tile), tile)] = (grad * act).astype(LOW)
+        return 0
+
+    lax.fori_loop(0, rows // step, part, 0)
+
+
+def ffn_middle(x, weight, grad, down):
+    rows, width = x.shape
+    units = down.shape[0]
+    tile = 256
+    tiles = units // tile
+    return pl.pallas_call(
+        ffn_kernel,
+        grid=(tiles,),
+        in_specs=[
+            pl.BlockSpec((rows, width), lambda j: (0, 0)),
+            pl.BlockSpec((width, tile), lambda j: (0, j)),
+            pl.BlockSpec((width, tile), lambda j: (0, tiles + j)),
+            pl.BlockSpec((rows, width), lambda j: (0, 0)),
+            pl.BlockSpec((tile, width), lambda j: (j, 0)),
+        ],
+        out_specs=[
+            pl.BlockSpec((rows, tile), lambda j: (0, j)),
+            pl.BlockSpec((rows, 2 * units), lambda j: (0, 0)),
+        ],
+        out_shape=[
+            jax.ShapeDtypeStruct((rows, units), LOW),
+            jax.ShapeDtypeStruct((rows, 2 * units), LOW),
+        ],
+        compiler_params=params(),
+        name="ffn_middle",
+    )(x, weight, weight, grad, down)
 
 
 def group_cuts(g):
@@ -485,22 +559,23 @@
     )(weight)
 
 
-def unpack_groups(parts):
-    rows = parts[0].shape[0]
-
-    def kernel(*refs):
-        for g, part in enumerate(refs[:-1]):
-            first = 0
-            for at, size in group_cuts(g):
-                refs[-1][:, at : at + size] = part[:, first : first + size].astype(F32)
-                first += size
+def unpack_groups(first, last):
+    rows = first.shape[0]
+    run = C3 // GROUPS
+
+    def kernel(first_ref, last_ref, qkv_ref):
+        for g in range(GROUPS):
+            part, at = (last_ref, 0) if g == GROUPS - 1 else (first_ref, g * run)
+            for to, size in group_cuts(g):
+                qkv_ref[:, to : to + size] = part[:, at : at + size].astype(F32)
+                at += size
 
     return pl.pallas_call(
         kernel,
         out_shape=jax.ShapeDtypeStruct((rows, C3), F32),
         compiler_params=pltpu.CompilerParams(vmem_limit_bytes=48 * 2**20),
         name="unpack_groups",
-    )(*parts)
+    )(first, last)
 
 
 def swap(values, axis, bit):
@@ -553,16 +628,31 @@
         return self.value
 
 
+def scattered_sums():
+    return all(bits_of(axis) is not None for axis in ("fsdp", "dp", "seq"))
+
+
+def scatter(grad):
+    if not scattered_sums():
+        shard = lax.psum_scatter(grad, "fsdp", scatter_dimension=0, tiled=True)
+        return lax.psum(shard, ("dp", "seq"))
+    return lax.psum_scatter(grad, ("fsdp", "dp"), scatter_dimension=0, tiled=True)
+
+
 class ShardSum(Mover):
-    def __init__(self, grad, scattered=False):
+    def __init__(self, grad, scattered=False, ready=False):
         super().__init__()
         self.value = grad.astype(LOW)
+        if ready and not scattered_sums():
+            return
         self.plain = any(bits_of(axis) is None for axis in ("fsdp", "dp", "seq"))
         if self.plain:
             shard = lax.psum_scatter(self.value, "fsdp", scatter_dimension=0, tiled=True)
             self.value = lax.psum(shard, ("dp", "seq"))
             return
-        if scattered:
+        if ready:
+            scattered = True
+        elif scattered:
             self.value = lax.psum_scatter(
                 self.value, ("fsdp", "dp"), scatter_dimension=0, tiled=True
             )
@@ -613,6 +703,23 @@
         )
 
 
+class Chain(Mover):
+    def __init__(self, through, offsets, spec, step):
+        super().__init__()
+        last = lax.axis_size("seq") - 1
+        for hop in range(last) if step > 0 else range(last, 0, -1):
+            self.todo.append((partial(self.leave, through, offsets, spec, hop, step), self.take))
+
+    def leave(self, through, offsets, spec, hop, step):
+        leaving = offsets
+        if self.value is not None:
+            leaving = leaving + jnp.einsum(spec, through, self.value, preferred_element_type=F32)
+        return lax.ppermute(leaving.astype(LOW), "seq", [(hop, hop + step)])
+
+    def take(self, came):
+        return came if self.value is None else self.value + came
+
+
 class AllSum(Mover):
     def __init__(self, values):
         super().__init__()
@@ -665,6 +772,24 @@
                 lambda came: assemble((shard, beside, self.value, came)),
             ),
         ]
+
+
+def gather_halves(shard):
+    count = lax.axis_size("dp")
+    part = shard.reshape((count, shard.shape[0] // count) + shard.shape[1:])
+    part = lax.dynamic_index_in_dim(part, lax.axis_index("dp"), 0, keepdims=False)
+    return lax.all_gather(part, ("fsdp", "dp"), axis=0, tiled=True)
+
+
+def gather_small(values):
+    if lax.axis_size("fsdp") != 4:
+        return lax.all_gather(values, "fsdp", axis=0)
+    me = lax.axis_index("fsdp")
+    rows = [values] + [swap(values, "fsdp", bit) for bit in (1, 2, 3)]
+    out = jnp.zeros((4, values.shape[0]), values.dtype)
+    for i, row in enumerate(rows):
+        out = lax.dynamic_update_slice(out, row[None], (me ^ i, 0))
+    return out
 
 
 def assemble(pieces):
@@ -756,7 +881,7 @@
             decay_weight.reshape(-1),
         ]
     )
-    small = lax.all_gather(small, "fsdp", axis=0)
+    small = gather_small(small)
     cuts = [mixer_gain.size, ffn_gain.size, head_gain.size, conv_weight.size, decay_weight.size]
     pieces, first = [], 0
     for size in cuts:
@@ -772,9 +897,8 @@
     gathers = [ShardGather(packed[0])]
     begin(gathers[0])
     full_gate = lax.all_gather(gate_weight, "fsdp", axis=0, tiled=True)
-    full_out = lax.all_gather(out_weight, "fsdp", axis=0, tiled=True)
-    full_ffn_in = lax.all_gather(ffn_in_weight, "fsdp", axis=0, tiled=True)
-    full_down = lax.all_gather(down_weight, "fsdp", axis=0, tiled=True)
+    full_down = gather_halves(down_weight)
+    full_ffn_in = gather_halves(ffn_in_weight)
 
     rows_in = inputs.astype(F32).reshape(count, width)
     normed, pull_mixer_norm = jax.vjp(rms_norm, rows_in, full_mixer_gain)
@@ -792,167 +916,179 @@
     log_decay = -rate * jax.nn.softplus(shifted_decay)
     beta = jax.nn.sigmoid(decay_in[:, :, H:])
     cols, rows = token_columns(log_decay, beta, segment_ids, rim_seg)
-    hops = lax.axis_size("seq") - 1
     heads = H // GROUPS
-    made, states, pre_convs, full_qkv = [], [None] * GROUPS, [], []
-
-    def state_hop(hop, g):
-        _, _, _, _, through, offsets = made[g]
-        leaving = offsets
-        if hop > 0:
-            leaving = leaving + jnp.einsum(
-                "hsij,hsjv->hsiv", through, states[g], preferred_element_type=F32
-            )
-        came = lax.ppermute(leaving.astype(LOW), "seq", [(hop, hop + 1)])
-        states[g] = came if hop == 0 else states[g] + came
+    made, states, pre_convs, full_qkv = [], [], [], []
 
     def mixer_group(g):
         weight = gathers[g].finish()
         full_qkv.append(weight)
         pre_convs.append(jnp.dot(normed_all, weight, preferred_element_type=F32).astype(LOW))
         made.append(mixer_forward(pre_convs[g], full_conv[g], cols, rows, g * heads, heads))
+        states.append(Chain(made[g][4], made[g][5], "hsij,hsjv->hsiv", 1))
+
+    def head_group(g, kept):
+        _, _, local_part, carried, _, _ = made[g]
+        state = states[g].finish()
+        return heads_forward(
+            local_part, carried, state, gate_out, full_head_gain, g * heads, kept
+        )
 
     normed_all, cols, packed[1] = meet([gathers[0]], normed_all, cols, packed[1])
     gathers.append(ShardGather(packed[1]))
     begin(*gathers)
     mixer_group(0)
-    state_hop(0, 0)
+    begin(states[0])
     normed_all, packed[2], _ = meet([gathers[1]], normed_all, packed[2], made[0][1])
     gathers.append(ShardGather(packed[2]))
     begin(*gathers)
     mixer_group(1)
-    state_hop(0, 1)
-    state_hop(1, 0)
-    normed_all, _ = meet([gathers[2]], normed_all, made[1][1])
+    begin(states[1])
+    normed_all, out_shard, _ = meet([gathers[2], states[0]], normed_all, out_weight, made[1][1])
+    gathers.append(ShardGather(out_shard))
+    begin(gathers[2], states[0], gathers[3])
     mixer_group(2)
-    state_hop(0, 2)
-    state_hop(1, 1)
-    state_hop(2, 0)
-    state_hop(1, 2)
-    state_hop(2, 1)
-    state_hop(2, 2)
-    gate_out = jnp.dot(normed_low, full_gate, preferred_element_type=F32)
+    begin(states[2])
+    normed_gate, _ = meet([states[0], states[1]], normed_low, made[2][1])
+    begin(states[0], states[1])
+    gate_out = jnp.dot(normed_gate, full_gate, preferred_element_type=F32)
+    (gate_out,) = meet([states[0], states[1], states[2], gathers[3]], gate_out)
+    begin(states[1], states[2], gathers[3])
     gate_out = gate_out.reshape(batch, length, VD)
-    heads_low = None
-    for g in range(GROUPS):
-        _, _, local_part, carried, _, _ = made[g]
-        heads_low = heads_forward(
-            local_part, carried, states[g], gate_out, full_head_gain, g * heads, heads_low
-        )
+    heads_low = head_group(0, None)
+    (heads_low,) = meet([states[1], states[2], gathers[3]], heads_low)
+    begin(states[2])
+    heads_low = head_group(1, heads_low)
+    full_out = gathers[3].finish()
+    (heads_low,) = meet([states[2]], heads_low)
+    heads_low = head_group(2, heads_low)
     heads_low = heads_low.reshape(count, VD)
     middle = rows_in + jnp.dot(heads_low, full_out, preferred_element_type=F32)
     normed_ffn, pull_ffn_norm = jax.vjp(rms_norm, middle, full_ffn_gain)
     normed_ffn_low = normed_ffn.astype(LOW)
-    gate_up = jnp.dot(normed_ffn_low, full_ffn_in, preferred_element_type=F32)
-    hidden, pull_swiglu = jax.vjp(swiglu, gate_up)
-    hidden_low = hidden.astype(LOW)
-
     grad_rows = out_cotangent.reshape(count, width)
-    grad_hidden = jnp.einsum("rd,fd->rf", grad_rows, full_down, preferred_element_type=F32)
-    (grad_gate_up,) = pull_swiglu(grad_hidden)
-    grad_gate_up_low = grad_gate_up.astype(LOW)
-    grad_down = jnp.einsum("rf,rd->fd", hidden_low, grad_rows, preferred_element_type=F32)
-    grad_gate_up_low, grad_down = meet([], grad_gate_up_low, grad_down.astype(LOW))
-    r_down = ShardSum(grad_down, True)
+    hidden_low, grad_gate_up_low = ffn_middle(normed_ffn_low, full_ffn_in, grad_rows, full_down)
+    grad_in = jnp.einsum(
+        "rd,rf->df", normed_ffn_low, grad_gate_up_low, preferred_element_type=F32
+    )
+    grad_gate_up_low, grad_in = meet([], grad_gate_up_low, grad_in.astype(LOW))
+    r_in = ShardSum(grad_in, True)
     grad_normed_ffn = jnp.einsum(
         "rf,df->rd", grad_gate_up_low, full_ffn_in, preferred_element_type=F32
     )
     grad_middle_norm, grad_ffn_gain = pull_ffn_norm(grad_normed_ffn)
     grad_middle = grad_rows.astype(F32) + grad_middle_norm
-    grad_branch, grad_gate_up_low = meet([], grad_middle.astype(LOW), grad_gate_up_low)
-    grad_in = jnp.einsum(
-        "rd,rf->df", normed_ffn_low, grad_gate_up_low, preferred_element_type=F32
-    )
+    grad_branch = grad_middle.astype(LOW)
     grad_heads = jnp.einsum("rd,vd->rv", grad_branch, full_out, preferred_element_type=F32)
-    grad_out = jnp.einsum("rv,rd->vd", heads_low, grad_branch, preferred_element_type=F32)
-    grad_heads, grad_in, grad_out, r_down.value, hidden_low = meet(
-        [], grad_heads, grad_in.astype(LOW), grad_out.astype(LOW), r_down.value, hidden_low
-    )
-    r_in = ShardSum(grad_in, True)
-    r_out = ShardSum(grad_out, True)
-    begin(r_down)
     grad_heads = grad_heads.reshape(batch, length, VD)
-    back, grad_gate_low = [], None
-    for g in range(GROUPS):
+    back, grad_states = [], []
+
+    def heads_back(g, grad, kept):
         _, _, local_part, carried, _, _ = made[g]
         back.append(
             heads_backward(
-                local_part, carried, states[g], gate_out, full_head_gain, grad_heads,
-                g * heads, grad_gate_low,
+                local_part, carried, states[g].value, gate_out, full_head_gain, grad,
+                g * heads, kept,
             )
         )
-        grad_gate_low = back[g][1]
-    grad_head_gain = sum(jnp.sum(item[2], axis=(0, 1)) for item in back)
+        grad_states.append(Chain(made[g][4], back[g][3], "hsji,hsjv->hsiv", -1))
+        begin(grad_states[g])
+        return back[g][1]
+
+    kept = heads_back(0, grad_heads, None)
+    grad_heads, kept = meet([], grad_heads, kept)
+    kept = heads_back(1, grad_heads, kept)
+    grad_heads, kept = meet([grad_states[0]], grad_heads, kept)
+    begin(grad_states[0])
+    grad_gate_low = heads_back(2, grad_heads, kept)
+    hidden_late, heads_late, grad_gate_low = meet(
+        [grad_states[0], grad_states[1]], hidden_low, heads_low, grad_gate_low
+    )
+    begin(grad_states[0], grad_states[1])
+    grad_down = jnp.einsum("rf,rd->fd", hidden_late, grad_rows, preferred_element_type=F32)
+    heads_late, grad_down, grad_gate_low = meet(
+        grad_states, heads_late, grad_down.astype(LOW), grad_gate_low
+    )
+    p_down = scatter(grad_down)
+    begin(grad_states[1], grad_states[2])
     grad_gate_low = grad_gate_low.reshape(count, VD)
+    grad_out = jnp.einsum("rv,rd->vd", heads_late, grad_branch, preferred_element_type=F32)
     grad_gate = jnp.einsum("rd,rc->dc", normed_low, grad_gate_low, preferred_element_type=F32)
-    result = middle + jnp.dot(hidden_low, full_down, preferred_element_type=F32)
-    output = result.astype(LOW).reshape(batch, length, width)
-
-    grad_states = [None] * GROUPS
-    for hop in range(hops, 0, -1):
-        for g in range(GROUPS):
-            entering = back[g][3]
-            if hop < hops:
-                entering = entering + jnp.einsum(
-                    "hsji,hsjv->hsiv", made[g][4], grad_states[g], preferred_element_type=F32
-                )
-            came = lax.ppermute(entering.astype(LOW), "seq", [(hop, hop - 1)])
-            grad_states[g] = came if hop == hops else grad_states[g] + came
-    mixed_a, grad_gate, output = meet([r_down], back[0][0], grad_gate.astype(LOW), output)
-    r_gate = ShardSum(grad_gate, True)
-    begin(r_down)
-    mixed_a, grad_states[0] = meet([r_down], mixed_a, grad_states[0])
-
-    def mixer_back(g, grad_mixed):
+    mixed_a, grad_out, grad_gate, r_in.value = meet(
+        [grad_states[1], grad_states[2]],
+        back[0][0], grad_out.astype(LOW), grad_gate.astype(LOW), r_in.value,
+    )
+    p_out = scatter(grad_out)
+    r_gate = ShardSum(grad_gate)
+    begin(grad_states[2], r_gate, r_in)
+
+    run = heads * HEAD
+
+    def mixer_back(g, grad_mixed, place, width, kept):
         t, uw, _, _, _, _ = made[g]
         return mixer_backward(
-            pre_convs[g], full_conv[g], cols, rows, t, uw, states[g], grad_mixed, grad_states[g],
-            g * heads,
+            pre_convs[g], full_conv[g], cols, rows, t, uw, states[g].value, grad_mixed,
+            grad_states[g].finish(), g * heads, place, width, width, kept,
         )
 
-    def with_rim(grad_pre, grad_rim, grad_tail):
-        came = passed_along(grad_rim[:, RIM - margin :, :].astype(LOW), "seq", -1).astype(F32)
-        grad_tail = (grad_tail[:, RIM - margin :, :] + came).astype(LOW)
+    def rim_swap(grad_rim):
+        return passed_along(grad_rim[:, RIM - margin :, :].astype(LOW), "seq", -1)
+
+    def with_rim(grad_pre, came, grad_tail):
+        grad_tail = (grad_tail[:, RIM - margin :, :] + came.astype(F32)).astype(LOW)
         grad_pre = lax.dynamic_update_slice(grad_pre, grad_tail, (0, length - margin, 0))
-        return grad_pre.reshape(count, heads * HEAD)
-
-    def qkv_sum(grad_pre):
-        grad = jnp.einsum("rd,rc->dc", normed_low, grad_pre, preferred_element_type=F32)
-        return ShardSum(grad)
-
-    def normed_part(grad_pre, weight):
-        return jnp.einsum("rc,dc->rd", grad_pre, weight, preferred_element_type=F32)
-
-    begin(r_down)
-    got_a = mixer_back(0, mixed_a)
-    mixed_b, pre_a, rim_a, tail_a, r_in.value = meet(
-        [r_down], back[1][0], got_a[0], got_a[1], got_a[2], r_in.value
-    )
-    begin(r_down, r_in)
-    got_b = mixer_back(1, mixed_b)
-    pre_a = with_rim(pre_a, rim_a, tail_a)
-    mixed_c, pre_a, pre_b, rim_b, tail_b, r_out.value = meet(
-        [r_down, r_in], back[2][0], pre_a, got_b[0], got_b[1], got_b[2], r_out.value
-    )
-    sum_a = qkv_sum(pre_a)
-    begin(r_in, sum_a, r_out)
-    got_c = mixer_back(2, mixed_c)
-    pre_b = with_rim(pre_b, rim_b, tail_b)
-    pre_b, pre_c, rim_c, tail_c, grad_gate_low = meet(
-        [r_in, sum_a, r_out], pre_b, got_c[0], got_c[1], got_c[2], grad_gate_low
-    )
-    begin(r_in, sum_a, r_out)
-    sum_b = qkv_sum(pre_b)
-    pre_c = with_rim(pre_c, rim_c, tail_c)
-    pre_c, sum_b.value, grad_gate_low = meet([], pre_c, sum_b.value, grad_gate_low)
-    sum_c = qkv_sum(pre_c)
-    begin(sum_b, sum_c)
-    grad_normed = normed_part(pre_a, full_qkv[0]) + normed_part(pre_b, full_qkv[1])
-    pre_c, grad_normed = meet([r_in, sum_a, r_out, sum_b, sum_c], pre_c, grad_normed)
-    begin(r_in, sum_a, r_out, sum_b, sum_c)
+        return grad_pre.reshape(count, grad_pre.shape[2])
+
+    def weight_grad(grad):
+        return jnp.einsum("rd,rc->dc", normed_low, grad, preferred_element_type=F32).astype(LOW)
+
+    def normed_part(grad, weight):
+        return jnp.einsum("rc,dc->rd", grad, weight, preferred_element_type=F32)
+
+    got_a = mixer_back(0, mixed_a, 0, 2 * run, [])
+    mixed_b, *kept = meet([grad_states[2], r_gate, r_in], back[1][0], *got_a[:3])
+    begin(r_gate, r_in)
+    got_b = mixer_back(1, mixed_b, 1, 2 * run, kept)
+    mixed_c, pre_ab, rim_ab, tail_ab, grad_gate_low = meet(
+        [r_gate], back[2][0], *got_b[:3], grad_gate_low
+    )
+    begin(r_gate)
+    came_ab = rim_swap(rim_ab)
+    grad_normed = normed_part(grad_gate_low, full_gate)
+    pre_ab, came_ab, tail_ab, grad_normed = meet([], pre_ab, came_ab, tail_ab, grad_normed)
+    pre_ab = with_rim(pre_ab, came_ab, tail_ab)
+    grad_ab = weight_grad(pre_ab)
+    mixed_c, grad_ab = meet([r_in, r_gate], mixed_c, grad_ab)
+    sum_ab = ShardSum(grad_ab)
+    begin(sum_ab, r_in, r_gate)
+    got_c = mixer_back(2, mixed_c, 0, run, [])
+    pre_c, rim_c, tail_c, pre_ab, grad_normed = meet(
+        [sum_ab, r_in, r_gate], *got_c[:3], pre_ab, grad_normed
+    )
+    begin(sum_ab, r_in, r_gate)
+    came_c = rim_swap(rim_c)
+    grad_normed = grad_normed + normed_part(pre_ab[:, :run], full_qkv[0])
+    pre_c, came_c, tail_c, grad_normed = meet([], pre_c, came_c, tail_c, grad_normed)
+    pre_c = with_rim(pre_c, came_c, tail_c)
+    grad_c = weight_grad(pre_c)
+    grad_c, grad_normed, p_down, p_out = meet([r_gate], grad_c, grad_normed, p_down, p_out)
+    sum_c = ShardSum(grad_c)
+    r_late = ShardSum(jnp.concatenate([p_down, p_out], axis=0), ready=True)
+    begin(sum_c, r_late, r_gate)
+    grad_normed = grad_normed + normed_part(pre_ab[:, run:], full_qkv[1])
+    grad_normed, pre_c = meet([sum_ab, sum_c, r_late, r_gate, r_in], grad_normed, pre_c)
+    begin(sum_ab, sum_c, r_late, r_gate)
     grad_normed = grad_normed + normed_part(pre_c, full_qkv[2])
-    grad_cols = jnp.concatenate([got_a[4], got_b[4], got_c[4]], axis=0)
-    conv_parts = [got_a[3], got_b[3], got_c[3]]
+    made_late = [item for got in (got_a, got_b, got_c) for item in got[3:5]]
+    hidden_late, grad_normed, *made_late = meet(
+        [sum_ab, sum_c, r_late, r_gate], hidden_late, grad_normed, *made_late, *[item[2] for item in back]
+    )
+    made_late, head_gains = made_late[: 2 * GROUPS], made_late[2 * GROUPS :]
+    grad_head_gain = sum(jnp.sum(item, axis=(0, 1)) for item in head_gains)
+    begin(sum_ab, sum_c, r_late)
+    result = middle + jnp.dot(hidden_late, full_down, preferred_element_type=F32)
+    output = result.astype(LOW).reshape(batch, length, width)
+    grad_cols = jnp.concatenate(made_late[1::2], axis=0)
+    conv_parts = made_late[::2]
     spans = [0, heads * DK, 2 * heads * DK, heads * HEAD]
     grad_conv = jnp.concatenate(
         [part[:, low:top] for low, top in zip(spans, spans[1:]) for part in conv_parts], axis=1
@@ -966,9 +1102,6 @@
     grad_decay_low = grad_decay_low.reshape(count, 2 * H)
     grad_decay = jnp.einsum("rd,rc->dc", normed_low, grad_decay_low, preferred_element_type=F32)
     grad_normed = grad_normed + jnp.einsum(
-        "rc,dc->rd", grad_gate_low, full_gate, preferred_element_type=F32
-    )
-    grad_normed = grad_normed + jnp.einsum(
         "rc,dc->rd", grad_decay_low, full_decay, preferred_element_type=F32
     )
     grad_rows_norm, grad_mixer_gain = pull_mixer_norm(grad_normed)
@@ -984,15 +1117,18 @@
         grad_decay_bias,
     )
     small_grads = jnp.concatenate(little)
-    movers = [r_down, r_in, sum_a, sum_b, r_out, sum_c, r_gate]
-    small_grads, r_gate.value = meet(movers, small_grads, r_gate.value)
+    movers = [r_in, r_gate, sum_ab, sum_c, r_late]
+    (small_grads,) = meet(movers, small_grads)
     all_sum = AllSum(small_grads)
     movers.append(all_sum)
     while any(mover.todo for mover in movers):
         begin(*movers)
         meet(movers, small_grads)
     flat = all_sum.value
-    sum_qkv = unpack_groups([sum_a.value, sum_b.value, sum_c.value])
+    sum_qkv = unpack_groups(sum_ab.value, sum_c.value)
+    late = r_late.value.reshape(-1, p_down.shape[0] + p_out.shape[0], width)
+    sum_down = late[:, : p_down.shape[0]].reshape(-1, width)
+    sum_out = late[:, p_down.shape[0] :].reshape(-1, width)
     parts, first = [], 0
     for item in little:
         parts.append(flat[first : first + item.size])
@@ -1014,10 +1150,10 @@
         parts[5],
         parts[6],
         own(parts[2]),
-        r_out.value.astype(F32),
+        sum_out.astype(F32),
         own(parts[1]),
         r_in.value.astype(F32),
-        r_down.value.astype(F32),
+        sum_down.astype(F32),
     )
 
 

time: 707 us -> 618 us (0.87)
  matrix products: 170 us -> 120 us
  waiting for transfers between devices: 135 us -> 88.2 us
  Pallas kernels: 130 us -> 158 us
  blocking collectives: 16 us -> 0 us
  other arithmetic: 78.4 us -> 70.4 us
  local copies, waits for them, and re-layouts: 51.2 us -> 59.1 us
    dot_general x25 -> x22, matrix products: 105 us -> 59.9 us  [the longest x12 12.6 us: leave(): jnp.einsum(spec, through, self.value, preferred_element_type=F32)]
    pallas_call x3 -> x4, Pallas kernels: 59.3 us -> 86.2 us  [the longest x3 61.4 us: mixer_backward(): pl.pallas_call(kernel, grid=(heads,), in_specs=head_specs(seqs, count, fi...]
    ppermute x18, waiting for transfers between devices: 26.6 us -> 7.07 us  [leave(): return lax.ppermute(leaving.astype(LOW), 'seq', [(hop, hop + step)])]
    unnamed x1 -> x0, blocking collectives: 16 us -> none
    all_gather x3 -> x2, waiting for transfers between devices: 20.4 us -> 6.24 us  [gather_halves(): return lax.all_gather(part, ('fsdp', 'dp'), axis=0, tiled=True)]
    reduce_scatter x4 -> x1, waiting for transfers between devices: 12.6 us -> 0.01 us  [__init__(): lax.psum_scatter(self.value, ('fsdp', 'dp'), scatter_dimension=0, tiled=T...]
    convert_element_type x13 -> x11, other arithmetic: 16 us -> 6.74 us  [the longest x1 2.03 us: local(): sum_down.astype(F32)]
    add x13 -> x17, other arithmetic: 11.7 us -> 19 us  [the longest x12 11.6 us: take(): return came if self.value is None else self.value + came]
  transfers between devices with their start and end apart: 82 -> 77, of which waited for: 21 -> 18; matrix products, arithmetic and copies ran while one was open for 33% -> 32% of each run, Pallas kernels for 18% -> 22%
where the time goes in v3:
time: 618 us; the launch traced here: 613 us
  Pallas kernels  158 us (26%)
  matrix products  120 us (19%)
  starting transfers between devices  100 us (16%)
  waiting for transfers between devices  88.2 us (14%)
  other arithmetic  70.4 us (11%)
  local copies, waits for them, and re-layouts  59.1 us (10%)
  between operations  17 us (3%)
    ppermute x49, waiting for transfers between devices, swap(): return lax.ppermute(values, axis, [(at, at ^ bit) for at in range(count)])  73.2 us
    pallas_call x3, Pallas kernels, mixer_backward(): pl.pallas_call(kernel, grid=(heads,), in_specs=head_specs(seqs, count, fi...  61.4 us
    ppermute x49, starting transfers between devices, swap(): return lax.ppermute(values, axis, [(at, at ^ bit) for at in range(count)])  60.6 us
    pallas_call x3, Pallas kernels, mixer_forward(): pl.pallas_call(forward_kernel, grid=(heads,), in_specs=head_specs(seqs, c...  38.9 us
    unnamed x311, local copies, waits for them, and re-layouts  30.7 us
    ppermute x18, starting transfers between devices, leave(): return lax.ppermute(leaving.astype(LOW), 'seq', [(hop, hop + step)])  29.2 us
    pallas_call x1, Pallas kernels, ffn_middle(): pl.pallas_call(ffn_kernel, grid=(tiles,), in_specs=[pl.BlockSpec((rows, w...  24.8 us
    convert_element_type x19, other arithmetic, plus(): return (left.astype(F32) + right.astype(F32)).astype(LOW)  18.2 us
  transfers between devices with their start and end apart: 77, of which 18 were waited for; matrix products, arithmetic and copies ran while one was open for 32% of the time, Pallas kernels for 22%

profile of v3, /device:TPU:0, one launch (start us, length us, event | category | flops | bytes accessed | tf_op | source)
XLA Modules:
  0.0 613.1 jit_solution(2716352413936370066)
XLA Ops:
  15.2 3.7 collective-permute-start.4
  25.5 3.5 collective-permute-start.3
  40.3 5.1 collective-permute-done.5.refs_2_
  55.5 12.9 %mixer_forward.3 = (bf16[2,3,256,256]{3,2,1,0:T(8,128)(2,1)S(1)}, bf16[2,3,256,384]{3,2,1,0:T(8,128)(2,1)S(1)}, f32[3,256,512]{2,1,0:T(8,128)S(1)}, bf16[3,256,2...) custom-call(bf16[784,1024]{1,0:T(8,128)(2,1)} %convolution_convert_fusion.5.q_ref.k_ref.v_, ...), custom_call_target="tpu_custom_call" | custom-call | tf_op jit(solution)/shard_map/mixer_forward/pallas_call | solution.py:324
  72.2 3.7 collective-permute-start.12
  81.7 13.2 %mixer_forward.4 = (bf16[2,3,256,256]{3,2,1,0:T(8,128)(2,1)S(1)}, bf16[2,3,256,384]{3,2,1,0:T(8,128)(2,1)S(1)}, f32[3,256,512]{2,1,0:T(8,128)S(1)}, bf16[3,256,2...) custom-call(bf16[784,1024]{1,0:T(8,128)(2,1)} %convolution_convert_fusion.4.q_ref.k_ref.v_, ...), custom_call_target="tpu_custom_call" | custom-call | tf_op jit(solution)/shard_map/mixer_forward/pallas_call | solution.py:324
  97.4 4.2 collective-permute-start.16
  107.7 12.9 %mixer_forward.5 = (bf16[2,3,256,256]{3,2,1,0:T(8,128)(2,1)S(1)}, bf16[2,3,256,384]{3,2,1,0:T(8,128)(2,1)S(1)}, f32[3,256,512]{2,1,0:T(8,128)S(1)}, bf16[3,256,2...) custom-call(bf16[784,1024]{1,0:T(8,128)(2,1)} %convolution_convert_fusion.3.q_ref.k_ref.v_, ...), custom_call_target="tpu_custom_call" | custom-call | tf_op jit(solution)/shard_map/mixer_forward/pallas_call | solution.py:324
  128.8 7.1 %fusion.83 = f32[768,1536]{1,0:T(8,128)} fusion(bf16[768,1024]{1,0:T(8,128)(2,1)} %fusion.7, bf16[1024,1536]{1,0:T(8,128)(2,1)} %all-gather.6.cloned.1.call-done), kind=kOutput, calls=%fused_computation.225 | convolution fusion | flops 2415919104 | bytes 9437184 | tf_op jit(solution)/shard_map/dot_general | solution.py:953
  156.6 4.1 assemble.7
  169.8 6.2 %all-gather.8.cloned.1.call-done = bf16[1,1024,5632]{2,1,0:T(8,128)(2,1)} async-done(((bf16[1,128,5632]{2,1,0:T(8,128)(2,1)}), bf16[1,1024,5632]{2,1,0:T(8,128)(2,1)}) %all-gather.8.cloned.1.call-update) | async-done | bytes 11534352 | tf_op jit(solution)/shard_map/all_gather | solution.py:781
  178.9 24.8 %ffn_middle.1 = (bf16[768,2816]{1,0:T(8,128)(2,1)}, bf16[768,5632]{1,0:T(8,128)(2,1)}) custom-call(bf16[768,1024]{1,0:T(8,128)(2,1)S(1)} %copy-done.10, bf16[1024,5632]{1,0:T(8,128)(2,1)} %bitcast.293, bf16[1024,5632]{1,0:T(8,128)(2,1)} %bitcast.294, bf16[768,1024]{1,0:T(8,128)(2,1)S(1)} %bitcast.282, bf16[2816,1024]{1,0:T(8,128)(2,1)} %bitcast.299), custom_call_target="tpu_custom_call" | custom-call | tf_op jit(solution)/shard_map/ffn_middle/pallas_call | solution.py:507
  203.7 15.4 %convolution_convert_fusion = bf16[1024,5632]{1,0:T(8,128)(2,1)} fusion(bf16[768,1024]{1,0:T(8,128)(2,1)S(1)} %copy-done.10, bf16[768,5632]{1,0:T(8,128)(2,1)} %get-tuple-element.235), kind=kOutput, calls=%fused_computation | convolution fusion | flops 8864137216 | bytes 21757952 | tf_op jit(solution)/shard_map/rd,rf->df/dot_general | solution.py:970
  219.4 17.1 %multiply_reduce_fusion = (f32[1024]{0:T(1024)}, f32[768]{0:T(1024)S(1)}, f32[768,1024]{1,0:T(8,128)}) fusion(f32[768,1024]{1,0:T(8,128)} %copy-done.69, f32[768]{0:T(1024)S(1)} %fusion.68, f32[1024]{0:T(1024)S(1)} %bitcast.367, bf16[768,5632]{1,0:T(8,128)(2,1)} %get-tuple-element.235, bf16[1,1024,5632]{2,1,0:T(8,128)(2,1)} %all-gather.8.cloned.1.call-done), kind=kOutput, calls=%fused_computation.29 | convolution fusion | flops 8863086592 | bytes 26490880 | tf_op jit(solution)/shard_map/rf,df->rd/dot_general | solution.py:975
  239.8 4.4 fusion.38
  244.2 5.3 heads_backward.3
  250.5 5.2 heads_backward.4
  258.5 5.4 heads_backward.5
  271.5 8.7 %convolution_convert_fusion.1 = bf16[2816,1024]{1,0:T(8,128)(2,1)} fusion(bf16[768,2816]{1,0:T(8,128)(2,1)} %get-tuple-element.333, bf16[768,1024]{1,0:T(8,128)(2,1)S(1)} %bitcast.283), kind=kOutput, calls=%fused_computation.3 | convolution fusion | flops 4432068608 | bytes 11665408 | tf_op jit(solution)/shard_map/rf,rd->fd/dot_general | solution.py:1007
  280.3 6.7 %collective-permute-done.29 = bf16[2,3,128,256]{3,2,1,0:T(8,128)(2,1)} collective-permute-done((bf16[2,3,128,256]{3,2,1,0:T(8,128)(2,1)}, bf16[2,3,128,256]{3,2,1,0:T(8,128)(2,1)}, u32[]{:S(2)}, u32[]{:S(2)}) %collective-permute-start.29) | collective-permute-done | bytes 393248 | tf_op jit(solution)/shard_map/ppermute | solution.py:717
  296.6 4.1 convolution_convert_fusion.2
  300.7 6.7 %bitcast_convert_fusion.1 = bf16[1024,1536]{1,0:T(8,128)(2,1)} fusion(bf16[3,256,1536]{2,1,0:T(8,128)(2,1)} %get-tuple-element.259, bf16[3,256,1024]{2,1,0:T(8,128)(2,1)} %param.15, f32[1024]{0:T(1024)S(1)} %bitcast.359, f32[3,256]{1,0:T(4,128)} %copy-done.128), kind=kOutput, calls=%fused_computation.2 | convolution fusion | flops 2420637696 | bytes 7085056 | tf_op jit(solution)/shard_map/rd,rc->dc/dot_general | solution.py:1015
  311.1 6.0 collective-permute-start.36
  327.9 20.8 %mixer_backward.3 = (bf16[3,256,2048]{2,1,0:T(8,128)(2,1)}, f32[3,8,2048]{2,1,0:T(8,128)S(1)}, f32[3,8,2048]{2,1,0:T(8,128)S(1)}, f32[4,1024]{1,0:T(4,128)S(1)}, f32[2,3,8,256]{3,2,1,0:T(8,128)S(1)}) custom-call(bf16[784,1024]{1,0:T(8,128)(2,1)S(1)} %copy-done.3, bf16[784,1024]{1,0:T(8,128)(2,1)S(1)} %copy-done.3, bf16[784,1024]{1,0:T(8,128)(2,1)S(1)} %copy-done.3, ...), custom_call_target="tpu_custom_call" | custom-call | tf_op jit(solution)/shard_map/mixer_backward/pallas_call | solution.py:442
  356.3 20.9 %mixer_backward.4 = (bf16[3,256,2048]{2,1,0:T(8,128)(2,1)}, f32[3,8,2048]{2,1,0:T(8,128)S(1)}, f32[3,8,2048]{2,1,0:T(8,128)S(1)}, f32[4,1024]{1,0:T(4,128)S(1)}, f32[2,3,8,256]{3,2,1,0:T(8,128)S(1)}) custom-call(bf16[784,1024]{1,0:T(8,128)(2,1)S(1)} %copy-done.2, ...), custom_call_target="tpu_custom_call", output_to_operand_aliasing={{0}: (16, {}), {1}: (17, {}), {2}: (18, {})} | custom-call | tf_op jit(solution)/shard_map/mixer_backward/pallas_call | solution.py:442
  382.1 6.3 %fusion.84 = f32[768,1024]{1,0:T(8,128)} fusion(bf16[768,1536]{1,0:T(8,128)(2,1)S(1)} %bitcast.298, bf16[1024,1536]{1,0:T(8,128)(2,1)} %all-gather.6.cloned.1.call-done), kind=kOutput, calls=%fused_computation.226 | convolution fusion | flops 2415919104 | bytes 8650752 | tf_op jit(solution)/shard_map/rc,dc->rd/dot_general | solution.py:1045
  391.4 6.2 %bitcast_convert_fusion = bf16[1024,2048]{1,0:T(8,128)(2,1)S(1)} fusion(bf16[3,256,2048]{2,1,0:T(8,128)(2,1)} %dynamic_update_slice.22, bf16[3,256,1024]{2,1,0:T(8,128)(2,1)S(1)} %copy-done.66, f32[1024]{0:T(1024)S(1)} %bitcast.360, f32[3,256]{1,0:T(4,128)S(1)} %copy-done.129), kind=kOutput, calls=%fused_computation.1 | convolution fusion | flops 3226468352 | bytes 8920064 | tf_op jit(solution)/shard_map/rd,rc->dc/dot_general | solution.py:1042
  399.3 3.5 add_convert_fusion.1
  409.0 19.6 %mixer_backward.5 = (bf16[3,256,1024]{2,1,0:T(8,128)(2,1)S(1)}, f32[3,8,1024]{2,1,0:T(8,128)S(1)}, f32[3,8,1024]{2,1,0:T(8,128)S(1)}, f32[4,1024]{1,0:T(4,128)S(1)}, f32[2,3,8,256]{3,2,1,0:T(8,128)S(1)}) custom-call(bf16[784,1024]{1,0:T(8,128)(2,1)} %convolution_convert_fusion.3.q_ref.k_ref.v_ref.rq_ref.rk_ref.rv_ref.refs_0_.refs_1_.refs_2_.refs_3_.refs_4_.refs_5_, ...), custom_call_target="tpu_custom_call" | custom-call | tf_op jit(solution)/shard_map/mixer_backward/pallas_call | solution.py:442
  431.8 4.1 collective-permute-start.45
  442.4 3.2 maximum_select_fusion.2
  449.1 3.4 bitcast_convert_fusion.2
  461.4 13.3 %collective-permute-done.49 = bf16[64,1536]{1,0:T(8,128)(2,1)S(1)} collective-permute-done((bf16[64,1536]{1,0:T(8,128)(2,1)S(1)}, bf16[64,1536]{1,0:T(8,128)(2,1)S(1)}, u32[]{:S(2)}, u32[]{:S(2)}) %collective-permute-start.49) | collective-permute-done | bytes 196640 | tf_op jit(solution)/shard_map/ppermute | solution.py:583
  474.8 3.2 collective-permute-done.50
  484.3 3.3 maximum_select_fusion
  487.7 3.8 bitcast_convert_fusion.3
  494.3 5.2 collective-permute-done.54
  499.5 7.5 %collective-permute-done.53 = bf16[272,1024]{1,0:T(8,128)(2,1)S(1)} collective-permute-done((bf16[272,1024]{1,0:T(8,128)(2,1)S(1)}, bf16[272,1024]{1,0:T(8,128)(2,1)S(1)}, u32[]{:S(2)}, u32[]{:S(2)}) %collective-permute-start.53) | collective-permute-done | bytes 557088 | tf_op jit(solution)/shard_map/ppermute | solution.py:583
  521.7 5.9 add_convert_fusion
  529.7 4.6 collective-permute-done.57
  543.7 3.6 collective-permute-done.59
  547.2 3.5 collective-permute-done.58
  550.7 9.7 %collective-permute-done.60 = bf16[544,1024]{1,0:T(8,128)(2,1)S(1)} collective-permute-done((bf16[544,1024]{1,0:T(8,128)(2,1)S(1)}, bf16[544,1024]{1,0:T(8,128)(2,1)S(1)}, u32[]{:S(2)}, u32[]{:S(2)}) %collective-permute-start.60) | collective-permute-done | bytes 1114144 | tf_op jit(solution)/shard_map/ppermute | solution.py:583
  561.2 3.7 collective-permute-start.63
  566.1 3.5 collective-permute-done.64
  570.9 3.4 collective-permute-start.66
  577.3 6.8 %collective-permute-done.67 = f32[26892]{0:T(1024)S(1)} collective-permute-done((f32[26892]{0:T(1024)S(1)}, f32[26892]{0:T(1024)S(1)}, u32[]{:S(2)}, u32[]{:S(2)}) %collective-permute-start.67) | collective-permute-done | bytes 107600 | tf_op jit(solution)/shard_map/ppermute | solution.py:583
  586.8 3.4 collective-permute-start.69
  (643 shorter events, 237.3 us)
Async XLA Ops:
  7.2 121.6 %all-gather.6.cloned.1.call-start = ((), (), s32[]{:S(2)}) async-start(), calls=%async_computation.3 | async-start | bytes 3932160 | tf_op jit(solution)/shard_map/all_gather | solution.py:899
  7.9 161.9 %all-gather.10.cloned.1.call-start = ((), (), s32[]{:S(2)}) async-start(), calls=%async_computation.8 | async-start | bytes 6488064 | tf_op jit(solution)/shard_map/all_gather | solution.py:781
  10.2 165.9 %all-gather.8.cloned.1.call-start = ((), (), s32[]{:S(2)}) async-start(), calls=%async_computation.7 | async-start | bytes 12976128 | tf_op jit(solution)/shard_map/all_gather | solution.py:781
  11.5 295.9 %reduce-scatter.4.cloned.1.call-start = ((), (), s32[]{:S(2)}) async-start(), calls=%async_computation.4 | async-start | bytes 12976128 | tf_op jit(solution)/shard_map/reduce_scatter | solution.py:656
  12.5 16.8 %collective-permute-start.1 = (bf16[6720]{0:T(1024)(128)(2,1)S(1)}, bf16[6720]{0:T(1024)(128)(2,1)S(1)}, u32[]{:S(2)}, u32[]{:S(2)}) collective-permute-start(bf16[6720]{0:T(1024)(128)(2,1)S(1)} %concatenate.39), channel_id=1, source_target_pairs={{0,8},{4,12},{8,0},{12,4},{1,9},{5,13},{9,1},{13,5},{2,10},{6,14},... | collective-permute-start | bytes 40328 | tf_op jit(solution)/shard_map/ppermute | solution.py:583
  15.1 14.5 %collective-permute-start.2 = (bf16[6720]{0:T(1024)(128)(2,1)S(1)}, bf16[6720]{0:T(1024)(128)(2,1)S(1)}, u32[]{:S(2)}, u32[]{:S(2)}) collective-permute-start(bf16[6720]{0:T(1024)(128)(2,1)S(1)} %concatenate.39), channel_id=1, source_target_pairs={{0,12},{4,8},{8,4},{12,0},{1,13},{5,9},{9,5},{13,1},{2,14},{6,10},... | collective-permute-start | bytes 40328 | tf_op jit(solution)/shard_map/ppermute | solution.py:583
  19.8 25.6 %collective-permute-start.5 = (bf16[256,1024]{1,0:T(8,128)(2,1)}, bf16[256,1024]{1,0:T(8,128)(2,1)S(1)}, u32[]{:S(2)}, u32[]{:S(2)}) collective-permute-start(bf16[256,1024]{1,0:T(8,128)(2,1)} %get-tuple-element.191.refs_0_), channel_id=1, source_target_pairs={{0,8},{4,12},{8,0},{12,4},{1,9},{5,13},{9,1},{13,5},{2,10},{6,14},... | collective-permute-start | bytes 1572872 | tf_op jit(solution)/shard_map/ppermute | solution.py:583
  25.1 24.6 %collective-permute-start.6 = (bf16[256,1024]{1,0:T(8,128)(2,1)}, bf16[256,1024]{1,0:T(8,128)(2,1)S(1)}, u32[]{:S(2)}, u32[]{:S(2)}) collective-permute-start(bf16[256,1024]{1,0:T(8,128)(2,1)} %get-tuple-element.191.refs_0_), channel_id=1, source_target_pairs={{0,4},{4,0},{8,12},{12,8},{1,5},{5,1},{9,13},{13,9},{2,6},{6,2},{1... | collective-permute-start | bytes 1572872 | tf_op jit(solution)/shard_map/ppermute | solution.py:583
  45.5 26.0 %collective-permute-start.8 = (bf16[256,1024]{1,0:T(8,128)(2,1)S(1)}, bf16[256,1024]{1,0:T(8,128)(2,1)}, u32[]{:S(2)}, u32[]{:S(2)}) collective-permute-start(bf16[256,1024]{1,0:T(8,128)(2,1)S(1)} %get-tuple-element.197.refs_0_), channel_id=1, source_target_pairs={{0,8},{4,12},{8,0},{12,4},{1,9},{5,13},{9,1},{13,5},{2,10},{6,14},... | collective-permute-start | bytes 1572872 | tf_op jit(solution)/shard_map/ppermute | solution.py:583
  47.4 28.5 %collective-permute-start.9 = (bf16[256,1024]{1,0:T(8,128)(2,1)S(1)}, bf16[256,1024]{1,0:T(8,128)(2,1)}, u32[]{:S(2)}, u32[]{:S(2)}) collective-permute-start(bf16[256,1024]{1,0:T(8,128)(2,1)S(1)} %get-tuple-element.197.refs_0_), channel_id=1, source_target_pairs={{0,4},{4,0},{8,12},{12,8},{1,5},{5,1},{9,13},{13,9},{2,6},{6,2},{1... | collective-permute-start | bytes 1572872 | tf_op jit(solution)/shard_map/ppermute | solution.py:583
  71.8 24.3 %collective-permute-start.11 = (bf16[256,1024]{1,0:T(8,128)(2,1)S(1)}, bf16[256,1024]{1,0:T(8,128)(2,1)S(1)}, u32[]{:S(2)}, u32[]{:S(2)}) collective-permute-start(bf16[256,1024]{1,0:T(8,128)(2,1)S(1)} %get-tuple-element.201.refs_0_), channel_id=1, source_target_pairs={{0,8},{4,12},{8,0},{12,4},{1,9},{5,13},{9,1},{13,5},{2,10},{6,14},... | collective-permute-start | bytes 1572872 | tf_op jit(solution)/shard_map/ppermute | solution.py:583
  72.0 31.0 %collective-permute-start.13 = (bf16[256,1024]{1,0:T(8,128)(2,1)S(1)}, bf16[256,1024]{1,0:T(8,128)(2,1)S(1)}, u32[]{:S(2)}, u32[]{:S(2)}) collective-permute-start(bf16[256,1024]{1,0:T(8,128)(2,1)S(1)} %get-tuple-element.201.refs_0_), channel_id=1, source_target_pairs={{0,4},{4,0},{8,12},{12,8},{1,5},{5,1},{9,13},{13,9},{2,6},{6,2},{1... | collective-permute-start | bytes 1572872 | tf_op jit(solution)/shard_map/ppermute | solution.py:583
  72.2 23.9 %collective-permute-start.12 = (bf16[2,3,128,256]{3,2,1,0:T(8,128)(2,1)S(1)}, bf16[2,3,128,256]{3,2,1,0:T(8,128)(2,1)S(1)}, u32[]{:S(2)}, u32[]{:S(2)}) collective-permute-start(bf16[2,3,128,256]{3,2,1,0:T(8,128)(2,1)S(1)} %convert_element_type.446), channel_id=1, source_target_pairs={{0,1},{4,5},{8,9},{12,13},{16,17},{20,21},{24,25},{28,29}} | collective-permute-start | bytes 1179656 | tf_op jit(solution)/shard_map/ppermute | solution.py:717
  96.6 24.1 %collective-permute-start.15 = (bf16[2,3,128,256]{3,2,1,0:T(8,128)(2,1)S(1)}, bf16[2,3,128,256]{3,2,1,0:T(8,128)(2,1)S(1)}, u32[]{:S(2)}, u32[]{:S(2)}) collective-permute-start(bf16[2,3,128,256]{3,2,1,0:T(8,128)(2,1)S(1)} %fusion.21), channel_id=1, source_target_pairs={{1,2},{5,6},{9,10},{13,14},{17,18},{21,22},{25,26},{29,30}} | collective-permute-start | bytes 1179656 | tf_op jit(solution)/shard_map/ppermute | solution.py:717
  97.4 23.3 %collective-permute-start.16 = (bf16[2,3,128,256]{3,2,1,0:T(8,128)(2,1)S(1)}, bf16[2,3,128,256]{3,2,1,0:T(8,128)(2,1)S(1)}, u32[]{:S(2)}, u32[]{:S(2)}) collective-permute-start(bf16[2,3,128,256]{3,2,1,0:T(8,128)(2,1)S(1)} %convert_element_type.449), channel_id=1, source_target_pairs={{0,1},{4,5},{8,9},{12,13},{16,17},{20,21},{24,25},{28,29}} | collective-permute-start | bytes 1179656 | tf_op jit(solution)/shard_map/ppermute | solution.py:717
  101.6 34.4 %collective-permute-start.20 = (bf16[384,1024]{1,0:T(8,128)(2,1)}, bf16[384,1024]{1,0:T(8,128)(2,1)}, u32[]{:S(2)}, u32[]{:S(2)}) collective-permute-start(bf16[384,1024]{1,0:T(8,128)(2,1)} %refs_0_), channel_id=1, source_target_pairs={{0,8},{4,12},{8,0},{12,4},{1,9},{5,13},{9,1},{13,5},{2,10},{6,14},... | collective-permute-start | bytes 2359304 | tf_op jit(solution)/shard_map/ppermute | solution.py:583
  121.1 14.9 %collective-permute-start.17 = (bf16[2,3,128,256]{3,2,1,0:T(8,128)(2,1)S(1)}, bf16[2,3,128,256]{3,2,1,0:T(8,128)(2,1)}, u32[]{:S(2)}, u32[]{:S(2)}) collective-permute-start(bf16[2,3,128,256]{3,2,1,0:T(8,128)(2,1)S(1)} %fusion.22), channel_id=1, source_target_pairs={{2,3},{6,7},{10,11},{14,15},{18,19},{22,23},{26,27},{30,31}} | collective-permute-start | bytes 1179656 | tf_op jit(solution)/shard_map/ppermute | solution.py:717
  219.1 233.3 %reduce-scatter.6.cloned.1.call-start = ((), (), s32[]{:S(2)}) async-start(), calls=%async_computation.5 | async-start | bytes 6488064 | tf_op jit(solution)/shard_map/reduce_scatter | solution.py:639
  264.7 15.5 %collective-permute-start.31 = (bf16[2,3,128,256]{3,2,1,0:T(8,128)(2,1)}, bf16[2,3,128,256]{3,2,1,0:T(8,128)(2,1)}, u32[]{:S(2)}, u32[]{:S(2)}) collective-permute-start(bf16[2,3,128,256]{3,2,1,0:T(8,128)(2,1)} %convert_element_type.470), channel_id=1, source_target_pairs={{3,2},{7,6},{11,10},{15,14},{19,18},{23,22},{27,26},{31,30}} | collective-permute-start | bytes 1179656 | tf_op jit(solution)/shard_map/ppermute | solution.py:717
  267.3 19.6 %collective-permute-start.29 = (bf16[2,3,128,256]{3,2,1,0:T(8,128)(2,1)}, bf16[2,3,128,256]{3,2,1,0:T(8,128)(2,1)}, u32[]{:S(2)}, u32[]{:S(2)}) collective-permute-start(bf16[2,3,128,256]{3,2,1,0:T(8,128)(2,1)} %fusion.28), channel_id=1, source_target_pairs={{1,0},{5,4},{9,8},{13,12},{17,16},{21,20},{25,24},{29,28}} | collective-permute-start | bytes 1179656 | tf_op jit(solution)/shard_map/ppermute | solution.py:717
  269.7 17.2 %collective-permute-start.30 = (bf16[2,3,128,256]{3,2,1,0:T(8,128)(2,1)}, bf16[2,3,128,256]{3,2,1,0:T(8,128)(2,1)}, u32[]{:S(2)}, u32[]{:S(2)}) collective-permute-start(bf16[2,3,128,256]{3,2,1,0:T(8,128)(2,1)} %fusion.29), channel_id=1, source_target_pairs={{2,1},{6,5},{10,9},{14,13},{18,17},{22,21},{26,25},{30,29}} | collective-permute-start | bytes 1179656 | tf_op jit(solution)/shard_map/ppermute | solution.py:717
  286.9 165.5 %reduce-scatter.8.cloned.1.call-start = ((), (), s32[]{:S(2)}) async-start(), calls=%async_computation.6 | async-start | bytes 3538944 | tf_op jit(solution)/shard_map/reduce_scatter | solution.py:639
  291.7 15.7 %collective-permute-start.32 = (bf16[2,3,128,256]{3,2,1,0:T(8,128)(2,1)}, bf16[2,3,128,256]{3,2,1,0:T(8,128)(2,1)}, u32[]{:S(2)}, u32[]{:S(2)}) collective-permute-start(bf16[2,3,128,256]{3,2,1,0:T(8,128)(2,1)} %fusion.30), channel_id=1, source_target_pairs={{1,0},{5,4},{9,8},{13,12},{17,16},{21,20},{25,24},{29,28}} | collective-permute-start | bytes 1179656 | tf_op jit(solution)/shard_map/ppermute | solution.py:717
  310.2 38.5 %collective-permute-start.35 = (bf16[2,256,1536]{2,1,0:T(8,128)(2,1)}, bf16[2,256,1536]{2,1,0:T(8,128)(2,1)}, u32[]{:S(2)}, u32[]{:S(2)}) collective-permute-start(bf16[2,256,1536]{2,1,0:T(8,128)(2,1)} %dynamic-slice_bitcast_fusion.1), channel_id=1, source_target_pairs={{0,4},{4,0},{8,12},{12,8},{1,5},{5,1},{9,13},{13,9},{2,6},{6,2},{1... | collective-permute-start | bytes 4718600 | tf_op jit(solution)/shard_map/ppermute | solution.py:583
  311.1 37.6 %collective-permute-start.36 = (bf16[64,5632]{1,0:T(8,128)(2,1)}, bf16[64,5632]{1,0:T(8,128)(2,1)}, u32[]{:S(2)}, u32[]{:S(2)}) collective-permute-start(bf16[64,5632]{1,0:T(8,128)(2,1)} %dynamic-slice_bitcast_fusion.5), channel_id=1, source_target_pairs={{0,1},{1,0},{2,3},{3,2},{4,5},{5,4},{6,7},{7,6},{8,9},{9,8},{10,11... | collective-permute-start | bytes 2162696 | tf_op jit(solution)/shard_map/ppermute | solution.py:583
  319.4 29.3 %collective-permute-start.34 = (bf16[2,3,128,256]{3,2,1,0:T(8,128)(2,1)}, bf16[2,3,128,256]{3,2,1,0:T(8,128)(2,1)}, u32[]{:S(2)}, u32[]{:S(2)}) collective-permute-start(bf16[2,3,128,256]{3,2,1,0:T(8,128)(2,1)} %fusion.32), channel_id=1, source_target_pairs={{1,0},{5,4},{9,8},{13,12},{17,16},{21,20},{25,24},{29,28}} | collective-permute-start | bytes 1179656 | tf_op jit(solution)/shard_map/ppermute | solution.py:717
  350.9 27.4 %collective-permute-start.37 = (bf16[256,1536]{1,0:T(8,128)(2,1)S(1)}, bf16[256,1536]{1,0:T(8,128)(2,1)S(1)}, u32[]{:S(2)}, u32[]{:S(2)}) collective-permute-start(bf16[256,1536]{1,0:T(8,128)(2,1)S(1)} %dynamic-slice_bitcast_fusion.4), channel_id=1, source_target_pairs={{0,8},{4,12},{8,0},{12,4},{1,9},{5,13},{9,1},{13,5},{2,10},{6,14},... | collective-permute-start | bytes 2359304 | tf_op jit(solution)/shard_map/ppermute | solution.py:583
  353.2 44.4 %collective-permute-start.39 = (bf16[64,5632]{1,0:T(8,128)(2,1)S(1)}, bf16[64,5632]{1,0:T(8,128)(2,1)}, u32[]{:S(2)}, u32[]{:S(2)}) collective-permute-start(bf16[64,5632]{1,0:T(8,128)(2,1)S(1)} %fusion.20), channel_id=1, source_target_pairs={{0,2},{1,3},{2,0},{3,1},{4,6},{5,7},{6,4},{7,5},{8,10},{9,11},{10,... | collective-permute-start | bytes 2162696 | tf_op jit(solution)/shard_map/ppermute | solution.py:583
  380.7 16.9 %collective-permute-start.40 = (bf16[128,1536]{1,0:T(8,128)(2,1)}, bf16[128,1536]{1,0:T(8,128)(2,1)}, u32[]{:S(2)}, u32[]{:S(2)}) collective-permute-start(bf16[128,1536]{1,0:T(8,128)(2,1)} %dynamic-slice_bitcast_fusion.9), channel_id=1, source_target_pairs={{0,16},{16,0},{1,17},{17,1},{2,18},{18,2},{3,19},{19,3},{4,20},{20... | collective-permute-start | bytes 1179656 | tf_op jit(solution)/shard_map/ppermute | solution.py:583
  399.1 29.6 %collective-permute-start.41 = (bf16[2,256,2048]{2,1,0:T(8,128)(2,1)}, bf16[2,256,2048]{2,1,0:T(8,128)(2,1)}, u32[]{:S(2)}, u32[]{:S(2)}) collective-permute-start(bf16[2,256,2048]{2,1,0:T(8,128)(2,1)} %dynamic-slice_bitcast_fusion), channel_id=1, source_target_pairs={{0,4},{4,0},{8,12},{12,8},{1,5},{5,1},{9,13},{13,9},{2,6},{6,2},{1... | collective-permute-start | bytes 6291464 | tf_op jit(solution)/shard_map/ppermute | solution.py:583
  402.8 25.9 %collective-permute-start.42 = (bf16[64,5632]{1,0:T(8,128)(2,1)}, bf16[64,5632]{1,0:T(8,128)(2,1)}, u32[]{:S(2)}, u32[]{:S(2)}) collective-permute-start(bf16[64,5632]{1,0:T(8,128)(2,1)} %add_convert_fusion.1), channel_id=1, source_target_pairs={{0,1},{1,0},{2,3},{3,2},{4,5},{5,4},{6,7},{7,6},{8,9},{9,8},{10,11... | collective-permute-start | bytes 2162696 | tf_op jit(solution)/shard_map/ppermute | solution.py:583
  407.7 20.9 %collective-permute-start.43 = (bf16[64,1536]{1,0:T(8,128)(2,1)}, bf16[64,1536]{1,0:T(8,128)(2,1)}, u32[]{:S(2)}, u32[]{:S(2)}) collective-permute-start(bf16[64,1536]{1,0:T(8,128)(2,1)} %dynamic-slice_bitcast_fusion.12), channel_id=1, source_target_pairs={{0,1},{1,0},{2,3},{3,2},{4,5},{5,4},{6,7},{7,6},{8,9},{9,8},{10,11... | collective-permute-start | bytes 589832 | tf_op jit(solution)/shard_map/ppermute | solution.py:583
  428.7 20.1 %collective-permute-start.44 = (bf16[3,3,1024]{2,1,0:T(4,128)(2,1)S(1)}, bf16[3,3,1024]{2,1,0:T(4,128)(2,1)S(1)}, u32[]{:S(2)}, u32[]{:S(2)}) collective-permute-start(bf16[3,3,1024]{2,1,0:T(4,128)(2,1)S(1)} %slice.304), channel_id=1, source_target_pairs={{1,0},{2,1},{3,2},{5,4},{6,5},{7,6},{9,8},{10,9},{11,10},{13,12},{... | collective-permute-start | bytes 55304 | tf_op jit(solution)/shard_map/ppermute | solution.py:41
  431.8 20.6 %collective-permute-start.45 = (bf16[64,1536]{1,0:T(8,128)(2,1)}, bf16[64,1536]{1,0:T(8,128)(2,1)}, u32[]{:S(2)}, u32[]{:S(2)}) collective-permute-start(bf16[64,1536]{1,0:T(8,128)(2,1)} %fusion.47), channel_id=1, source_target_pairs={{0,2},{1,3},{2,0},{3,1},{4,6},{5,7},{6,4},{7,5},{8,10},{9,11},{10,... | collective-permute-start | bytes 589832 | tf_op jit(solution)/shard_map/ppermute | solution.py:583
  439.7 35.1 %collective-permute-start.46 = (bf16[256,2048]{1,0:T(8,128)(2,1)}, bf16[256,2048]{1,0:T(8,128)(2,1)}, u32[]{:S(2)}, u32[]{:S(2)}) collective-permute-start(bf16[256,2048]{1,0:T(8,128)(2,1)} %dynamic-slice_bitcast_fusion.3), channel_id=1, source_target_pairs={{0,8},{4,12},{8,0},{12,4},{1,9},{5,13},{9,1},{13,5},{2,10},{6,14},... | collective-permute-start | bytes 3145736 | tf_op jit(solution)/shard_map/ppermute | solution.py:583
  445.6 32.3 %collective-permute-start.50 = (bf16[128,5632]{1,0:T(8,128)(2,1)}, bf16[128,5632]{1,0:T(8,128)(2,1)}, u32[]{:S(2)}, u32[]{:S(2)}) collective-permute-start(bf16[128,5632]{1,0:T(8,128)(2,1)} %bitcast.51), channel_id=1, source_target_pairs={{0,16},{16,0},{1,17},{17,1},{2,18},{18,2},{3,19},{19,3},{4,20},{20... | collective-permute-start | bytes 4325384 | tf_op jit(solution)/shard_map/ppermute | solution.py:583
  454.0 20.8 %collective-permute-start.47 = (bf16[2,256,1024]{2,1,0:T(8,128)(2,1)S(1)}, bf16[2,256,1024]{2,1,0:T(8,128)(2,1)S(1)}, u32[]{:S(2)}, u32[]{:S(2)}) collective-permute-start(bf16[2,256,1024]{2,1,0:T(8,128)(2,1)S(1)} %dynamic-slice_bitcast_fusion.2), channel_id=1, source_target_pairs={{0,4},{4,0},{8,12},{12,8},{1,5},{5,1},{9,13},{13,9},{2,6},{6,2},{1... | collective-permute-start | bytes 3145736 | tf_op jit(solution)/shard_map/ppermute | solution.py:583
  455.3 19.4 %collective-permute-start.48 = (bf16[272,1024]{1,0:T(8,128)(2,1)S(1)}, bf16[272,1024]{1,0:T(8,128)(2,1)S(1)}, u32[]{:S(2)}, u32[]{:S(2)}) collective-permute-start(bf16[272,1024]{1,0:T(8,128)(2,1)S(1)} %dynamic-slice_bitcast_fusion.6), channel_id=1, source_target_pairs={{0,1},{1,0},{2,3},{3,2},{4,5},{5,4},{6,7},{7,6},{8,9},{9,8},{10,11... | collective-permute-start | bytes 1671176 | tf_op jit(solution)/shard_map/ppermute | solution.py:583
  458.5 16.3 %collective-permute-start.49 = (bf16[64,1536]{1,0:T(8,128)(2,1)S(1)}, bf16[64,1536]{1,0:T(8,128)(2,1)S(1)}, u32[]{:S(2)}, u32[]{:S(2)}) collective-permute-start(bf16[64,1536]{1,0:T(8,128)(2,1)S(1)} %add_convert_fusion.4), channel_id=1, source_target_pairs={{0,1},{1,0},{2,3},{3,2},{4,5},{5,4},{6,7},{7,6},{8,9},{9,8},{10,11... | collective-permute-start | bytes 589832 | tf_op jit(solution)/shard_map/ppermute | solution.py:583
  479.6 19.9 %collective-permute-start.51 = (bf16[128,2048]{1,0:T(8,128)(2,1)S(1)}, bf16[128,2048]{1,0:T(8,128)(2,1)S(1)}, u32[]{:S(2)}, u32[]{:S(2)}) collective-permute-start(bf16[128,2048]{1,0:T(8,128)(2,1)S(1)} %dynamic-slice_bitcast_fusion.8), channel_id=1, source_target_pairs={{0,16},{16,0},{1,17},{17,1},{2,18},{18,2},{3,19},{19,3},{4,20},{20... | collective-permute-start | bytes 1572872 | tf_op jit(solution)/shard_map/ppermute | solution.py:583
  480.9 18.6 %collective-permute-start.52 = (bf16[256,1024]{1,0:T(8,128)(2,1)S(1)}, bf16[256,1024]{1,0:T(8,128)(2,1)S(1)}, u32[]{:S(2)}, u32[]{:S(2)}) collective-permute-start(bf16[256,1024]{1,0:T(8,128)(2,1)S(1)} %dynamic-slice_bitcast_fusion.7), channel_id=1, source_target_pairs={{0,8},{4,12},{8,0},{12,4},{1,9},{5,13},{9,1},{13,5},{2,10},{6,14},... | collective-permute-start | bytes 1572872 | tf_op jit(solution)/shard_map/ppermute | solution.py:583
  482.3 24.6 %collective-permute-start.53 = (bf16[272,1024]{1,0:T(8,128)(2,1)S(1)}, bf16[272,1024]{1,0:T(8,128)(2,1)S(1)}, u32[]{:S(2)}, u32[]{:S(2)}) collective-permute-start(bf16[272,1024]{1,0:T(8,128)(2,1)S(1)} %fusion.33), channel_id=1, source_target_pairs={{0,2},{1,3},{2,0},{3,1},{4,6},{5,7},{6,4},{7,5},{8,10},{9,11},{10,... | collective-permute-start | bytes 1671176 | tf_op jit(solution)/shard_map/ppermute | solution.py:583
  482.9 16.6 %collective-permute-start.54 = (bf16[128,1536]{1,0:T(8,128)(2,1)S(1)}, bf16[128,1536]{1,0:T(8,128)(2,1)S(1)}, u32[]{:S(2)}, u32[]{:S(2)}) collective-permute-start(bf16[128,1536]{1,0:T(8,128)(2,1)S(1)} %bitcast.326), channel_id=1, source_target_pairs={{0,16},{16,0},{1,17},{17,1},{2,18},{18,2},{3,19},{19,3},{4,20},{20... | collective-permute-start | bytes 1179656 | tf_op jit(solution)/shard_map/ppermute | solution.py:583
  515.0 14.7 %collective-permute-start.55 = (bf16[64,2048]{1,0:T(8,128)(2,1)S(1)}, bf16[64,2048]{1,0:T(8,128)(2,1)}, u32[]{:S(2)}, u32[]{:S(2)}) collective-permute-start(bf16[64,2048]{1,0:T(8,128)(2,1)S(1)} %dynamic-slice_bitcast_fusion.11), channel_id=1, source_target_pairs={{0,1},{1,0},{2,3},{3,2},{4,5},{5,4},{6,7},{7,6},{8,9},{9,8},{10,11... | collective-permute-start | bytes 786440 | tf_op jit(solution)/shard_map/ppermute | solution.py:583
  516.0 13.7 %collective-permute-start.56 = (bf16[128,1024]{1,0:T(8,128)(2,1)}, bf16[128,1024]{1,0:T(8,128)(2,1)}, u32[]{:S(2)}, u32[]{:S(2)}) collective-permute-start(bf16[128,1024]{1,0:T(8,128)(2,1)} %dynamic-slice_bitcast_fusion.10), channel_id=1, source_target_pairs={{0,16},{16,0},{1,17},{17,1},{2,18},{18,2},{3,19},{19,3},{4,20},{20... | collective-permute-start | bytes 786440 | tf_op jit(solution)/shard_map/ppermute | solution.py:583
  517.4 17.0 %collective-permute-start.57 = (bf16[272,1024]{1,0:T(8,128)(2,1)S(1)}, bf16[272,1024]{1,0:T(8,128)(2,1)}, u32[]{:S(2)}, u32[]{:S(2)}) collective-permute-start(bf16[272,1024]{1,0:T(8,128)(2,1)S(1)} %add_convert_fusion.2), channel_id=1, source_target_pairs={{0,1},{1,0},{2,3},{3,2},{4,5},{5,4},{6,7},{7,6},{8,9},{9,8},{10,11... | collective-permute-start | bytes 1671176 | tf_op jit(solution)/shard_map/ppermute | solution.py:583
  535.7 24.7 %collective-permute-start.60 = (bf16[544,1024]{1,0:T(8,128)(2,1)S(1)}, bf16[544,1024]{1,0:T(8,128)(2,1)S(1)}, u32[]{:S(2)}, u32[]{:S(2)}) collective-permute-start(bf16[544,1024]{1,0:T(8,128)(2,1)S(1)} %bitcast.302), channel_id=1, source_target_pairs={{0,16},{16,0},{1,17},{17,1},{2,18},{18,2},{3,19},{19,3},{4,20},{20... | collective-permute-start | bytes 3342344 | tf_op jit(solution)/shard_map/ppermute | solution.py:583
  569.7 14.4 %collective-permute-start.65 = (bf16[128,2048]{1,0:T(8,128)(2,1)S(1)}, bf16[128,2048]{1,0:T(8,128)(2,1)S(1)}, u32[]{:S(2)}, u32[]{:S(2)}) collective-permute-start(bf16[128,2048]{1,0:T(8,128)(2,1)S(1)} %bitcast.319), channel_id=1, source_target_pairs={{0,16},{16,0},{1,17},{17,1},{2,18},{18,2},{3,19},{19,3},{4,20},{20... | collective-permute-start | bytes 1572872 | tf_op jit(solution)/shard_map/ppermute | solution.py:583
  (173 other events, 1370.2 us)
Sparse Core Ops, SparseCore 0:
  9.6 44.2 all-gather.5
  55.7 47.3 all-gather.9
  105.0 70.9 all-gather.7
  219.3 87.6 reduce-scatter.3
  310.8 66.9 reduce-scatter.5
  381.4 46.2 reduce-scatter.7

commit v4 on v3

--- a/solution.py
+++ b/solution.py
@@ -725,26 +725,27 @@
         super().__init__()
         self.value = values
         for axis in ("fsdp", "dp", "seq"):
-            bits = bits_of(axis)
-            if bits is None:
+            count = lax.axis_size(axis)
+            if bits_of(axis) is None or count > 4:
                 self.value = lax.psum(self.value, axis)
             else:
-                for bit in bits:
-                    self.step(axis, bit)
-
-    def step(self, axis, bit):
-        self.todo.append(
-            (lambda: swap(self.value, axis, bit), lambda came: self.value + came)
-        )
+                self.todo.append((partial(self.send, axis, count), self.take))
+
+    def send(self, axis, count):
+        return tuple(swap(self.value, axis, bit) for bit in range(1, count))
+
+    def take(self, came):
+        if len(came) == 1:
+            return self.value + came[0]
+        return (self.value + came[0]) + (came[1] + came[2])
 
 
 def meet(movers, *arrays):
     movers = [mover for mover in movers if mover.pending is not None]
-    count = len(arrays)
-    out = lax.optimization_barrier(tuple(arrays) + tuple(mover.pending for mover in movers))
-    for mover, came in zip(movers, out[count:]):
-        mover.settle(came)
-    return out[:count]
+    arrays, came = lax.optimization_barrier((arrays, [mover.pending for mover in movers]))
+    for mover, values in zip(movers, came):
+        mover.settle(values)
+    return arrays
 
 
 def begin(*movers):
@@ -1012,12 +1013,15 @@
     begin(grad_states[1], grad_states[2])
     grad_gate_low = grad_gate_low.reshape(count, VD)
     grad_out = jnp.einsum("rv,rd->vd", heads_late, grad_branch, preferred_element_type=F32)
+    grad_out, r_in.value, grad_gate_low = meet(
+        [], grad_out.astype(LOW), r_in.value, grad_gate_low
+    )
+    p_out = scatter(grad_out)
+    begin(r_in)
     grad_gate = jnp.einsum("rd,rc->dc", normed_low, grad_gate_low, preferred_element_type=F32)
-    mixed_a, grad_out, grad_gate, r_in.value = meet(
-        [grad_states[1], grad_states[2]],
-        back[0][0], grad_out.astype(LOW), grad_gate.astype(LOW), r_in.value,
-    )
-    p_out = scatter(grad_out)
+    mixed_a, grad_gate = meet(
+        [grad_states[1], grad_states[2], r_in], back[0][0], grad_gate.astype(LOW)
+    )
     r_gate = ShardSum(grad_gate)
     begin(grad_states[2], r_gate, r_in)
 
@@ -1048,43 +1052,46 @@
     mixed_b, *kept = meet([grad_states[2], r_gate, r_in], back[1][0], *got_a[:3])
     begin(r_gate, r_in)
     got_b = mixer_back(1, mixed_b, 1, 2 * run, kept)
-    mixed_c, pre_ab, rim_ab, tail_ab, grad_gate_low = meet(
-        [r_gate], back[2][0], *got_b[:3], grad_gate_low
-    )
-    begin(r_gate)
+    mixed_c, pre_ab, rim_ab, tail_ab, grad_gate_low, p_down = meet(
+        [r_gate, r_in], back[2][0], *got_b[:3], grad_gate_low, p_down
+    )
+    r_down = ShardSum(p_down, ready=True)
+    begin(r_gate, r_in, r_down)
     came_ab = rim_swap(rim_ab)
     grad_normed = normed_part(grad_gate_low, full_gate)
     pre_ab, came_ab, tail_ab, grad_normed = meet([], pre_ab, came_ab, tail_ab, grad_normed)
     pre_ab = with_rim(pre_ab, came_ab, tail_ab)
     grad_ab = weight_grad(pre_ab)
-    mixed_c, grad_ab = meet([r_in, r_gate], mixed_c, grad_ab)
-    sum_ab = ShardSum(grad_ab)
-    begin(sum_ab, r_in, r_gate)
+    mixed_c, grad_ab = meet([r_gate, r_down], mixed_c, grad_ab)
+    p_ab = scatter(grad_ab)
+    begin(r_gate, r_down)
     got_c = mixer_back(2, mixed_c, 0, run, [])
-    pre_c, rim_c, tail_c, pre_ab, grad_normed = meet(
-        [sum_ab, r_in, r_gate], *got_c[:3], pre_ab, grad_normed
-    )
-    begin(sum_ab, r_in, r_gate)
+    pre_c, rim_c, tail_c, pre_ab, grad_normed, p_out = meet(
+        [r_in, r_gate, r_down], *got_c[:3], pre_ab, grad_normed, p_out
+    )
+    r_out = ShardSum(p_out, ready=True)
+    begin(r_gate, r_down, r_out)
     came_c = rim_swap(rim_c)
     grad_normed = grad_normed + normed_part(pre_ab[:, :run], full_qkv[0])
     pre_c, came_c, tail_c, grad_normed = meet([], pre_c, came_c, tail_c, grad_normed)
     pre_c = with_rim(pre_c, came_c, tail_c)
     grad_c = weight_grad(pre_c)
-    grad_c, grad_normed, p_down, p_out = meet([r_gate], grad_c, grad_normed, p_down, p_out)
+    grad_c, grad_normed = meet([r_gate, r_down, r_out], grad_c, grad_normed)
     sum_c = ShardSum(grad_c)
-    r_late = ShardSum(jnp.concatenate([p_down, p_out], axis=0), ready=True)
-    begin(sum_c, r_late, r_gate)
+    begin(sum_c, r_out, r_gate, r_down)
     grad_normed = grad_normed + normed_part(pre_ab[:, run:], full_qkv[1])
-    grad_normed, pre_c = meet([sum_ab, sum_c, r_late, r_gate, r_in], grad_normed, pre_c)
-    begin(sum_ab, sum_c, r_late, r_gate)
+    grad_normed, pre_c = meet([sum_c, r_out, r_gate], grad_normed, pre_c)
+    begin(sum_c, r_out, r_gate)
     grad_normed = grad_normed + normed_part(pre_c, full_qkv[2])
     made_late = [item for got in (got_a, got_b, got_c) for item in got[3:5]]
-    hidden_late, grad_normed, *made_late = meet(
-        [sum_ab, sum_c, r_late, r_gate], hidden_late, grad_normed, *made_late, *[item[2] for item in back]
-    )
+    hidden_late, grad_normed, p_ab, *made_late = meet(
+        [sum_c, r_out, r_gate],
+        hidden_late, grad_normed, p_ab, *made_late, *[item[2] for item in back],
+    )
+    sum_ab = ShardSum(p_ab, ready=True)
     made_late, head_gains = made_late[: 2 * GROUPS], made_late[2 * GROUPS :]
     grad_head_gain = sum(jnp.sum(item, axis=(0, 1)) for item in head_gains)
-    begin(sum_ab, sum_c, r_late)
+    begin(sum_ab, sum_c, r_out)
     result = middle + jnp.dot(hidden_late, full_down, preferred_element_type=F32)
     output = result.astype(LOW).reshape(batch, length, width)
     grad_cols = jnp.concatenate(made_late[1::2], axis=0)
@@ -1117,7 +1124,7 @@
         grad_decay_bias,
     )
     small_grads = jnp.concatenate(little)
-    movers = [r_in, r_gate, sum_ab, sum_c, r_late]
+    movers = [r_in, r_gate, r_down, sum_ab, sum_c, r_out]
     (small_grads,) = meet(movers, small_grads)
     all_sum = AllSum(small_grads)
     movers.append(all_sum)
@@ -1126,9 +1133,7 @@
         meet(movers, small_grads)
     flat = all_sum.value
     sum_qkv = unpack_groups(sum_ab.value, sum_c.value)
-    late = r_late.value.reshape(-1, p_down.shape[0] + p_out.shape[0], width)
-    sum_down = late[:, : p_down.shape[0]].reshape(-1, width)
-    sum_out = late[:, p_down.shape[0] :].reshape(-1, width)
+    sum_down, sum_out = r_down.value, r_out.value
     parts, first = [], 0
     for item in little:
         parts.append(flat[first : first + item.size])

time: 618 us -> 601 us (0.972)
  waiting for transfers between devices: 88.2 us -> 80 us
  starting transfers between devices: 100 us -> 92.9 us
    ppermute x49 -> x52, waiting for transfers between devices: 73.2 us -> 57.4 us  [swap(): return lax.ppermute(values, axis, [(at, at ^ bit) for at in range(count)])]
    reduce_scatter x1, waiting for transfers between devices: 0.01 us -> 8.71 us  [__init__(): lax.psum_scatter(self.value, ('fsdp', 'dp'), scatter_dimension=0, tiled=T...]
    ppermute x49 -> x52, starting transfers between devices: 60.6 us -> 53.9 us  [swap(): return lax.ppermute(values, axis, [(at, at ^ bit) for at in range(count)])]
    unnamed x311 -> x317, local copies, waits for them, and re-layouts: 30.7 us -> 35.1 us
    convert_element_type x19 -> x18, other arithmetic: 18.2 us -> 17.3 us  [plus(): return (left.astype(F32) + right.astype(F32)).astype(LOW)]
  transfers between devices with their start and end apart: 77 -> 81, of which waited for: 18 -> 20; matrix products, arithmetic and copies ran while one was open for 32% -> 33% of each run, Pallas kernels for 22% -> 22%
where the time goes in v4:
time: 601 us; the launch traced here: 596 us
  Pallas kernels  157 us (26%)
  matrix products  120 us (20%)
  starting transfers between devices  92.9 us (15%)
  waiting for transfers between devices  80 us (13%)
  other arithmetic  72.2 us (12%)
  local copies, waits for them, and re-layouts  58.1 us (10%)
  between operations  17.1 us (3%)
    pallas_call x3, Pallas kernels, mixer_backward(): pl.pallas_call(kernel, grid=(heads,), in_specs=head_specs(seqs, count, fi...  61 us
    ppermute x52, waiting for transfers between devices, swap(): return lax.ppermute(values, axis, [(at, at ^ bit) for at in range(count)])  57.4 us
    ppermute x52, starting transfers between devices, swap(): return lax.ppermute(values, axis, [(at, at ^ bit) for at in range(count)])  53.9 us
    pallas_call x3, Pallas kernels, mixer_forward(): pl.pallas_call(forward_kernel, grid=(heads,), in_specs=head_specs(seqs, c...  38.8 us
    unnamed x317, local copies, waits for them, and re-layouts  35.1 us
    ppermute x18, starting transfers between devices, leave(): return lax.ppermute(leaving.astype(LOW), 'seq', [(hop, hop + step)])  28.3 us
    pallas_call x1, Pallas kernels, ffn_middle(): pl.pallas_call(ffn_kernel, grid=(tiles,), in_specs=[pl.BlockSpec((rows, w...  24.8 us
    convert_element_type x18, other arithmetic, plus(): return (left.astype(F32) + right.astype(F32)).astype(LOW)  17.3 us
  transfers between devices with their start and end apart: 81, of which 20 were waited for; matrix products, arithmetic and copies ran while one was open for 33% of the time, Pallas kernels for 22%

profile of v4, /device:TPU:0, one launch (start us, length us, event | category | flops | bytes accessed | tf_op | source)
XLA Modules:
  0.0 596.4 jit_solution(5108307937344378011)
XLA Ops:
  15.2 3.7 collective-permute-start.4
  25.9 3.5 collective-permute-start.3
  35.1 3.0 fusion.6
  41.1 5.1 collective-permute-done.5.refs_2_
  56.1 12.9 %mixer_forward.3 = (bf16[2,3,256,256]{3,2,1,0:T(8,128)(2,1)S(1)}, bf16[2,3,256,384]{3,2,1,0:T(8,128)(2,1)S(1)}, f32[3,256,512]{2,1,0:T(8,128)S(1)}, bf16[3,256,2...) custom-call(bf16[784,1024]{1,0:T(8,128)(2,1)} %convolution_convert_fusion.6.q_ref.k_ref.v_, ...), custom_call_target="tpu_custom_call" | custom-call | tf_op jit(solution)/shard_map/mixer_forward/pallas_call | solution.py:324
  72.8 3.8 collective-permute-start.12
  79.4 3.0 convolution_convert_fusion.5.q_ref.k_ref.v_ref.rq_ref.rk_ref.rv_ref.refs_0_.refs_1_.refs_2_.refs_3_.refs_4_.refs_5_
  82.4 13.0 %mixer_forward.4 = (bf16[2,3,256,256]{3,2,1,0:T(8,128)(2,1)S(1)}, bf16[2,3,256,384]{3,2,1,0:T(8,128)(2,1)S(1)}, f32[3,256,512]{2,1,0:T(8,128)S(1)}, bf16[3,256,2...) custom-call(bf16[784,1024]{1,0:T(8,128)(2,1)} %convolution_convert_fusion.5.q_ref.k_ref.v_, ...), custom_call_target="tpu_custom_call" | custom-call | tf_op jit(solution)/shard_map/mixer_forward/pallas_call | solution.py:324
  98.1 4.0 collective-permute-start.16
  105.2 3.0 convolution_convert_fusion.4.q_ref.k_ref.v_ref.rq_ref.rk_ref.rv_ref.refs_0_.refs_1_.refs_2_.refs_3_.refs_4_.refs_5_
  108.2 12.9 %mixer_forward.5 = (bf16[2,3,256,256]{3,2,1,0:T(8,128)(2,1)S(1)}, bf16[2,3,256,384]{3,2,1,0:T(8,128)(2,1)S(1)}, f32[3,256,512]{2,1,0:T(8,128)S(1)}, bf16[3,256,2...) custom-call(bf16[784,1024]{1,0:T(8,128)(2,1)} %convolution_convert_fusion.4.q_ref.k_ref.v_, ...), custom_call_target="tpu_custom_call" | custom-call | tf_op jit(solution)/shard_map/mixer_forward/pallas_call | solution.py:324
  129.2 7.2 %fusion.80 = f32[768,1536]{1,0:T(8,128)} fusion(bf16[768,1024]{1,0:T(8,128)(2,1)} %fusion.6, bf16[1024,1536]{1,0:T(8,128)(2,1)} %all-gather.6.cloned.1.call-done), kind=kOutput, calls=%fused_computation.223 | convolution fusion | flops 2415919104 | bytes 9437184 | tf_op jit(solution)/shard_map/dot_general | solution.py:954
  157.2 4.1 assemble.7
  170.4 6.0 %all-gather.8.cloned.1.call-done = bf16[1,1024,5632]{2,1,0:T(8,128)(2,1)} async-done(((bf16[1,128,5632]{2,1,0:T(8,128)(2,1)}), bf16[1,1024,5632]{2,1,0:T(8,128)(2,1)}) %all-gather.8.cloned.1.call-update) | async-done | bytes 11534352 | tf_op jit(solution)/shard_map/all_gather | solution.py:782
  179.2 24.8 %ffn_middle.1 = (bf16[768,2816]{1,0:T(8,128)(2,1)}, bf16[768,5632]{1,0:T(8,128)(2,1)}) custom-call(bf16[768,1024]{1,0:T(8,128)(2,1)S(1)} %copy-done.10, bf16[1024,5632]{1,0:T(8,128)(2,1)} %bitcast.286, bf16[1024,5632]{1,0:T(8,128)(2,1)} %bitcast.287, bf16[768,1024]{1,0:T(8,128)(2,1)S(1)} %bitcast.275, bf16[2816,1024]{1,0:T(8,128)(2,1)} %bitcast.293), custom_call_target="tpu_custom_call" | custom-call | tf_op jit(solution)/shard_map/ffn_middle/pallas_call | solution.py:507
  204.1 15.4 %convolution_convert_fusion = bf16[1024,5632]{1,0:T(8,128)(2,1)} fusion(bf16[768,1024]{1,0:T(8,128)(2,1)S(1)} %copy-done.10, bf16[768,5632]{1,0:T(8,128)(2,1)} %get-tuple-element.240), kind=kOutput, calls=%fused_computation | convolution fusion | flops 8864137216 | bytes 21757952 | tf_op jit(solution)/shard_map/rd,rf->df/dot_general | solution.py:971
  219.7 16.6 %multiply_reduce_fusion = (f32[1024]{0:T(1024)S(1)}, f32[768]{0:T(1024)S(1)}, f32[768,1024]{1,0:T(8,128)}) fusion(f32[768,1024]{1,0:T(8,128)} %copy-done.73, f32[768]{0:T(1024)S(1)} %fusion.65, f32[1024]{0:T(1024)S(1)} %bitcast.361, bf16[768,5632]{1,0:T(8,128)(2,1)} %get-tuple-element.240, bf16[1,1024,5632]{2,1,0:T(8,128)(2,1)} %all-gather.8.cloned.1.call-done), kind=kOutput, calls=%fused_computation.27 | convolution fusion | flops 8863086592 | bytes 26490880 | tf_op jit(solution)/shard_map/rf,df->rd/dot_general | solution.py:976
  236.3 3.3 fusion
  239.8 4.4 fusion.38
  244.2 5.2 heads_backward.3
  250.4 5.2 heads_backward.4
  258.4 5.4 heads_backward.5
  271.2 8.7 %convolution_convert_fusion.1 = bf16[2816,1024]{1,0:T(8,128)(2,1)} fusion(bf16[768,2816]{1,0:T(8,128)(2,1)} %get-tuple-element.340, bf16[768,1024]{1,0:T(8,128)(2,1)S(1)} %bitcast.276), kind=kOutput, calls=%fused_computation.2 | convolution fusion | flops 4432068608 | bytes 11665408 | tf_op jit(solution)/shard_map/rf,rd->fd/dot_general | solution.py:1008
  279.9 6.7 %collective-permute-done.29 = bf16[2,3,128,256]{3,2,1,0:T(8,128)(2,1)} collective-permute-done((bf16[2,3,128,256]{3,2,1,0:T(8,128)(2,1)}, bf16[2,3,128,256]{3,2,1,0:T(8,128)(2,1)}, u32[]{:S(2)}, u32[]{:S(2)}) %collective-permute-start.29) | collective-permute-done | bytes 393248 | tf_op jit(solution)/shard_map/ppermute | solution.py:717
  292.5 6.0 convolution_convert_fusion.3
  298.4 8.7 %reduce-scatter.5.cloned.1.call-done = bf16[128,5632]{1,0:T(8,128)(2,1)} async-done(((bf16[1024,5632]{1,0:T(8,128)(2,1)}), bf16[128,5632]{1,0:T(8,128)(2,1)}) %reduce-scatter.5.cloned.1.call-update) | async-done | bytes 1441808 | tf_op jit(solution)/shard_map/reduce_scatter | solution.py:656
  311.9 4.6 convolution_convert_fusion.2
  316.5 9.8 %collective-permute-done.34 = bf16[64,5632]{1,0:T(8,128)(2,1)S(1)} collective-permute-done((bf16[64,5632]{1,0:T(8,128)(2,1)S(1)}, bf16[64,5632]{1,0:T(8,128)(2,1)S(1)}, u32[]{:S(2)}, u32[]{:S(2)}) %collective-permute-start.34) | collective-permute-done | bytes 720928 | tf_op jit(solution)/shard_map/ppermute | solution.py:583
  339.7 20.8 %mixer_backward.3 = (bf16[3,256,2048]{2,1,0:T(8,128)(2,1)}, f32[3,8,2048]{2,1,0:T(8,128)S(1)}, f32[3,8,2048]{2,1,0:T(8,128)S(1)}, f32[4,1024]{1,0:T(4,128)S(1)}, f32[2,3,8,256]{3,2,1,0:T(8,128)S(1)}) custom-call(bf16[784,1024]{1,0:T(8,128)(2,1)S(1)} %copy-done.3, bf16[784,1024]{1,0:T(8,128)(2,1)S(1)} %copy-done.3, bf16[784,1024]{1,0:T(8,128)(2,1)S(1)} %copy-done.3, ...), custom_call_target="tpu_custom_call" | custom-call | tf_op jit(solution)/shard_map/mixer_backward/pallas_call | solution.py:442
  360.5 3.2 collective-permute-done.37
  375.8 20.7 %mixer_backward.4 = (bf16[3,256,2048]{2,1,0:T(8,128)(2,1)}, f32[3,8,2048]{2,1,0:T(8,128)S(1)}, f32[3,8,2048]{2,1,0:T(8,128)S(1)}, f32[4,1024]{1,0:T(4,128)S(1)}, f32[2,3,8,256]{3,2,1,0:T(8,128)S(1)}) custom-call(bf16[784,1024]{1,0:T(8,128)(2,1)S(1)} %copy-done.2, ...), custom_call_target="tpu_custom_call", output_to_operand_aliasing={{0}: (16, {}), {1}: (17, {}), {2}: (18, {})} | custom-call | tf_op jit(solution)/shard_map/mixer_backward/pallas_call | solution.py:442
  404.7 3.1 maximum_select_fusion.1
  409.1 4.4 fusion.81
  415.6 7.3 %bitcast_convert_fusion = bf16[1024,2048]{1,0:T(8,128)(2,1)} fusion(bf16[3,256,2048]{2,1,0:T(8,128)(2,1)} %dynamic_update_slice.22, bf16[3,256,1024]{2,1,0:T(8,128)(2,1)S(1)} %copy-done.69, f32[1024]{0:T(1024)S(1)} %bitcast.353, f32[3,256]{1,0:T(4,128)S(1)} %copy-done.133), kind=kOutput, calls=%fused_computation.1 | convolution fusion | flops 3226468352 | bytes 8920064 | tf_op jit(solution)/shard_map/rd,rc->dc/dot_general | solution.py:1046
  424.8 3.4 collective-permute-start.45
  431.6 19.4 %mixer_backward.5 = (bf16[3,256,1024]{2,1,0:T(8,128)(2,1)S(1)}, f32[3,8,1024]{2,1,0:T(8,128)S(1)}, f32[3,8,1024]{2,1,0:T(8,128)S(1)}, f32[4,1024]{1,0:T(4,128)S(1)}, f32[2,3,8,256]{3,2,1,0:T(8,128)S(1)}) custom-call(bf16[784,1024]{1,0:T(8,128)(2,1)} %convolution_convert_fusion.4.q_ref.k_ref.v_ref.rq_ref.rk_ref.rv_ref.refs_0_.refs_1_.refs_2_.refs_3_.refs_4_.refs_5_, ...), custom_call_target="tpu_custom_call" | custom-call | tf_op jit(solution)/shard_map/mixer_backward/pallas_call | solution.py:442
  454.6 3.5 collective-permute-start.47
  462.4 3.4 maximum_select_fusion
  465.9 3.7 bitcast_convert_fusion.2
  474.9 3.6 bitcast_convert_fusion.1
  489.2 3.8 collective-permute-done.51
  501.6 12.0 %collective-permute-done.55 = bf16[128,1536]{1,0:T(8,128)(2,1)S(1)} collective-permute-done((bf16[128,1536]{1,0:T(8,128)(2,1)S(1)}, bf16[128,1536]{1,0:T(8,128)(2,1)S(1)}, u32[]{:S(2)}, u32[]{:S(2)}) %collective-permute-start.55) | collective-permute-done | bytes 393248 | tf_op jit(solution)/shard_map/ppermute | solution.py:583
  514.9 3.3 fusion.7
  526.9 5.9 add_convert_fusion
  546.0 5.1 collective-permute-done.61
  551.0 3.6 collective-permute-done.60
  554.9 3.2 collective-permute-start.66
  573.8 5.0 collective-permute-done.71
  (652 shorter events, 230.9 us)
Async XLA Ops:
  7.2 122.0 %all-gather.6.cloned.1.call-start = ((), (), s32[]{:S(2)}) async-start(), calls=%async_computation.4 | async-start | bytes 3932160 | tf_op jit(solution)/shard_map/all_gather | solution.py:900
  7.9 162.5 %all-gather.10.cloned.1.call-start = ((), (), s32[]{:S(2)}) async-start(), calls=%async_computation.10 | async-start | bytes 6488064 | tf_op jit(solution)/shard_map/all_gather | solution.py:782
  10.1 166.3 %all-gather.8.cloned.1.call-start = ((), (), s32[]{:S(2)}) async-start(), calls=%async_computation.9 | async-start | bytes 12976128 | tf_op jit(solution)/shard_map/all_gather | solution.py:782
  11.5 295.7 %reduce-scatter.5.cloned.1.call-start = ((), (), s32[]{:S(2)}) async-start(), calls=%async_computation.5 | async-start | bytes 12976128 | tf_op jit(solution)/shard_map/reduce_scatter | solution.py:656
  12.0 13.9 %collective-permute-start = (bf16[6720]{0:T(1024)(128)(2,1)S(1)}, bf16[6720]{0:T(1024)(128)(2,1)S(1)}, u32[]{:S(2)}, u32[]{:S(2)}) collective-permute-start(bf16[6720]{0:T(1024)(128)(2,1)S(1)} %concatenate.36), channel_id=1, source_target_pairs={{0,4},{4,0},{8,12},{12,8},{1,5},{5,1},{9,13},{13,9},{2,6},{6,2},{1... | collective-permute-start | bytes 40328 | tf_op jit(solution)/shard_map/ppermute | solution.py:583
  12.5 17.2 %collective-permute-start.1 = (bf16[6720]{0:T(1024)(128)(2,1)S(1)}, bf16[6720]{0:T(1024)(128)(2,1)S(1)}, u32[]{:S(2)}, u32[]{:S(2)}) collective-permute-start(bf16[6720]{0:T(1024)(128)(2,1)S(1)} %concatenate.36), channel_id=1, source_target_pairs={{0,8},{4,12},{8,0},{12,4},{1,9},{5,13},{9,1},{13,5},{2,10},{6,14},... | collective-permute-start | bytes 40328 | tf_op jit(solution)/shard_map/ppermute | solution.py:583
  15.1 14.9 %collective-permute-start.2 = (bf16[6720]{0:T(1024)(128)(2,1)S(1)}, bf16[6720]{0:T(1024)(128)(2,1)S(1)}, u32[]{:S(2)}, u32[]{:S(2)}) collective-permute-start(bf16[6720]{0:T(1024)(128)(2,1)S(1)} %concatenate.36), channel_id=1, source_target_pairs={{0,12},{4,8},{8,4},{12,0},{1,13},{5,9},{9,5},{13,1},{2,14},{6,10},... | collective-permute-start | bytes 40328 | tf_op jit(solution)/shard_map/ppermute | solution.py:583
  20.6 25.6 %collective-permute-start.5 = (bf16[256,1024]{1,0:T(8,128)(2,1)S(1)}, bf16[256,1024]{1,0:T(8,128)(2,1)S(1)}, u32[]{:S(2)}, u32[]{:S(2)}) collective-permute-start(bf16[256,1024]{1,0:T(8,128)(2,1)S(1)} %get-tuple-element.196.refs_0_), channel_id=1, source_target_pairs={{0,8},{4,12},{8,0},{12,4},{1,9},{5,13},{9,1},{13,5},{2,10},{6,14},... | collective-permute-start | bytes 1572872 | tf_op jit(solution)/shard_map/ppermute | solution.py:583
  25.6 24.8 %collective-permute-start.6 = (bf16[256,1024]{1,0:T(8,128)(2,1)S(1)}, bf16[256,1024]{1,0:T(8,128)(2,1)S(1)}, u32[]{:S(2)}, u32[]{:S(2)}) collective-permute-start(bf16[256,1024]{1,0:T(8,128)(2,1)S(1)} %get-tuple-element.196.refs_0_), channel_id=1, source_target_pairs={{0,4},{4,0},{8,12},{12,8},{1,5},{5,1},{9,13},{13,9},{2,6},{6,2},{1... | collective-permute-start | bytes 1572872 | tf_op jit(solution)/shard_map/ppermute | solution.py:583
  46.3 25.8 %collective-permute-start.8 = (bf16[256,1024]{1,0:T(8,128)(2,1)S(1)}, bf16[256,1024]{1,0:T(8,128)(2,1)}, u32[]{:S(2)}, u32[]{:S(2)}) collective-permute-start(bf16[256,1024]{1,0:T(8,128)(2,1)S(1)} %get-tuple-element.202.refs_0_), channel_id=1, source_target_pairs={{0,8},{4,12},{8,0},{12,4},{1,9},{5,13},{9,1},{13,5},{2,10},{6,14},... | collective-permute-start | bytes 1572872 | tf_op jit(solution)/shard_map/ppermute | solution.py:583
  48.0 28.5 %collective-permute-start.9 = (bf16[256,1024]{1,0:T(8,128)(2,1)S(1)}, bf16[256,1024]{1,0:T(8,128)(2,1)}, u32[]{:S(2)}, u32[]{:S(2)}) collective-permute-start(bf16[256,1024]{1,0:T(8,128)(2,1)S(1)} %get-tuple-element.202.refs_0_), channel_id=1, source_target_pairs={{0,4},{4,0},{8,12},{12,8},{1,5},{5,1},{9,13},{13,9},{2,6},{6,2},{1... | collective-permute-start | bytes 1572872 | tf_op jit(solution)/shard_map/ppermute | solution.py:583
  72.4 24.3 %collective-permute-start.11 = (bf16[256,1024]{1,0:T(8,128)(2,1)S(1)}, bf16[256,1024]{1,0:T(8,128)(2,1)S(1)}, u32[]{:S(2)}, u32[]{:S(2)}) collective-permute-start(bf16[256,1024]{1,0:T(8,128)(2,1)S(1)} %get-tuple-element.206.refs_0_), channel_id=1, source_target_pairs={{0,8},{4,12},{8,0},{12,4},{1,9},{5,13},{9,1},{13,5},{2,10},{6,14},... | collective-permute-start | bytes 1572872 | tf_op jit(solution)/shard_map/ppermute | solution.py:583
  72.7 30.8 %collective-permute-start.13 = (bf16[256,1024]{1,0:T(8,128)(2,1)S(1)}, bf16[256,1024]{1,0:T(8,128)(2,1)S(1)}, u32[]{:S(2)}, u32[]{:S(2)}) collective-permute-start(bf16[256,1024]{1,0:T(8,128)(2,1)S(1)} %get-tuple-element.206.refs_0_), channel_id=1, source_target_pairs={{0,4},{4,0},{8,12},{12,8},{1,5},{5,1},{9,13},{13,9},{2,6},{6,2},{1... | collective-permute-start | bytes 1572872 | tf_op jit(solution)/shard_map/ppermute | solution.py:583
  72.8 23.9 %collective-permute-start.12 = (bf16[2,3,128,256]{3,2,1,0:T(8,128)(2,1)S(1)}, bf16[2,3,128,256]{3,2,1,0:T(8,128)(2,1)S(1)}, u32[]{:S(2)}, u32[]{:S(2)}) collective-permute-start(bf16[2,3,128,256]{3,2,1,0:T(8,128)(2,1)S(1)} %convert_element_type.430), channel_id=1, source_target_pairs={{0,1},{4,5},{8,9},{12,13},{16,17},{20,21},{24,25},{28,29}} | collective-permute-start | bytes 1179656 | tf_op jit(solution)/shard_map/ppermute | solution.py:717
  97.3 23.8 %collective-permute-start.15 = (bf16[2,3,128,256]{3,2,1,0:T(8,128)(2,1)S(1)}, bf16[2,3,128,256]{3,2,1,0:T(8,128)(2,1)S(1)}, u32[]{:S(2)}, u32[]{:S(2)}) collective-permute-start(bf16[2,3,128,256]{3,2,1,0:T(8,128)(2,1)S(1)} %fusion.19), channel_id=1, source_target_pairs={{1,2},{5,6},{9,10},{13,14},{17,18},{21,22},{25,26},{29,30}} | collective-permute-start | bytes 1179656 | tf_op jit(solution)/shard_map/ppermute | solution.py:717
  98.1 23.1 %collective-permute-start.16 = (bf16[2,3,128,256]{3,2,1,0:T(8,128)(2,1)S(1)}, bf16[2,3,128,256]{3,2,1,0:T(8,128)(2,1)S(1)}, u32[]{:S(2)}, u32[]{:S(2)}) collective-permute-start(bf16[2,3,128,256]{3,2,1,0:T(8,128)(2,1)S(1)} %convert_element_type.433), channel_id=1, source_target_pairs={{0,1},{4,5},{8,9},{12,13},{16,17},{20,21},{24,25},{28,29}} | collective-permute-start | bytes 1179656 | tf_op jit(solution)/shard_map/ppermute | solution.py:717
  102.1 34.3 %collective-permute-start.20 = (bf16[384,1024]{1,0:T(8,128)(2,1)}, bf16[384,1024]{1,0:T(8,128)(2,1)}, u32[]{:S(2)}, u32[]{:S(2)}) collective-permute-start(bf16[384,1024]{1,0:T(8,128)(2,1)} %refs_0_), channel_id=1, source_target_pairs={{0,8},{4,12},{8,0},{12,4},{1,9},{5,13},{9,1},{13,5},{2,10},{6,14},... | collective-permute-start | bytes 2359304 | tf_op jit(solution)/shard_map/ppermute | solution.py:583
  121.6 14.8 %collective-permute-start.17 = (bf16[2,3,128,256]{3,2,1,0:T(8,128)(2,1)S(1)}, bf16[2,3,128,256]{3,2,1,0:T(8,128)(2,1)}, u32[]{:S(2)}, u32[]{:S(2)}) collective-permute-start(bf16[2,3,128,256]{3,2,1,0:T(8,128)(2,1)S(1)} %fusion.20), channel_id=1, source_target_pairs={{2,3},{6,7},{10,11},{14,15},{18,19},{22,23},{26,27},{30,31}} | collective-permute-start | bytes 1179656 | tf_op jit(solution)/shard_map/ppermute | solution.py:717
  219.5 177.0 %reduce-scatter.7.cloned.1.call-start = ((), (), s32[]{:S(2)}) async-start(), calls=%async_computation.6 | async-start | bytes 6488064 | tf_op jit(solution)/shard_map/reduce_scatter | solution.py:639
  264.6 15.4 %collective-permute-start.31 = (bf16[2,3,128,256]{3,2,1,0:T(8,128)(2,1)}, bf16[2,3,128,256]{3,2,1,0:T(8,128)(2,1)}, u32[]{:S(2)}, u32[]{:S(2)}) collective-permute-start(bf16[2,3,128,256]{3,2,1,0:T(8,128)(2,1)} %convert_element_type.454), channel_id=1, source_target_pairs={{3,2},{7,6},{11,10},{15,14},{19,18},{23,22},{27,26},{31,30}} | collective-permute-start | bytes 1179656 | tf_op jit(solution)/shard_map/ppermute | solution.py:717
  267.2 19.5 %collective-permute-start.29 = (bf16[2,3,128,256]{3,2,1,0:T(8,128)(2,1)}, bf16[2,3,128,256]{3,2,1,0:T(8,128)(2,1)}, u32[]{:S(2)}, u32[]{:S(2)}) collective-permute-start(bf16[2,3,128,256]{3,2,1,0:T(8,128)(2,1)} %fusion.26), channel_id=1, source_target_pairs={{1,0},{5,4},{9,8},{13,12},{17,16},{21,20},{25,24},{29,28}} | collective-permute-start | bytes 1179656 | tf_op jit(solution)/shard_map/ppermute | solution.py:717
  269.6 17.1 %collective-permute-start.30 = (bf16[2,3,128,256]{3,2,1,0:T(8,128)(2,1)}, bf16[2,3,128,256]{3,2,1,0:T(8,128)(2,1)}, u32[]{:S(2)}, u32[]{:S(2)}) collective-permute-start(bf16[2,3,128,256]{3,2,1,0:T(8,128)(2,1)} %fusion.27), channel_id=1, source_target_pairs={{2,1},{6,5},{10,9},{14,13},{18,17},{22,21},{26,25},{30,29}} | collective-permute-start | bytes 1179656 | tf_op jit(solution)/shard_map/ppermute | solution.py:717
  286.7 165.5 %reduce-scatter.9.cloned.1.call-start = ((), (), s32[]{:S(2)}) async-start(), calls=%async_computation.7 | async-start | bytes 3538944 | tf_op jit(solution)/shard_map/reduce_scatter | solution.py:639
  291.2 25.3 %collective-permute-start.32 = (bf16[2,3,128,256]{3,2,1,0:T(8,128)(2,1)}, bf16[2,3,128,256]{3,2,1,0:T(8,128)(2,1)}, u32[]{:S(2)}, u32[]{:S(2)}) collective-permute-start(bf16[2,3,128,256]{3,2,1,0:T(8,128)(2,1)} %fusion.28), channel_id=1, source_target_pairs={{1,0},{5,4},{9,8},{13,12},{17,16},{21,20},{25,24},{29,28}} | collective-permute-start | bytes 1179656 | tf_op jit(solution)/shard_map/ppermute | solution.py:717
  308.3 17.9 %collective-permute-start.34 = (bf16[64,5632]{1,0:T(8,128)(2,1)S(1)}, bf16[64,5632]{1,0:T(8,128)(2,1)S(1)}, u32[]{:S(2)}, u32[]{:S(2)}) collective-permute-start(bf16[64,5632]{1,0:T(8,128)(2,1)S(1)} %dynamic-slice_bitcast_fusion.3), channel_id=1, source_target_pairs={{0,1},{1,0},{2,3},{3,2},{4,5},{5,4},{6,7},{7,6},{8,9},{9,8},{10,11... | collective-permute-start | bytes 2162696 | tf_op jit(solution)/shard_map/ppermute | solution.py:583
  327.5 36.3 %collective-permute-start.36 = (bf16[2,256,1536]{2,1,0:T(8,128)(2,1)}, bf16[2,256,1536]{2,1,0:T(8,128)(2,1)}, u32[]{:S(2)}, u32[]{:S(2)}) collective-permute-start(bf16[2,256,1536]{2,1,0:T(8,128)(2,1)} %dynamic-slice_bitcast_fusion), channel_id=1, source_target_pairs={{0,4},{4,0},{8,12},{12,8},{1,5},{5,1},{9,13},{13,9},{2,6},{6,2},{1... | collective-permute-start | bytes 4718600 | tf_op jit(solution)/shard_map/ppermute | solution.py:583
  328.6 35.2 %collective-permute-start.37 = (bf16[64,5632]{1,0:T(8,128)(2,1)}, bf16[64,5632]{1,0:T(8,128)(2,1)}, u32[]{:S(2)}, u32[]{:S(2)}) collective-permute-start(bf16[64,5632]{1,0:T(8,128)(2,1)} %fusion.18), channel_id=1, source_target_pairs={{0,2},{1,3},{2,0},{3,1},{4,6},{5,7},{6,4},{7,5},{8,10},{9,11},{10,... | collective-permute-start | bytes 2162696 | tf_op jit(solution)/shard_map/ppermute | solution.py:583
  333.2 27.4 %collective-permute-start.35 = (bf16[2,3,128,256]{3,2,1,0:T(8,128)(2,1)}, bf16[2,3,128,256]{3,2,1,0:T(8,128)(2,1)}, u32[]{:S(2)}, u32[]{:S(2)}) collective-permute-start(bf16[2,3,128,256]{3,2,1,0:T(8,128)(2,1)} %fusion.30), channel_id=1, source_target_pairs={{1,0},{5,4},{9,8},{13,12},{17,16},{21,20},{25,24},{29,28}} | collective-permute-start | bytes 1179656 | tf_op jit(solution)/shard_map/ppermute | solution.py:717
  367.7 28.8 %collective-permute-start.38 = (bf16[256,1536]{1,0:T(8,128)(2,1)}, bf16[256,1536]{1,0:T(8,128)(2,1)}, u32[]{:S(2)}, u32[]{:S(2)}) collective-permute-start(bf16[256,1536]{1,0:T(8,128)(2,1)} %dynamic-slice_bitcast_fusion.2), channel_id=1, source_target_pairs={{0,8},{4,12},{8,0},{12,4},{1,9},{5,13},{9,1},{13,5},{2,10},{6,14},... | collective-permute-start | bytes 2359304 | tf_op jit(solution)/shard_map/ppermute | solution.py:583
  371.4 25.1 %collective-permute-start.39 = (bf16[64,5632]{1,0:T(8,128)(2,1)}, bf16[64,5632]{1,0:T(8,128)(2,1)}, u32[]{:S(2)}, u32[]{:S(2)}) collective-permute-start(bf16[64,5632]{1,0:T(8,128)(2,1)} %add_convert_fusion.1), channel_id=1, source_target_pairs={{0,1},{1,0},{2,3},{3,2},{4,5},{5,4},{6,7},{7,6},{8,9},{9,8},{10,11... | collective-permute-start | bytes 2162696 | tf_op jit(solution)/shard_map/ppermute | solution.py:583
  371.9 142.6 %reduce-scatter.11.cloned.1.call-start = ((), (), s32[]{:S(2)}) async-start(), calls=%async_computation.8 | async-start | bytes 4718592 | tf_op jit(solution)/shard_map/reduce_scatter | solution.py:639
  396.6 16.9 %collective-permute-start.40 = (bf16[3,3,2048]{2,1,0:T(4,128)(2,1)S(1)}, bf16[3,3,2048]{2,1,0:T(4,128)(2,1)S(1)}, u32[]{:S(2)}, u32[]{:S(2)}) collective-permute-start(bf16[3,3,2048]{2,1,0:T(4,128)(2,1)S(1)} %slice.293), channel_id=1, source_target_pairs={{1,0},{2,1},{3,2},{5,4},{6,5},{7,6},{9,8},{10,9},{11,10},{13,12},{... | collective-permute-start | bytes 110600 | tf_op jit(solution)/shard_map/ppermute | solution.py:41
  400.7 22.2 %collective-permute-start.41 = (bf16[128,1536]{1,0:T(8,128)(2,1)}, bf16[128,1536]{1,0:T(8,128)(2,1)S(1)}, u32[]{:S(2)}, u32[]{:S(2)}) collective-permute-start(bf16[128,1536]{1,0:T(8,128)(2,1)} %dynamic-slice_bitcast_fusion.5), channel_id=1, source_target_pairs={{0,16},{16,0},{1,17},{17,1},{2,18},{18,2},{3,19},{19,3},{4,20},{20... | collective-permute-start | bytes 1179656 | tf_op jit(solution)/shard_map/ppermute | solution.py:583
  402.5 20.4 %collective-permute-start.42 = (bf16[176,1024]{1,0:T(8,128)(2,1)}, bf16[176,1024]{1,0:T(8,128)(2,1)}, u32[]{:S(2)}, u32[]{:S(2)}) collective-permute-start(bf16[176,1024]{1,0:T(8,128)(2,1)} %dynamic-slice_bitcast_fusion.6), channel_id=1, source_target_pairs={{0,1},{1,0},{2,3},{3,2},{4,5},{5,4},{6,7},{7,6},{8,9},{9,8},{10,11... | collective-permute-start | bytes 1081352 | tf_op jit(solution)/shard_map/ppermute | solution.py:583
  407.9 44.3 %collective-permute-start.43 = (bf16[128,5632]{1,0:T(8,128)(2,1)}, bf16[128,5632]{1,0:T(8,128)(2,1)}, u32[]{:S(2)}, u32[]{:S(2)}) collective-permute-start(bf16[128,5632]{1,0:T(8,128)(2,1)} %bitcast.38), channel_id=1, source_target_pairs={{0,16},{16,0},{1,17},{17,1},{2,18},{18,2},{3,19},{19,3},{4,20},{20... | collective-permute-start | bytes 4325384 | tf_op jit(solution)/shard_map/ppermute | solution.py:583
  424.8 27.4 %collective-permute-start.45 = (bf16[176,1024]{1,0:T(8,128)(2,1)}, bf16[176,1024]{1,0:T(8,128)(2,1)}, u32[]{:S(2)}, u32[]{:S(2)}) collective-permute-start(bf16[176,1024]{1,0:T(8,128)(2,1)} %fusion.40), channel_id=1, source_target_pairs={{0,2},{1,3},{2,0},{3,1},{4,6},{5,7},{6,4},{7,5},{8,10},{9,11},{10,... | collective-permute-start | bytes 1081352 | tf_op jit(solution)/shard_map/ppermute | solution.py:583
  428.4 23.8 %collective-permute-start.44 = (bf16[64,1536]{1,0:T(8,128)(2,1)S(1)}, bf16[64,1536]{1,0:T(8,128)(2,1)}, u32[]{:S(2)}, u32[]{:S(2)}) collective-permute-start(bf16[64,1536]{1,0:T(8,128)(2,1)S(1)} %dynamic-slice_bitcast_fusion.10), channel_id=1, source_target_pairs={{0,1},{1,0},{2,3},{3,2},{4,5},{5,4},{6,7},{7,6},{8,9},{9,8},{10,11... | collective-permute-start | bytes 589832 | tf_op jit(solution)/shard_map/ppermute | solution.py:583
  452.3 22.4 %collective-permute-start.46 = (bf16[3,3,1024]{2,1,0:T(4,128)(2,1)S(1)}, bf16[3,3,1024]{2,1,0:T(4,128)(2,1)S(1)}, u32[]{:S(2)}, u32[]{:S(2)}) collective-permute-start(bf16[3,3,1024]{2,1,0:T(4,128)(2,1)S(1)} %slice.294), channel_id=1, source_target_pairs={{1,0},{2,1},{3,2},{5,4},{6,5},{7,6},{9,8},{10,9},{11,10},{13,12},{... | collective-permute-start | bytes 55304 | tf_op jit(solution)/shard_map/ppermute | solution.py:41
  454.6 23.9 %collective-permute-start.47 = (bf16[64,1536]{1,0:T(8,128)(2,1)S(1)}, bf16[64,1536]{1,0:T(8,128)(2,1)S(1)}, u32[]{:S(2)}, u32[]{:S(2)}) collective-permute-start(bf16[64,1536]{1,0:T(8,128)(2,1)S(1)} %fusion.44), channel_id=1, source_target_pairs={{0,2},{1,3},{2,0},{3,1},{4,6},{5,7},{6,4},{7,5},{8,10},{9,11},{10,... | collective-permute-start | bytes 589832 | tf_op jit(solution)/shard_map/ppermute | solution.py:583
  459.3 19.3 %collective-permute-start.48 = (bf16[176,1024]{1,0:T(8,128)(2,1)S(1)}, bf16[176,1024]{1,0:T(8,128)(2,1)S(1)}, u32[]{:S(2)}, u32[]{:S(2)}) collective-permute-start(bf16[176,1024]{1,0:T(8,128)(2,1)S(1)} %add_convert_fusion.2), channel_id=1, source_target_pairs={{0,1},{1,0},{2,3},{3,2},{4,5},{5,4},{6,7},{7,6},{8,9},{9,8},{10,11... | collective-permute-start | bytes 1081352 | tf_op jit(solution)/shard_map/ppermute | solution.py:583
  460.4 18.2 %collective-permute-start.49 = (bf16[96,1024]{1,0:T(8,128)(2,1)S(1)}, bf16[96,1024]{1,0:T(8,128)(2,1)S(1)}, u32[]{:S(2)}, u32[]{:S(2)}) collective-permute-start(bf16[96,1024]{1,0:T(8,128)(2,1)S(1)} %dynamic-slice_bitcast_fusion.9), channel_id=1, source_target_pairs={{0,1},{1,0},{2,3},{3,2},{4,5},{5,4},{6,7},{7,6},{8,9},{9,8},{10,11... | collective-permute-start | bytes 589832 | tf_op jit(solution)/shard_map/ppermute | solution.py:583
  487.1 46.9 %collective-permute-start.56 = (bf16[352,1024]{1,0:T(8,128)(2,1)}, bf16[352,1024]{1,0:T(8,128)(2,1)}, u32[]{:S(2)}, u32[]{:S(2)}) collective-permute-start(bf16[352,1024]{1,0:T(8,128)(2,1)} %bitcast.65), channel_id=1, source_target_pairs={{0,16},{16,0},{1,17},{17,1},{2,18},{18,2},{3,19},{19,3},{4,20},{20... | collective-permute-start | bytes 2162696 | tf_op jit(solution)/shard_map/ppermute | solution.py:583
  494.3 20.1 %collective-permute-start.53 = (bf16[256,1024]{1,0:T(8,128)(2,1)S(1)}, bf16[256,1024]{1,0:T(8,128)(2,1)}, u32[]{:S(2)}, u32[]{:S(2)}) collective-permute-start(bf16[256,1024]{1,0:T(8,128)(2,1)S(1)} %dynamic-slice_bitcast_fusion.4), channel_id=1, source_target_pairs={{0,8},{4,12},{8,0},{12,4},{1,9},{5,13},{9,1},{13,5},{2,10},{6,14},... | collective-permute-start | bytes 1572872 | tf_op jit(solution)/shard_map/ppermute | solution.py:583
  495.5 18.1 %collective-permute-start.55 = (bf16[128,1536]{1,0:T(8,128)(2,1)S(1)}, bf16[128,1536]{1,0:T(8,128)(2,1)S(1)}, u32[]{:S(2)}, u32[]{:S(2)}) collective-permute-start(bf16[128,1536]{1,0:T(8,128)(2,1)S(1)} %bitcast.311), channel_id=1, source_target_pairs={{0,16},{16,0},{1,17},{17,1},{2,18},{18,2},{3,19},{19,3},{4,20},{20... | collective-permute-start | bytes 1179656 | tf_op jit(solution)/shard_map/ppermute | solution.py:583
  519.1 14.9 %collective-permute-start.57 = (bf16[64,2048]{1,0:T(8,128)(2,1)}, bf16[64,2048]{1,0:T(8,128)(2,1)}, u32[]{:S(2)}, u32[]{:S(2)}) collective-permute-start(bf16[64,2048]{1,0:T(8,128)(2,1)} %dynamic-slice_bitcast_fusion.8), channel_id=1, source_target_pairs={{0,1},{1,0},{2,3},{3,2},{4,5},{5,4},{6,7},{7,6},{8,9},{9,8},{10,11... | collective-permute-start | bytes 786440 | tf_op jit(solution)/shard_map/ppermute | solution.py:583
  522.2 14.5 %collective-permute-start.59 = (bf16[192,1024]{1,0:T(8,128)(2,1)S(1)}, bf16[192,1024]{1,0:T(8,128)(2,1)}, u32[]{:S(2)}, u32[]{:S(2)}) collective-permute-start(bf16[192,1024]{1,0:T(8,128)(2,1)S(1)} %bitcast.309), channel_id=1, source_target_pairs={{0,16},{16,0},{1,17},{17,1},{2,18},{18,2},{3,19},{19,3},{4,20},{20... | collective-permute-start | bytes 1179656 | tf_op jit(solution)/shard_map/ppermute | solution.py:583
  539.6 15.1 %collective-permute-start.60 = (bf16[64,2048]{1,0:T(8,128)(2,1)S(1)}, bf16[64,2048]{1,0:T(8,128)(2,1)S(1)}, u32[]{:S(2)}, u32[]{:S(2)}) collective-permute-start(bf16[64,2048]{1,0:T(8,128)(2,1)S(1)} %fusion.42), channel_id=1, source_target_pairs={{0,2},{1,3},{2,0},{3,1},{4,6},{5,7},{6,4},{7,5},{8,10},{9,11},{10,... | collective-permute-start | bytes 786440 | tf_op jit(solution)/shard_map/ppermute | solution.py:583
  565.4 13.9 %collective-permute-start.68 = (bf16[128,2048]{1,0:T(8,128)(2,1)S(1)}, bf16[128,2048]{1,0:T(8,128)(2,1)S(1)}, u32[]{:S(2)}, u32[]{:S(2)}) collective-permute-start(bf16[128,2048]{1,0:T(8,128)(2,1)S(1)} %bitcast.304), channel_id=1, source_target_pairs={{0,16},{16,0},{1,17},{17,1},{2,18},{18,2},{3,19},{19,3},{4,20},{20... | collective-permute-start | bytes 1572872 | tf_op jit(solution)/shard_map/ppermute | solution.py:583
  (180 other events, 1260.7 us)
Sparse Core Ops, SparseCore 0:
  9.6 43.6 all-gather.5
  55.2 48.5 all-gather.9
  105.6 70.7 all-gather.7
  219.6 87.5 reduce-scatter.4
  311.0 59.0 reduce-scatter.6
  373.7 52.7 reduce-scatter.8
  430.6 50.6 reduce-scatter.10

commit v5 on v4

--- a/solution.py
+++ b/solution.py
@@ -1013,15 +1013,12 @@
     begin(grad_states[1], grad_states[2])
     grad_gate_low = grad_gate_low.reshape(count, VD)
     grad_out = jnp.einsum("rv,rd->vd", heads_late, grad_branch, preferred_element_type=F32)
-    grad_out, r_in.value, grad_gate_low = meet(
-        [], grad_out.astype(LOW), r_in.value, grad_gate_low
+    grad_gate = jnp.einsum("rd,rc->dc", normed_low, grad_gate_low, preferred_element_type=F32)
+    mixed_a, grad_out, grad_gate, r_in.value = meet(
+        [grad_states[1], grad_states[2]],
+        back[0][0], grad_out.astype(LOW), grad_gate.astype(LOW), r_in.value,
     )
     p_out = scatter(grad_out)
-    begin(r_in)
-    grad_gate = jnp.einsum("rd,rc->dc", normed_low, grad_gate_low, preferred_element_type=F32)
-    mixed_a, grad_gate = meet(
-        [grad_states[1], grad_states[2], r_in], back[0][0], grad_gate.astype(LOW)
-    )
     r_gate = ShardSum(grad_gate)
     begin(grad_states[2], r_gate, r_in)
 
@@ -1053,24 +1050,24 @@
     begin(r_gate, r_in)
     got_b = mixer_back(1, mixed_b, 1, 2 * run, kept)
     mixed_c, pre_ab, rim_ab, tail_ab, grad_gate_low, p_down = meet(
-        [r_gate, r_in], back[2][0], *got_b[:3], grad_gate_low, p_down
+        [r_gate], back[2][0], *got_b[:3], grad_gate_low, p_down
     )
     r_down = ShardSum(p_down, ready=True)
-    begin(r_gate, r_in, r_down)
+    begin(r_gate, r_down)
     came_ab = rim_swap(rim_ab)
     grad_normed = normed_part(grad_gate_low, full_gate)
     pre_ab, came_ab, tail_ab, grad_normed = meet([], pre_ab, came_ab, tail_ab, grad_normed)
     pre_ab = with_rim(pre_ab, came_ab, tail_ab)
     grad_ab = weight_grad(pre_ab)
-    mixed_c, grad_ab = meet([r_gate, r_down], mixed_c, grad_ab)
+    mixed_c, grad_ab = meet([r_gate, r_down, r_in], mixed_c, grad_ab)
     p_ab = scatter(grad_ab)
-    begin(r_gate, r_down)
+    begin(r_gate, r_down, r_in)
     got_c = mixer_back(2, mixed_c, 0, run, [])
     pre_c, rim_c, tail_c, pre_ab, grad_normed, p_out = meet(
         [r_in, r_gate, r_down], *got_c[:3], pre_ab, grad_normed, p_out
     )
     r_out = ShardSum(p_out, ready=True)
-    begin(r_gate, r_down, r_out)
+    begin(r_in, r_gate, r_down, r_out)
     came_c = rim_swap(rim_c)
     grad_normed = grad_normed + normed_part(pre_ab[:, :run], full_qkv[0])
     pre_c, came_c, tail_c, grad_normed = meet([], pre_c, came_c, tail_c, grad_normed)
@@ -1085,7 +1082,7 @@
     grad_normed = grad_normed + normed_part(pre_c, full_qkv[2])
     made_late = [item for got in (got_a, got_b, got_c) for item in got[3:5]]
     hidden_late, grad_normed, p_ab, *made_late = meet(
-        [sum_c, r_out, r_gate],
+        [sum_c, r_out, r_gate, r_in],
         hidden_late, grad_normed, p_ab, *made_late, *[item[2] for item in back],
     )
     sum_ab = ShardSum(p_ab, ready=True)

time: 601 us -> 632 us (1.052)
  waiting for transfers between devices: 80 us -> 92.4 us
  local copies, waits for them, and re-layouts: 58.1 us -> 66 us
    ppermute x52, waiting for transfers between devices: 57.4 us -> 78.5 us  [swap(): return lax.ppermute(values, axis, [(at, at ^ bit) for at in range(count)])]
    reduce_scatter x1, waiting for transfers between devices: 8.71 us -> 0.01 us  [__init__(): lax.psum_scatter(self.value, ('fsdp', 'dp'), scatter_dimension=0, tiled=T...]
    unnamed x317 -> x341, local copies, waits for them, and re-layouts: 35.1 us -> 37.9 us
  transfers between devices with their start and end apart: 81 -> 81, of which waited for: 20 -> 17; matrix products, arithmetic and copies ran while one was open for 33% -> 34% of each run, Pallas kernels for 22% -> 21%
where the time goes in v5:
time: 632 us; the launch traced here: 627 us
  Pallas kernels  157 us (25%)
  matrix products  122 us (19%)
  starting transfers between devices  98.3 us (16%)
  waiting for transfers between devices  92.4 us (15%)
  other arithmetic  74.3 us (12%)
  local copies, waits for them, and re-layouts  66 us (10%)
  between operations  17 us (3%)
    ppermute x52, waiting for transfers between devices, swap(): return lax.ppermute(values, axis, [(at, at ^ bit) for at in range(count)])  78.5 us
    pallas_call x3, Pallas kernels, mixer_backward(): pl.pallas_call(kernel, grid=(heads,), in_specs=head_specs(seqs, count, fi...  61.2 us
    ppermute x52, starting transfers between devices, swap(): return lax.ppermute(values, axis, [(at, at ^ bit) for at in range(count)])  58.1 us
    pallas_call x3, Pallas kernels, mixer_forward(): pl.pallas_call(forward_kernel, grid=(heads,), in_specs=head_specs(seqs, c...  38.7 us
    unnamed x341, local copies, waits for them, and re-layouts  37.9 us
    ppermute x18, starting transfers between devices, leave(): return lax.ppermute(leaving.astype(LOW), 'seq', [(hop, hop + step)])  29.3 us
    pallas_call x1, Pallas kernels, ffn_middle(): pl.pallas_call(ffn_kernel, grid=(tiles,), in_specs=[pl.BlockSpec((rows, w...  24.8 us
    convert_element_type x18, other arithmetic, plus(): return (left.astype(F32) + right.astype(F32)).astype(LOW)  20.7 us
  transfers between devices with their start and end apart: 81, of which 17 were waited for; matrix products, arithmetic and copies ran while one was open for 34% of the time, Pallas kernels for 21%

profile of v5, /device:TPU:0, one launch (start us, length us, event | category | flops | bytes accessed | tf_op | source)
XLA Modules:
  0.0 627.0 jit_solution(9374935139870632837)
XLA Ops:
  15.2 3.7 collective-permute-start.4
  25.9 3.5 collective-permute-start.3
  35.1 3.0 fusion.6
  41.1 5.1 collective-permute-done.5.refs_2_
  53.2 3.0 convolution_convert_fusion.5.q_ref.k_ref.v_ref.rq_ref.rk_ref.rv_ref.refs_0_.refs_1_.refs_2_.refs_3_.refs_4_.refs_5_
  56.2 12.9 %mixer_forward.3 = (bf16[2,3,256,256]{3,2,1,0:T(8,128)(2,1)S(1)}, bf16[2,3,256,384]{3,2,1,0:T(8,128)(2,1)S(1)}, f32[3,256,512]{2,1,0:T(8,128)S(1)}, bf16[3,256,2...) custom-call(bf16[784,1024]{1,0:T(8,128)(2,1)} %convolution_convert_fusion.5.q_ref.k_ref.v_, ...), custom_call_target="tpu_custom_call" | custom-call | tf_op jit(solution)/shard_map/mixer_forward/pallas_call | solution.py:324
  72.9 3.8 collective-permute-start.12
  79.5 3.0 convolution_convert_fusion.4.q_ref.k_ref.v_ref.rq_ref.rk_ref.rv_ref.refs_0_.refs_1_.refs_2_.refs_3_.refs_4_.refs_5_
  82.6 12.9 %mixer_forward.4 = (bf16[2,3,256,256]{3,2,1,0:T(8,128)(2,1)S(1)}, bf16[2,3,256,384]{3,2,1,0:T(8,128)(2,1)S(1)}, f32[3,256,512]{2,1,0:T(8,128)S(1)}, bf16[3,256,2...) custom-call(bf16[784,1024]{1,0:T(8,128)(2,1)} %convolution_convert_fusion.4.q_ref.k_ref.v_, ...), custom_call_target="tpu_custom_call" | custom-call | tf_op jit(solution)/shard_map/mixer_forward/pallas_call | solution.py:324
  98.0 4.2 collective-permute-start.16
  105.2 3.0 convolution_convert_fusion.3.q_ref.k_ref.v_ref.rq_ref.rk_ref.rv_ref.refs_0_.refs_1_.refs_2_.refs_3_.refs_4_.refs_5_
  108.2 12.9 %mixer_forward.5 = (bf16[2,3,256,256]{3,2,1,0:T(8,128)(2,1)S(1)}, bf16[2,3,256,384]{3,2,1,0:T(8,128)(2,1)S(1)}, f32[3,256,512]{2,1,0:T(8,128)S(1)}, bf16[3,256,2...) custom-call(bf16[784,1024]{1,0:T(8,128)(2,1)} %convolution_convert_fusion.3.q_ref.k_ref.v_, ...), custom_call_target="tpu_custom_call" | custom-call | tf_op jit(solution)/shard_map/mixer_forward/pallas_call | solution.py:324
  129.2 7.2 %fusion.81 = f32[768,1536]{1,0:T(8,128)} fusion(bf16[768,1024]{1,0:T(8,128)(2,1)} %fusion.6, bf16[1024,1536]{1,0:T(8,128)(2,1)} %all-gather.6.cloned.1.call-done), kind=kOutput, calls=%fused_computation.223 | convolution fusion | flops 2415919104 | bytes 9437184 | tf_op jit(solution)/shard_map/dot_general | solution.py:954
  157.2 4.1 assemble.7
  170.4 5.9 all-gather.8.cloned.1.call-done
  179.1 24.8 %ffn_middle.1 = (bf16[768,2816]{1,0:T(8,128)(2,1)}, bf16[768,5632]{1,0:T(8,128)(2,1)}) custom-call(bf16[768,1024]{1,0:T(8,128)(2,1)S(1)} %copy-done.10, bf16[1024,5632]{1,0:T(8,128)(2,1)} %bitcast.287, bf16[1024,5632]{1,0:T(8,128)(2,1)} %bitcast.288, bf16[768,1024]{1,0:T(8,128)(2,1)S(1)} %bitcast.276, bf16[2816,1024]{1,0:T(8,128)(2,1)} %bitcast.295), custom_call_target="tpu_custom_call" | custom-call | tf_op jit(solution)/shard_map/ffn_middle/pallas_call | solution.py:507
  203.9 15.4 %convolution_convert_fusion = bf16[1024,5632]{1,0:T(8,128)(2,1)} fusion(bf16[768,1024]{1,0:T(8,128)(2,1)S(1)} %copy-done.10, bf16[768,5632]{1,0:T(8,128)(2,1)} %get-tuple-element.239), kind=kOutput, calls=%fused_computation | convolution fusion | flops 8864137216 | bytes 21757952 | tf_op jit(solution)/shard_map/rd,rf->df/dot_general | solution.py:971
  219.6 17.1 %multiply_reduce_fusion = (f32[1024]{0:T(1024)}, f32[768]{0:T(1024)S(1)}, f32[768,1024]{1,0:T(8,128)}) fusion(f32[768,1024]{1,0:T(8,128)} %copy-done.81, f32[768]{0:T(1024)S(1)} %fusion.66, f32[1024]{0:T(1024)S(1)} %bitcast.360, bf16[768,5632]{1,0:T(8,128)(2,1)} %get-tuple-element.239, bf16[1,1024,5632]{2,1,0:T(8,128)(2,1)} %all-gather.8.cloned.1.call-done), kind=kOutput, calls=%fused_computation.27 | convolution fusion | flops 8863086592 | bytes 26490880 | tf_op jit(solution)/shard_map/rf,df->rd/dot_general | solution.py:976
  236.7 3.1 fusion
  240.0 4.4 fusion.34
  244.4 5.3 heads_backward.3
  250.7 5.1 heads_backward.4
  258.6 5.4 heads_backward.5
  271.5 8.7 %convolution_convert_fusion.1 = bf16[2816,1024]{1,0:T(8,128)(2,1)} fusion(bf16[768,2816]{1,0:T(8,128)(2,1)} %get-tuple-element.338, bf16[768,1024]{1,0:T(8,128)(2,1)S(1)} %bitcast.277), kind=kOutput, calls=%fused_computation.3 | convolution fusion | flops 4432068608 | bytes 11665408 | tf_op jit(solution)/shard_map/rf,rd->fd/dot_general | solution.py:1008
  280.2 6.8 %collective-permute-done.29 = bf16[2,3,128,256]{3,2,1,0:T(8,128)(2,1)} collective-permute-done((bf16[2,3,128,256]{3,2,1,0:T(8,128)(2,1)}, bf16[2,3,128,256]{3,2,1,0:T(8,128)(2,1)}, u32[]{:S(2)}, u32[]{:S(2)}) %collective-permute-start.29) | collective-permute-done | bytes 393248 | tf_op jit(solution)/shard_map/ppermute | solution.py:717
  296.7 4.0 convolution_convert_fusion.2
  300.7 6.6 %bitcast_convert_fusion.1 = bf16[1024,1536]{1,0:T(8,128)(2,1)} fusion(bf16[3,256,1536]{2,1,0:T(8,128)(2,1)} %get-tuple-element.263, bf16[3,256,1024]{2,1,0:T(8,128)(2,1)} %param.15, f32[1024]{0:T(1024)S(1)} %bitcast.352, f32[3,256]{1,0:T(4,128)S(1)} %copy-done.141), kind=kOutput, calls=%fused_computation.2 | convolution fusion | flops 2420637696 | bytes 7085056 | tf_op jit(solution)/shard_map/rd,rc->dc/dot_general | solution.py:1016
  307.4 2.8 dynamic-slice_bitcast_fusion
  311.0 5.9 collective-permute-start.36
  327.8 20.8 %mixer_backward.3 = (bf16[3,256,2048]{2,1,0:T(8,128)(2,1)}, f32[3,8,2048]{2,1,0:T(8,128)S(1)}, f32[3,8,2048]{2,1,0:T(8,128)S(1)}, f32[4,1024]{1,0:T(4,128)S(1)}, f32[2,3,8,256]{3,2,1,0:T(8,128)S(1)}) custom-call(bf16[784,1024]{1,0:T(8,128)(2,1)S(1)} %copy-done.3, bf16[784,1024]{1,0:T(8,128)(2,1)S(1)} %copy-done.3, bf16[784,1024]{1,0:T(8,128)(2,1)S(1)} %copy-done.3, ...), custom_call_target="tpu_custom_call" | custom-call | tf_op jit(solution)/shard_map/mixer_backward/pallas_call | solution.py:442
  357.6 20.9 %mixer_backward.4 = (bf16[3,256,2048]{2,1,0:T(8,128)(2,1)}, f32[3,8,2048]{2,1,0:T(8,128)S(1)}, f32[3,8,2048]{2,1,0:T(8,128)S(1)}, f32[4,1024]{1,0:T(4,128)S(1)}, f32[2,3,8,256]{3,2,1,0:T(8,128)S(1)}) custom-call(bf16[784,1024]{1,0:T(8,128)(2,1)S(1)} %copy-done.2, ...), custom_call_target="tpu_custom_call", output_to_operand_aliasing={{0}: (16, {}), {1}: (17, {}), {2}: (18, {})} | custom-call | tf_op jit(solution)/shard_map/mixer_backward/pallas_call | solution.py:442
  385.2 3.5 collective-permute-start.40
  388.7 6.5 %fusion.82 = f32[768,1024]{1,0:T(8,128)} fusion(bf16[768,1536]{1,0:T(8,128)(2,1)S(1)} %bitcast.292, bf16[1024,1536]{1,0:T(8,128)(2,1)} %all-gather.6.cloned.1.call-done), kind=kOutput, calls=%fused_computation.224 | convolution fusion | flops 2415919104 | bytes 8650752 | tf_op jit(solution)/shard_map/rc,dc->rd/dot_general | solution.py:1046
  397.3 7.3 %bitcast_convert_fusion = bf16[1024,2048]{1,0:T(8,128)(2,1)} fusion(bf16[3,256,2048]{2,1,0:T(8,128)(2,1)} %dynamic_update_slice.22, bf16[3,256,1024]{2,1,0:T(8,128)(2,1)S(1)} %copy-done.77, f32[1024]{0:T(1024)S(1)} %bitcast.353, f32[3,256]{1,0:T(4,128)S(1)} %copy-done.142), kind=kOutput, calls=%fused_computation.1 | convolution fusion | flops 3226468352 | bytes 8920064 | tf_op jit(solution)/shard_map/rd,rc->dc/dot_general | solution.py:1043
  408.9 3.5 collective-permute-start.44
  416.9 19.5 %mixer_backward.5 = (bf16[3,256,1024]{2,1,0:T(8,128)(2,1)S(1)}, f32[3,8,1024]{2,1,0:T(8,128)S(1)}, f32[3,8,1024]{2,1,0:T(8,128)S(1)}, f32[4,1024]{1,0:T(4,128)S(1)}, f32[2,3,8,256]{3,2,1,0:T(8,128)S(1)}) custom-call(bf16[784,1024]{1,0:T(8,128)(2,1)} %convolution_convert_fusion.3.q_ref.k_ref.v_ref.rq_ref.rk_ref.rv_ref.refs_0_.refs_1_.refs_2_.refs_3_.refs_4_.refs_5_, ...), custom_call_target="tpu_custom_call" | custom-call | tf_op jit(solution)/shard_map/mixer_backward/pallas_call | solution.py:442
  442.6 3.6 collective-permute-start.46
  451.7 3.2 maximum_select_fusion.1
  454.9 3.4 fusion.16
  482.5 27.8 %collective-permute-done.55 = bf16[128,5632]{1,0:T(8,128)(2,1)S(1)} collective-permute-done((bf16[128,5632]{1,0:T(8,128)(2,1)S(1)}, bf16[128,5632]{1,0:T(8,128)(2,1)S(1)}, u32[]{:S(2)}, u32[]{:S(2)}) %collective-permute-start.55) | collective-permute-done | bytes 1441824 | tf_op jit(solution)/shard_map/ppermute | solution.py:583
  510.3 22.6 %collective-permute-done.54 = bf16[128,1536]{1,0:T(8,128)(2,1)S(1)} collective-permute-done((bf16[128,1536]{1,0:T(8,128)(2,1)S(1)}, bf16[128,1536]{1,0:T(8,128)(2,1)S(1)}, u32[]{:S(2)}, u32[]{:S(2)}) %collective-permute-start.54) | collective-permute-done | bytes 393248 | tf_op jit(solution)/shard_map/ppermute | solution.py:583
  534.6 2.8 fusion.7
  550.4 3.8 bitcast_convert_fusion.3
  558.8 5.7 add_convert_fusion
  576.2 5.3 collective-permute-done.61
  581.5 3.7 collective-permute-done.60
  585.4 2.8 collective-permute-start.66
  604.1 5.2 collective-permute-done.71
  (676 shorter events, 234.6 us)
Async XLA Ops:
  7.2 122.0 %all-gather.6.cloned.1.call-start = ((), (), s32[]{:S(2)}) async-start(), calls=%async_computation.4 | async-start | bytes 3932160 | tf_op jit(solution)/shard_map/all_gather | solution.py:900
  7.9 162.5 %all-gather.10.cloned.1.call-start = ((), (), s32[]{:S(2)}) async-start(), calls=%async_computation.10 | async-start | bytes 6488064 | tf_op jit(solution)/shard_map/all_gather | solution.py:782
  10.2 166.1 %all-gather.8.cloned.1.call-start = ((), (), s32[]{:S(2)}) async-start(), calls=%async_computation.9 | async-start | bytes 12976128 | tf_op jit(solution)/shard_map/all_gather | solution.py:782
  11.5 295.8 %reduce-scatter.5.cloned.1.call-start = ((), (), s32[]{:S(2)}) async-start(), calls=%async_computation.5 | async-start | bytes 12976128 | tf_op jit(solution)/shard_map/reduce_scatter | solution.py:656
  12.5 17.2 %collective-permute-start.1 = (bf16[6720]{0:T(1024)(128)(2,1)S(1)}, bf16[6720]{0:T(1024)(128)(2,1)S(1)}, u32[]{:S(2)}, u32[]{:S(2)}) collective-permute-start(bf16[6720]{0:T(1024)(128)(2,1)S(1)} %concatenate.36), channel_id=1, source_target_pairs={{0,8},{4,12},{8,0},{12,4},{1,9},{5,13},{9,1},{13,5},{2,10},{6,14},... | collective-permute-start | bytes 40328 | tf_op jit(solution)/shard_map/ppermute | solution.py:583
  15.1 14.9 %collective-permute-start.2 = (bf16[6720]{0:T(1024)(128)(2,1)S(1)}, bf16[6720]{0:T(1024)(128)(2,1)S(1)}, u32[]{:S(2)}, u32[]{:S(2)}) collective-permute-start(bf16[6720]{0:T(1024)(128)(2,1)S(1)} %concatenate.36), channel_id=1, source_target_pairs={{0,12},{4,8},{8,4},{12,0},{1,13},{5,9},{9,5},{13,1},{2,14},{6,10},... | collective-permute-start | bytes 40328 | tf_op jit(solution)/shard_map/ppermute | solution.py:583
  20.6 25.6 %collective-permute-start.5 = (bf16[256,1024]{1,0:T(8,128)(2,1)S(1)}, bf16[256,1024]{1,0:T(8,128)(2,1)S(1)}, u32[]{:S(2)}, u32[]{:S(2)}) collective-permute-start(bf16[256,1024]{1,0:T(8,128)(2,1)S(1)} %get-tuple-element.195.refs_0_), channel_id=1, source_target_pairs={{0,8},{4,12},{8,0},{12,4},{1,9},{5,13},{9,1},{13,5},{2,10},{6,14},... | collective-permute-start | bytes 1572872 | tf_op jit(solution)/shard_map/ppermute | solution.py:583
  25.6 24.8 %collective-permute-start.6 = (bf16[256,1024]{1,0:T(8,128)(2,1)S(1)}, bf16[256,1024]{1,0:T(8,128)(2,1)S(1)}, u32[]{:S(2)}, u32[]{:S(2)}) collective-permute-start(bf16[256,1024]{1,0:T(8,128)(2,1)S(1)} %get-tuple-element.195.refs_0_), channel_id=1, source_target_pairs={{0,4},{4,0},{8,12},{12,8},{1,5},{5,1},{9,13},{13,9},{2,6},{6,2},{1... | collective-permute-start | bytes 1572872 | tf_op jit(solution)/shard_map/ppermute | solution.py:583
  46.3 25.9 %collective-permute-start.8 = (bf16[256,1024]{1,0:T(8,128)(2,1)S(1)}, bf16[256,1024]{1,0:T(8,128)(2,1)}, u32[]{:S(2)}, u32[]{:S(2)}) collective-permute-start(bf16[256,1024]{1,0:T(8,128)(2,1)S(1)} %get-tuple-element.201.refs_0_), channel_id=1, source_target_pairs={{0,8},{4,12},{8,0},{12,4},{1,9},{5,13},{9,1},{13,5},{2,10},{6,14},... | collective-permute-start | bytes 1572872 | tf_op jit(solution)/shard_map/ppermute | solution.py:583
  48.1 28.6 %collective-permute-start.9 = (bf16[256,1024]{1,0:T(8,128)(2,1)S(1)}, bf16[256,1024]{1,0:T(8,128)(2,1)}, u32[]{:S(2)}, u32[]{:S(2)}) collective-permute-start(bf16[256,1024]{1,0:T(8,128)(2,1)S(1)} %get-tuple-element.201.refs_0_), channel_id=1, source_target_pairs={{0,4},{4,0},{8,12},{12,8},{1,5},{5,1},{9,13},{13,9},{2,6},{6,2},{1... | collective-permute-start | bytes 1572872 | tf_op jit(solution)/shard_map/ppermute | solution.py:583
  72.5 24.2 %collective-permute-start.11 = (bf16[256,1024]{1,0:T(8,128)(2,1)S(1)}, bf16[256,1024]{1,0:T(8,128)(2,1)S(1)}, u32[]{:S(2)}, u32[]{:S(2)}) collective-permute-start(bf16[256,1024]{1,0:T(8,128)(2,1)S(1)} %get-tuple-element.205.refs_0_), channel_id=1, source_target_pairs={{0,8},{4,12},{8,0},{12,4},{1,9},{5,13},{9,1},{13,5},{2,10},{6,14},... | collective-permute-start | bytes 1572872 | tf_op jit(solution)/shard_map/ppermute | solution.py:583
  72.8 30.8 %collective-permute-start.13 = (bf16[256,1024]{1,0:T(8,128)(2,1)S(1)}, bf16[256,1024]{1,0:T(8,128)(2,1)S(1)}, u32[]{:S(2)}, u32[]{:S(2)}) collective-permute-start(bf16[256,1024]{1,0:T(8,128)(2,1)S(1)} %get-tuple-element.205.refs_0_), channel_id=1, source_target_pairs={{0,4},{4,0},{8,12},{12,8},{1,5},{5,1},{9,13},{13,9},{2,6},{6,2},{1... | collective-permute-start | bytes 1572872 | tf_op jit(solution)/shard_map/ppermute | solution.py:583
  72.9 23.8 %collective-permute-start.12 = (bf16[2,3,128,256]{3,2,1,0:T(8,128)(2,1)S(1)}, bf16[2,3,128,256]{3,2,1,0:T(8,128)(2,1)S(1)}, u32[]{:S(2)}, u32[]{:S(2)}) collective-permute-start(bf16[2,3,128,256]{3,2,1,0:T(8,128)(2,1)S(1)} %convert_element_type.431), channel_id=1, source_target_pairs={{0,1},{4,5},{8,9},{12,13},{16,17},{20,21},{24,25},{28,29}} | collective-permute-start | bytes 1179656 | tf_op jit(solution)/shard_map/ppermute | solution.py:717
  97.2 23.9 %collective-permute-start.15 = (bf16[2,3,128,256]{3,2,1,0:T(8,128)(2,1)S(1)}, bf16[2,3,128,256]{3,2,1,0:T(8,128)(2,1)S(1)}, u32[]{:S(2)}, u32[]{:S(2)}) collective-permute-start(bf16[2,3,128,256]{3,2,1,0:T(8,128)(2,1)S(1)} %fusion.19), channel_id=1, source_target_pairs={{1,2},{5,6},{9,10},{13,14},{17,18},{21,22},{25,26},{29,30}} | collective-permute-start | bytes 1179656 | tf_op jit(solution)/shard_map/ppermute | solution.py:717
  98.0 23.2 %collective-permute-start.16 = (bf16[2,3,128,256]{3,2,1,0:T(8,128)(2,1)S(1)}, bf16[2,3,128,256]{3,2,1,0:T(8,128)(2,1)S(1)}, u32[]{:S(2)}, u32[]{:S(2)}) collective-permute-start(bf16[2,3,128,256]{3,2,1,0:T(8,128)(2,1)S(1)} %convert_element_type.434), channel_id=1, source_target_pairs={{0,1},{4,5},{8,9},{12,13},{16,17},{20,21},{24,25},{28,29}} | collective-permute-start | bytes 1179656 | tf_op jit(solution)/shard_map/ppermute | solution.py:717
  102.2 34.2 %collective-permute-start.20 = (bf16[384,1024]{1,0:T(8,128)(2,1)}, bf16[384,1024]{1,0:T(8,128)(2,1)}, u32[]{:S(2)}, u32[]{:S(2)}) collective-permute-start(bf16[384,1024]{1,0:T(8,128)(2,1)} %refs_0_), channel_id=1, source_target_pairs={{0,8},{4,12},{8,0},{12,4},{1,9},{5,13},{9,1},{13,5},{2,10},{6,14},... | collective-permute-start | bytes 2359304 | tf_op jit(solution)/shard_map/ppermute | solution.py:583
  121.6 14.8 %collective-permute-start.17 = (bf16[2,3,128,256]{3,2,1,0:T(8,128)(2,1)S(1)}, bf16[2,3,128,256]{3,2,1,0:T(8,128)(2,1)}, u32[]{:S(2)}, u32[]{:S(2)}) collective-permute-start(bf16[2,3,128,256]{3,2,1,0:T(8,128)(2,1)S(1)} %fusion.20), channel_id=1, source_target_pairs={{2,3},{6,7},{10,11},{14,15},{18,19},{22,23},{26,27},{30,31}} | collective-permute-start | bytes 1179656 | tf_op jit(solution)/shard_map/ppermute | solution.py:717
  219.3 159.8 %reduce-scatter.7.cloned.1.call-start = ((), (), s32[]{:S(2)}) async-start(), calls=%async_computation.6 | async-start | bytes 6488064 | tf_op jit(solution)/shard_map/reduce_scatter | solution.py:639
  264.9 15.4 %collective-permute-start.31 = (bf16[2,3,128,256]{3,2,1,0:T(8,128)(2,1)}, bf16[2,3,128,256]{3,2,1,0:T(8,128)(2,1)}, u32[]{:S(2)}, u32[]{:S(2)}) collective-permute-start(bf16[2,3,128,256]{3,2,1,0:T(8,128)(2,1)} %convert_element_type.455), channel_id=1, source_target_pairs={{3,2},{7,6},{11,10},{15,14},{19,18},{23,22},{27,26},{31,30}} | collective-permute-start | bytes 1179656 | tf_op jit(solution)/shard_map/ppermute | solution.py:717
  267.5 19.5 %collective-permute-start.29 = (bf16[2,3,128,256]{3,2,1,0:T(8,128)(2,1)}, bf16[2,3,128,256]{3,2,1,0:T(8,128)(2,1)}, u32[]{:S(2)}, u32[]{:S(2)}) collective-permute-start(bf16[2,3,128,256]{3,2,1,0:T(8,128)(2,1)} %fusion.26), channel_id=1, source_target_pairs={{1,0},{5,4},{9,8},{13,12},{17,16},{21,20},{25,24},{29,28}} | collective-permute-start | bytes 1179656 | tf_op jit(solution)/shard_map/ppermute | solution.py:717
  269.9 17.2 %collective-permute-start.30 = (bf16[2,3,128,256]{3,2,1,0:T(8,128)(2,1)}, bf16[2,3,128,256]{3,2,1,0:T(8,128)(2,1)}, u32[]{:S(2)}, u32[]{:S(2)}) collective-permute-start(bf16[2,3,128,256]{3,2,1,0:T(8,128)(2,1)} %fusion.27), channel_id=1, source_target_pairs={{2,1},{6,5},{10,9},{14,13},{18,17},{22,21},{26,25},{30,29}} | collective-permute-start | bytes 1179656 | tf_op jit(solution)/shard_map/ppermute | solution.py:717
  287.0 151.2 %reduce-scatter.9.cloned.1.call-start = ((), (), s32[]{:S(2)}) async-start(), calls=%async_computation.7 | async-start | bytes 3538944 | tf_op jit(solution)/shard_map/reduce_scatter | solution.py:639
  291.8 15.6 %collective-permute-start.32 = (bf16[2,3,128,256]{3,2,1,0:T(8,128)(2,1)}, bf16[2,3,128,256]{3,2,1,0:T(8,128)(2,1)}, u32[]{:S(2)}, u32[]{:S(2)}) collective-permute-start(bf16[2,3,128,256]{3,2,1,0:T(8,128)(2,1)} %fusion.28), channel_id=1, source_target_pairs={{1,0},{5,4},{9,8},{13,12},{17,16},{21,20},{25,24},{29,28}} | collective-permute-start | bytes 1179656 | tf_op jit(solution)/shard_map/ppermute | solution.py:717
  310.1 38.5 %collective-permute-start.35 = (bf16[2,256,1536]{2,1,0:T(8,128)(2,1)}, bf16[2,256,1536]{2,1,0:T(8,128)(2,1)}, u32[]{:S(2)}, u32[]{:S(2)}) collective-permute-start(bf16[2,256,1536]{2,1,0:T(8,128)(2,1)} %dynamic-slice_bitcast_fusion), channel_id=1, source_target_pairs={{0,4},{4,0},{8,12},{12,8},{1,5},{5,1},{9,13},{13,9},{2,6},{6,2},{1... | collective-permute-start | bytes 4718600 | tf_op jit(solution)/shard_map/ppermute | solution.py:583
  311.0 37.6 %collective-permute-start.36 = (bf16[64,5632]{1,0:T(8,128)(2,1)}, bf16[64,5632]{1,0:T(8,128)(2,1)}, u32[]{:S(2)}, u32[]{:S(2)}) collective-permute-start(bf16[64,5632]{1,0:T(8,128)(2,1)} %dynamic-slice_bitcast_fusion.3), channel_id=1, source_target_pairs={{0,1},{1,0},{2,3},{3,2},{4,5},{5,4},{6,7},{7,6},{8,9},{9,8},{10,11... | collective-permute-start | bytes 2162696 | tf_op jit(solution)/shard_map/ppermute | solution.py:583
  319.3 29.3 %collective-permute-start.34 = (bf16[2,3,128,256]{3,2,1,0:T(8,128)(2,1)}, bf16[2,3,128,256]{3,2,1,0:T(8,128)(2,1)}, u32[]{:S(2)}, u32[]{:S(2)}) collective-permute-start(bf16[2,3,128,256]{3,2,1,0:T(8,128)(2,1)} %fusion.30), channel_id=1, source_target_pairs={{1,0},{5,4},{9,8},{13,12},{17,16},{21,20},{25,24},{29,28}} | collective-permute-start | bytes 1179656 | tf_op jit(solution)/shard_map/ppermute | solution.py:717
  323.6 210.1 %reduce-scatter.11.cloned.1.call-start = ((), (), s32[]{:S(2)}) async-start(), calls=%async_computation.8 | async-start | bytes 4718592 | tf_op jit(solution)/shard_map/reduce_scatter | solution.py:639
  351.6 27.7 %collective-permute-start.37 = (bf16[256,1536]{1,0:T(8,128)(2,1)}, bf16[256,1536]{1,0:T(8,128)(2,1)}, u32[]{:S(2)}, u32[]{:S(2)}) collective-permute-start(bf16[256,1536]{1,0:T(8,128)(2,1)} %dynamic-slice_bitcast_fusion.2), channel_id=1, source_target_pairs={{0,8},{4,12},{8,0},{12,4},{1,9},{5,13},{9,1},{13,5},{2,10},{6,14},... | collective-permute-start | bytes 2359304 | tf_op jit(solution)/shard_map/ppermute | solution.py:583
  354.9 49.7 %collective-permute-start.41 = (bf16[64,5632]{1,0:T(8,128)(2,1)}, bf16[64,5632]{1,0:T(8,128)(2,1)}, u32[]{:S(2)}, u32[]{:S(2)}) collective-permute-start(bf16[64,5632]{1,0:T(8,128)(2,1)} %fusion.18), channel_id=1, source_target_pairs={{0,2},{1,3},{2,0},{3,1},{4,6},{5,7},{6,4},{7,5},{8,10},{9,11},{10,... | collective-permute-start | bytes 2162696 | tf_op jit(solution)/shard_map/ppermute | solution.py:583
  379.3 15.9 %collective-permute-start.38 = (bf16[3,3,2048]{2,1,0:T(4,128)(2,1)S(1)}, bf16[3,3,2048]{2,1,0:T(4,128)(2,1)S(1)}, u32[]{:S(2)}, u32[]{:S(2)}) collective-permute-start(bf16[3,3,2048]{2,1,0:T(4,128)(2,1)S(1)} %slice.293), channel_id=1, source_target_pairs={{1,0},{2,1},{3,2},{5,4},{6,5},{7,6},{9,8},{10,9},{11,10},{13,12},{... | collective-permute-start | bytes 110600 | tf_op jit(solution)/shard_map/ppermute | solution.py:41
  382.9 21.6 %collective-permute-start.39 = (bf16[128,1536]{1,0:T(8,128)(2,1)}, bf16[128,1536]{1,0:T(8,128)(2,1)}, u32[]{:S(2)}, u32[]{:S(2)}) collective-permute-start(bf16[128,1536]{1,0:T(8,128)(2,1)} %dynamic-slice_bitcast_fusion.5), channel_id=1, source_target_pairs={{0,16},{16,0},{1,17},{17,1},{2,18},{18,2},{3,19},{19,3},{4,20},{20... | collective-permute-start | bytes 1179656 | tf_op jit(solution)/shard_map/ppermute | solution.py:583
  385.2 19.3 %collective-permute-start.40 = (bf16[176,1024]{1,0:T(8,128)(2,1)}, bf16[176,1024]{1,0:T(8,128)(2,1)}, u32[]{:S(2)}, u32[]{:S(2)}) collective-permute-start(bf16[176,1024]{1,0:T(8,128)(2,1)} %dynamic-slice_bitcast_fusion.6), channel_id=1, source_target_pairs={{0,1},{1,0},{2,3},{3,2},{4,5},{5,4},{6,7},{7,6},{8,9},{9,8},{10,11... | collective-permute-start | bytes 1081352 | tf_op jit(solution)/shard_map/ppermute | solution.py:583
  406.9 31.3 %collective-permute-start.42 = (bf16[64,5632]{1,0:T(8,128)(2,1)}, bf16[64,5632]{1,0:T(8,128)(2,1)}, u32[]{:S(2)}, u32[]{:S(2)}) collective-permute-start(bf16[64,5632]{1,0:T(8,128)(2,1)} %add_convert_fusion.1), channel_id=1, source_target_pairs={{0,1},{1,0},{2,3},{3,2},{4,5},{5,4},{6,7},{7,6},{8,9},{9,8},{10,11... | collective-permute-start | bytes 2162696 | tf_op jit(solution)/shard_map/ppermute | solution.py:583
  408.9 29.3 %collective-permute-start.44 = (bf16[176,1024]{1,0:T(8,128)(2,1)}, bf16[176,1024]{1,0:T(8,128)(2,1)}, u32[]{:S(2)}, u32[]{:S(2)}) collective-permute-start(bf16[176,1024]{1,0:T(8,128)(2,1)} %fusion.36), channel_id=1, source_target_pairs={{0,2},{1,3},{2,0},{3,1},{4,6},{5,7},{6,4},{7,5},{8,10},{9,11},{10,... | collective-permute-start | bytes 1081352 | tf_op jit(solution)/shard_map/ppermute | solution.py:583
  415.1 23.1 %collective-permute-start.43 = (bf16[64,1536]{1,0:T(8,128)(2,1)}, bf16[64,1536]{1,0:T(8,128)(2,1)}, u32[]{:S(2)}, u32[]{:S(2)}) collective-permute-start(bf16[64,1536]{1,0:T(8,128)(2,1)} %dynamic-slice_bitcast_fusion.10), channel_id=1, source_target_pairs={{0,1},{1,0},{2,3},{3,2},{4,5},{5,4},{6,7},{7,6},{8,9},{9,8},{10,11... | collective-permute-start | bytes 589832 | tf_op jit(solution)/shard_map/ppermute | solution.py:583
  439.3 21.8 %collective-permute-start.45 = (bf16[3,3,1024]{2,1,0:T(4,128)(2,1)S(1)}, bf16[3,3,1024]{2,1,0:T(4,128)(2,1)S(1)}, u32[]{:S(2)}, u32[]{:S(2)}) collective-permute-start(bf16[3,3,1024]{2,1,0:T(4,128)(2,1)S(1)} %slice.294), channel_id=1, source_target_pairs={{1,0},{2,1},{3,2},{5,4},{6,5},{7,6},{9,8},{10,9},{11,10},{13,12},{... | collective-permute-start | bytes 55304 | tf_op jit(solution)/shard_map/ppermute | solution.py:41
  442.6 20.8 %collective-permute-start.46 = (bf16[64,1536]{1,0:T(8,128)(2,1)}, bf16[64,1536]{1,0:T(8,128)(2,1)}, u32[]{:S(2)}, u32[]{:S(2)}) collective-permute-start(bf16[64,1536]{1,0:T(8,128)(2,1)} %fusion.45), channel_id=1, source_target_pairs={{0,2},{1,3},{2,0},{3,1},{4,6},{5,7},{6,4},{7,5},{8,10},{9,11},{10,... | collective-permute-start | bytes 589832 | tf_op jit(solution)/shard_map/ppermute | solution.py:583
  448.1 15.3 %collective-permute-start.47 = (bf16[176,1024]{1,0:T(8,128)(2,1)}, bf16[176,1024]{1,0:T(8,128)(2,1)}, u32[]{:S(2)}, u32[]{:S(2)}) collective-permute-start(bf16[176,1024]{1,0:T(8,128)(2,1)} %add_convert_fusion.2), channel_id=1, source_target_pairs={{0,1},{1,0},{2,3},{3,2},{4,5},{5,4},{6,7},{7,6},{8,9},{9,8},{10,11... | collective-permute-start | bytes 1081352 | tf_op jit(solution)/shard_map/ppermute | solution.py:583
  463.5 14.0 %collective-permute-start.49 = (bf16[2,256,1024]{2,1,0:T(8,128)(2,1)S(1)}, bf16[2,256,1024]{2,1,0:T(8,128)(2,1)S(1)}, u32[]{:S(2)}, u32[]{:S(2)}) collective-permute-start(bf16[2,256,1024]{2,1,0:T(8,128)(2,1)S(1)} %dynamic-slice_bitcast_fusion.1), channel_id=1, source_target_pairs={{0,4},{4,0},{8,12},{12,8},{1,5},{5,1},{9,13},{13,9},{2,6},{6,2},{1... | collective-permute-start | bytes 3145736 | tf_op jit(solution)/shard_map/ppermute | solution.py:583
  470.1 40.2 %collective-permute-start.55 = (bf16[128,5632]{1,0:T(8,128)(2,1)S(1)}, bf16[128,5632]{1,0:T(8,128)(2,1)S(1)}, u32[]{:S(2)}, u32[]{:S(2)}) collective-permute-start(bf16[128,5632]{1,0:T(8,128)(2,1)S(1)} %bitcast.293), channel_id=1, source_target_pairs={{0,16},{16,0},{1,17},{17,1},{2,18},{18,2},{3,19},{19,3},{4,20},{20... | collective-permute-start | bytes 4325384 | tf_op jit(solution)/shard_map/ppermute | solution.py:583
  472.9 94.1 %collective-permute-start.56 = (bf16[352,1024]{1,0:T(8,128)(2,1)}, bf16[352,1024]{1,0:T(8,128)(2,1)}, u32[]{:S(2)}, u32[]{:S(2)}) collective-permute-start(bf16[352,1024]{1,0:T(8,128)(2,1)} %bitcast.66), channel_id=1, source_target_pairs={{0,16},{16,0},{1,17},{17,1},{2,18},{18,2},{3,19},{19,3},{4,20},{20... | collective-permute-start | bytes 2162696 | tf_op jit(solution)/shard_map/ppermute | solution.py:583
  478.0 55.7 %collective-permute-start.52 = (bf16[256,1024]{1,0:T(8,128)(2,1)S(1)}, bf16[256,1024]{1,0:T(8,128)(2,1)}, u32[]{:S(2)}, u32[]{:S(2)}) collective-permute-start(bf16[256,1024]{1,0:T(8,128)(2,1)S(1)} %dynamic-slice_bitcast_fusion.4), channel_id=1, source_target_pairs={{0,8},{4,12},{8,0},{12,4},{1,9},{5,13},{9,1},{13,5},{2,10},{6,14},... | collective-permute-start | bytes 1572872 | tf_op jit(solution)/shard_map/ppermute | solution.py:583
  479.3 31.0 %collective-permute-start.53 = (bf16[96,1024]{1,0:T(8,128)(2,1)S(1)}, bf16[96,1024]{1,0:T(8,128)(2,1)S(1)}, u32[]{:S(2)}, u32[]{:S(2)}) collective-permute-start(bf16[96,1024]{1,0:T(8,128)(2,1)S(1)} %add_convert_fusion.4), channel_id=1, source_target_pairs={{0,1},{1,0},{2,3},{3,2},{4,5},{5,4},{6,7},{7,6},{8,9},{9,8},{10,11... | collective-permute-start | bytes 589832 | tf_op jit(solution)/shard_map/ppermute | solution.py:583
  479.5 53.4 %collective-permute-start.54 = (bf16[128,1536]{1,0:T(8,128)(2,1)S(1)}, bf16[128,1536]{1,0:T(8,128)(2,1)S(1)}, u32[]{:S(2)}, u32[]{:S(2)}) collective-permute-start(bf16[128,1536]{1,0:T(8,128)(2,1)S(1)} %bitcast.311), channel_id=1, source_target_pairs={{0,16},{16,0},{1,17},{17,1},{2,18},{18,2},{3,19},{19,3},{4,20},{20... | collective-permute-start | bytes 1179656 | tf_op jit(solution)/shard_map/ppermute | solution.py:583
  542.9 24.1 %collective-permute-start.57 = (bf16[64,2048]{1,0:T(8,128)(2,1)}, bf16[64,2048]{1,0:T(8,128)(2,1)}, u32[]{:S(2)}, u32[]{:S(2)}) collective-permute-start(bf16[64,2048]{1,0:T(8,128)(2,1)} %dynamic-slice_bitcast_fusion.8), channel_id=1, source_target_pairs={{0,1},{1,0},{2,3},{3,2},{4,5},{5,4},{6,7},{7,6},{8,9},{9,8},{10,11... | collective-permute-start | bytes 786440 | tf_op jit(solution)/shard_map/ppermute | solution.py:583
  545.3 21.8 %collective-permute-start.58 = (bf16[128,1024]{1,0:T(8,128)(2,1)}, bf16[128,1024]{1,0:T(8,128)(2,1)}, u32[]{:S(2)}, u32[]{:S(2)}) collective-permute-start(bf16[128,1024]{1,0:T(8,128)(2,1)} %dynamic-slice_bitcast_fusion.7), channel_id=1, source_target_pairs={{0,16},{16,0},{1,17},{17,1},{2,18},{18,2},{3,19},{19,3},{4,20},{20... | collective-permute-start | bytes 786440 | tf_op jit(solution)/shard_map/ppermute | solution.py:583
  546.5 20.6 %collective-permute-start.59 = (bf16[192,1024]{1,0:T(8,128)(2,1)}, bf16[192,1024]{1,0:T(8,128)(2,1)}, u32[]{:S(2)}, u32[]{:S(2)}) collective-permute-start(bf16[192,1024]{1,0:T(8,128)(2,1)} %bitcast.74), channel_id=1, source_target_pairs={{0,16},{16,0},{1,17},{17,1},{2,18},{18,2},{3,19},{19,3},{4,20},{20... | collective-permute-start | bytes 1179656 | tf_op jit(solution)/shard_map/ppermute | solution.py:583
  570.1 15.1 %collective-permute-start.60 = (bf16[64,2048]{1,0:T(8,128)(2,1)S(1)}, bf16[64,2048]{1,0:T(8,128)(2,1)S(1)}, u32[]{:S(2)}, u32[]{:S(2)}) collective-permute-start(bf16[64,2048]{1,0:T(8,128)(2,1)S(1)} %fusion.38), channel_id=1, source_target_pairs={{0,2},{1,3},{2,0},{3,1},{4,6},{5,7},{6,4},{7,5},{8,10},{9,11},{10,... | collective-permute-start | bytes 786440 | tf_op jit(solution)/shard_map/ppermute | solution.py:583
  (192 other events, 1915.8 us)
Sparse Core Ops, SparseCore 0:
  9.6 43.6 all-gather.5
  55.2 48.6 all-gather.9
  105.7 70.5 all-gather.7
  219.4 87.7 reduce-scatter.4
  311.1 67.6 reduce-scatter.6
  382.4 46.2 reduce-scatter.8
  432.6 56.9 reduce-scatter.10
